TPU v7x, 128 devices: a whole 4x4x4 slice. The times are simulated.
128 devices in a mesh: dp: 32 (over z, x, core), tensor: 4 (over y).
Axes of the slice: x: 4, y: 4, z: 4, core: 2. Of those that a mesh axis runs over, the one named last changes fastest.
Arguments:
- hidden_in: float32 [8192, 1152], P('dp'), may hold values from -6 to 6
- out_grad: float32 [8192, 1152], P('dp'), may hold values from -6 to 6
- segment_ids: int32 [8192], P('dp'), may hold values from 0 to 19, never falling along the last dimension, each value on 1 to 800 neighbouring positions
- w_query: float32 [1152, 1024], P('dp', 'tensor'), may hold values from -0.1875 to 0.1875
- w_keyval: float32 [2, 1152, 256], P(None, 'dp', 'tensor'), may hold values from -0.1875 to 0.1875
- w_output: float32 [1024, 1152], P('tensor', 'dp'), may hold values from -0.1875 to 0.1875
- w_gateup: float32 [2, 1152, 6912], P(None, 'dp', 'tensor'), may hold values from -0.1875 to 0.1875
- w_down: float32 [6912, 1152], P('tensor', 'dp'), may hold values from -0.078125 to 0.078125
- norm_gains: float32 [4, 1152], P(None, 'dp'), may hold values from 0.34 to 2.3
- qk_gains: float32 [2, 256], P(None, ('dp', 'tensor')), may hold values from 0.5 to 1.5
- mom_query: float32 [1152, 1024], P('dp', 'tensor'), may hold values from -217.2232 to 217.2232
- mom_keyval: float32 [2, 1152, 256], P(None, 'dp', 'tensor'), may hold values from -217.2232 to 217.2232
- mom_output: float32 [1024, 1152], P('tensor', 'dp'), may hold values from -217.2232 to 217.2232
- mom_gateup: float32 [2, 1152, 6912], P(None, 'dp', 'tensor'), may hold values from -217.2232 to 217.2232
- mom_down: float32 [6912, 1152], P('tensor', 'dp'), may hold values from -217.2232 to 217.2232
- gain_moms: float32 [4, 1152], P(None, 'dp'), may hold values from -64 to 64
- qk_moms: float32 [2, 256], P(None, ('dp', 'tensor')), may hold values from -128 to 128
Outputs:
- block_out: float32 [8192, 1152], P('dp')
- input_grad: float32 [8192, 1152], P('dp')
- new_query: float32 [1152, 1024], P('dp', 'tensor')
- new_keyval: float32 [2, 1152, 256], P(None, 'dp', 'tensor')
- new_output: float32 [1024, 1152], P('tensor', 'dp')
- new_gateup: float32 [2, 1152, 6912], P(None, 'dp', 'tensor')
- new_down: float32 [6912, 1152], P('tensor', 'dp')
- next_mom_query: float32 [1152, 1024], P('dp', 'tensor')
- next_mom_keyval: float32 [2, 1152, 256], P(None, 'dp', 'tensor')
- next_mom_output: float32 [1024, 1152], P('tensor', 'dp')
- next_mom_gateup: float32 [2, 1152, 6912], P(None, 'dp', 'tensor')
- next_mom_down: float32 [6912, 1152], P('tensor', 'dp')
- new_norm_gains: float32 [4, 1152], P(None, 'dp')
- next_gain_moms: float32 [4, 1152], P(None, 'dp')
- new_qk_gains: float32 [2, 256], P(None, ('dp', 'tensor'))
- next_qk_moms: float32 [2, 256], P(None, ('dp', 'tensor'))
Inputs may be any that keep to these rules, and one draw needn't show every extreme that they name: `segment_ids`: segment numbers never fall along the sequence; each document holds 1 to 800 tokens and one holds exactly 800.
All inputs are finite; a program needn't handle non-finite values.
Results may differ from a plain program's by a relative error of at most 0.04.
Values may be sent and summed in bfloat16 or wider, within the bound.
A program may use at most 128 MiB of HBM per device.

v0:
```python
import math

import jax
import jax.numpy as jnp
from jax import lax
from jax.sharding import PartitionSpec as P

WINDOW = 512
NS_STEPS = 3


EPSILON = 1e-06
COEF_ONE = 3.4445
COEF_TWO = -4.775
COEF_THREE = 2.0315


def passed_along(array, axis, by):
    length = lax.axis_size(axis)
    pairs = [(i, i + by) for i in range(length) if 0 <= i + by < length]
    return lax.ppermute(array, axis, pairs)


def rms_norm(values, scales):
    return values * lax.rsqrt(jnp.mean(values * values, axis=-1, keepdims=True) + EPSILON) * scales


def rotate(values, cosine, sine_wave):
    middle = values.shape[-1] // 2
    front_part = values[..., :middle]
    back_part = values[..., middle:]
    return jnp.concatenate(
        [front_part * cosine - back_part * sine_wave, back_part * cosine + front_part * sine_wave],
        axis=-1,
    )


def angles(positions, width):
    freqs = 10000.0 ** (-jnp.arange(width // 2, dtype=jnp.float32) * 2.0 / width)
    turned = positions.astype(jnp.float32)[:, None] * freqs[None, :]
    return (jnp.cos(turned), jnp.sin(turned))


def gated_gelu(gate_in, up_in):
    return jax.nn.gelu(gate_in, approximate=True) * up_in


def tensor_total(partial_value):
    return lax.psum(partial_value.astype(jnp.bfloat16), "tensor").astype(jnp.float32)


def local(
    hidden_in,
    out_grad,
    segment_ids,
    w_query,
    w_keyval,
    w_output,
    w_gateup,
    w_down,
    norm_gains,
    qk_gains,
    mom_query,
    mom_keyval,
    mom_output,
    mom_gateup,
    mom_down,
    gain_moms,
    qk_moms,
):
    dp_size = lax.axis_size("dp")
    tp_size = lax.axis_size("tensor")
    dp_index = lax.axis_index("dp")
    tp_index = lax.axis_index("tensor")
    tok_rows = hidden_in.shape[0]
    model_width = hidden_in.shape[1]
    head_dim = qk_gains.shape[1] * dp_size * tp_size
    kv_cols = w_keyval.shape[2]
    window_steps = max(1, WINDOW // tok_rows)
    attn_scale = head_dim ** (-0.5)
    shared_kv, shared_qk = (
        lax.all_gather(w_keyval.astype(jnp.bfloat16), "tensor", axis=2, tiled=True),
        lax.all_gather(qk_gains.astype(jnp.bfloat16), "tensor", axis=1, tiled=True),
    )
    query_w, keyval_w, output_w, gateup_w, down_w, gains_low, qk_low = (
        lax.all_gather(w_query.astype(jnp.bfloat16), "dp", axis=0, tiled=True),
        lax.all_gather(shared_kv, "dp", axis=1, tiled=True),
        lax.all_gather(w_output.astype(jnp.bfloat16), "dp", axis=1, tiled=True),
        lax.all_gather(w_gateup.astype(jnp.bfloat16), "dp", axis=1, tiled=True),
        lax.all_gather(w_down.astype(jnp.bfloat16), "dp", axis=1, tiled=True),
        lax.all_gather(norm_gains.astype(jnp.bfloat16), "dp", axis=1, tiled=True),
        lax.all_gather(shared_qk, "dp", axis=1, tiled=True),
    )
    gains_full = gains_low.astype(jnp.float32)
    qk_full = qk_low.astype(jnp.float32)
    query_pos = dp_index * tok_rows + jnp.arange(tok_rows, dtype=jnp.int32)
    cosine, sine_wave = angles(query_pos, head_dim)
    normed_in, pull_input = jax.vjp(rms_norm, hidden_in, gains_full[0])
    normed_low = normed_in.astype(jnp.bfloat16)
    query_raw = jnp.dot(normed_low, query_w, preferred_element_type=jnp.float32)
    heads_here = query_raw.shape[1] // head_dim
    query_raw = query_raw.reshape(tok_rows, heads_here, head_dim)
    keyval_raw = jnp.einsum("td,cde->cte", normed_low, keyval_w, preferred_element_type=jnp.float32)

    def query_side(values, scales):
        return rotate(rms_norm(values, scales), cosine[:, None, :], sine_wave[:, None, :])

    def key_side(values, scales):
        return rotate(rms_norm(values, scales), cosine, sine_wave)

    query_rot, pull_query = jax.vjp(query_side, query_raw, qk_full[0])
    key_rot, pull_key = jax.vjp(key_side, keyval_raw[0], qk_full[1])
    query_low = query_rot.astype(jnp.bfloat16)
    own_keys = jnp.stack([key_rot, keyval_raw[1]]).astype(jnp.bfloat16)
    own_segs = segment_ids.astype(jnp.bfloat16)
    key_parts = []
    seg_parts = []
    for distance in range(window_steps, 0, -1):
        moved_keys, moved_segs = passed_along((own_keys, own_segs), "dp", distance)
        key_parts.append(moved_keys)
        seg_parts.append(moved_segs)
    key_parts.append(own_keys)
    seg_parts.append(own_segs)
    all_keys = jnp.concatenate(key_parts, axis=1)
    all_segs = jnp.concatenate(seg_parts, axis=0).astype(jnp.float32)
    key_pos = (dp_index - window_steps) * tok_rows + jnp.arange(all_keys.shape[1], dtype=jnp.int32)
    key_gap = query_pos[:, None] - key_pos[None, :]
    allowed = (
        (own_segs.astype(jnp.float32)[:, None] == all_segs[None, :])
        & (key_gap >= 0)
        & (key_gap < WINDOW)
        & (key_pos >= 0)[None, :]
    )
    scores = (
        jnp.einsum("thd,kd->htk", query_low, all_keys[0], preferred_element_type=jnp.float32)
        * attn_scale
    )
    masked = jnp.where(allowed[None], scores, -1e30)
    biggest = jnp.max(masked, axis=-1, keepdims=True)
    exp_total = jnp.sum(jnp.exp(masked - biggest), axis=-1, keepdims=True)
    log_total = biggest + jnp.log(exp_total)
    softmax_out = jnp.exp(masked - log_total)
    softmax_low = softmax_out.astype(jnp.bfloat16)
    attended = jnp.einsum(
        "htk,kd->thd", softmax_low, all_keys[1], preferred_element_type=jnp.float32
    )
    attended_low = attended.astype(jnp.bfloat16).reshape(tok_rows, heads_here * head_dim)
    attn_out = tensor_total(jnp.dot(attended_low, output_w, preferred_element_type=jnp.float32))
    attn_normed, pull_attn = jax.vjp(rms_norm, attn_out, gains_full[1])
    middle = hidden_in + attn_normed
    ffn_in, pull_ffn_in = jax.vjp(rms_norm, middle, gains_full[2])
    ffn_low = ffn_in.astype(jnp.bfloat16)
    gateup = jnp.einsum("td,cdf->ctf", ffn_low, gateup_w, preferred_element_type=jnp.float32)
    mixed, pull_mix = jax.vjp(gated_gelu, gateup[0], gateup[1])
    mixed_low = mixed.astype(jnp.bfloat16)
    ffn_out = tensor_total(jnp.dot(mixed_low, down_w, preferred_element_type=jnp.float32))
    ffn_normed, pull_ffn_out = jax.vjp(rms_norm, ffn_out, gains_full[3])
    block_out = middle + ffn_normed
    ffn_grad, gain3_grad = pull_ffn_out(out_grad)
    ffn_grad_low = ffn_grad.astype(jnp.bfloat16)
    mixed_grad = jnp.dot(ffn_grad_low, down_w.T, preferred_element_type=jnp.float32)
    gate_grad, up_grad = pull_mix(mixed_grad)
    gateup_grad_low = jnp.stack([gate_grad, up_grad]).astype(jnp.bfloat16)
    gateup_wgrad = jnp.einsum(
        "td,ctf->cdf", ffn_low, gateup_grad_low, preferred_element_type=jnp.float32
    )
    down_wgrad = jnp.dot(mixed_low.T, ffn_grad_low, preferred_element_type=jnp.float32)
    ffn_in_grad = tensor_total(
        jnp.einsum("ctf,cdf->td", gateup_grad_low, gateup_w, preferred_element_type=jnp.float32)
    )
    middle_part, gain2_grad = pull_ffn_in(ffn_in_grad)
    middle_grad = out_grad + middle_part
    attn_grad, gain1_grad = pull_attn(middle_grad)
    attn_grad_low = attn_grad.astype(jnp.bfloat16)
    output_wgrad = jnp.dot(attended_low.T, attn_grad_low, preferred_element_type=jnp.float32)
    attended_grad = (
        jnp.dot(attn_grad_low, output_w.T, preferred_element_type=jnp.float32)
        .astype(jnp.bfloat16)
        .reshape(tok_rows, heads_here, head_dim)
    )
    again_scores = (
        jnp.einsum("thd,kd->htk", query_low, all_keys[0], preferred_element_type=jnp.float32)
        * attn_scale
    )
    again_probs = jnp.exp(jnp.where(allowed[None], again_scores, -1e30) - log_total)
    again_low = again_probs.astype(jnp.bfloat16)
    prob_grad = jnp.einsum(
        "thd,kd->htk", attended_grad, all_keys[1], preferred_element_type=jnp.float32
    )
    value_grad = jnp.einsum(
        "htk,thd->kd", again_low, attended_grad, preferred_element_type=jnp.float32
    )
    score_grad = again_probs * (
        prob_grad - jnp.sum(again_probs * prob_grad, axis=-1, keepdims=True)
    )
    score_low = score_grad.astype(jnp.bfloat16)
    query_rot_grad = (
        jnp.einsum("htk,kd->thd", score_low, all_keys[0], preferred_element_type=jnp.float32)
        * attn_scale
    )
    key_rot_grad = (
        jnp.einsum("htk,thd->kd", score_low, query_low, preferred_element_type=jnp.float32)
        * attn_scale
    )
    key_grads = jnp.stack([key_rot_grad, value_grad])
    own_grads = key_grads[:, window_steps * tok_rows :]
    for distance in range(window_steps, 0, -1):
        block_index = window_steps - distance
        grad_piece = key_grads[:, block_index * tok_rows : (block_index + 1) * tok_rows]
        own_grads = own_grads + passed_along(
            grad_piece.astype(jnp.bfloat16), "dp", -distance
        ).astype(grad_piece.dtype)
    query_grad, qgain_grad = pull_query(query_rot_grad)
    own_grads, qgain_grad = (
        lax.psum(own_grads.astype(jnp.bfloat16), "tensor").astype(jnp.float32),
        lax.psum(qgain_grad.astype(jnp.bfloat16), "tensor").astype(jnp.float32),
    )
    key_grad, kgain_grad = pull_key(own_grads[0])
    keyval_low = jnp.stack([key_grad, own_grads[1]]).astype(jnp.bfloat16)
    query_grad_low = query_grad.astype(jnp.bfloat16).reshape(tok_rows, heads_here * head_dim)
    normed_grad = tensor_total(
        jnp.dot(query_grad_low, query_w.T, preferred_element_type=jnp.float32)
    ) + jnp.einsum("cte,cde->td", keyval_low, keyval_w, preferred_element_type=jnp.float32)
    input_part, gain0_grad = pull_input(normed_grad)
    input_grad = middle_grad + input_part
    query_wgrad = jnp.dot(normed_low.T, query_grad_low, preferred_element_type=jnp.float32)
    keyval_cols = lax.dynamic_slice_in_dim(keyval_low, tp_index * kv_cols, kv_cols, 2)
    keyval_wgrad = jnp.einsum(
        "td,cte->cde", normed_low, keyval_cols, preferred_element_type=jnp.float32
    )
    gain_grads = jnp.stack([gain0_grad, gain1_grad, gain2_grad, gain3_grad])
    qk_grads = jnp.stack([qgain_grad, kgain_grad])
    query_red, keyval_red, output_red, gains_red, qk_red = (
        lax.psum_scatter(
            query_wgrad.astype(jnp.bfloat16), "dp", scatter_dimension=0, tiled=True
        ).astype(jnp.float32),
        lax.psum_scatter(
            keyval_wgrad.astype(jnp.bfloat16), "dp", scatter_dimension=1, tiled=True
        ).astype(jnp.float32),
        lax.psum_scatter(
            output_wgrad.astype(jnp.bfloat16), "dp", scatter_dimension=1, tiled=True
        ).astype(jnp.float32),
        lax.psum_scatter(
            gain_grads.astype(jnp.bfloat16), "dp", scatter_dimension=1, tiled=True
        ).astype(jnp.float32),
        lax.psum_scatter(
            qk_grads.astype(jnp.bfloat16), "dp", scatter_dimension=1, tiled=True
        ).astype(jnp.float32),
    )
    gateup_red, down_red = (
        lax.psum_scatter(
            gateup_wgrad.astype(jnp.bfloat16), "dp", scatter_dimension=1, tiled=True
        ).astype(jnp.float32),
        lax.psum_scatter(
            down_wgrad.astype(jnp.bfloat16), "dp", scatter_dimension=1, tiled=True
        ).astype(jnp.float32),
    )
    qk_width = qk_red.shape[1] // tp_size
    qk_red = lax.dynamic_slice_in_dim(qk_red, tp_index * qk_width, qk_width, 1)
    next_query = 0.95 * mom_query + query_red
    next_keyval = 0.95 * mom_keyval + keyval_red
    next_output = 0.95 * mom_output + output_red
    next_gateup = 0.95 * mom_gateup + gateup_red
    next_down = 0.95 * mom_down + down_red
    matrices = [
        next_query,
        next_keyval[0],
        next_keyval[1],
        next_output.T,
        next_gateup[0],
        next_gateup[1],
        next_down.T,
    ]
    squares = [jnp.sum(matrix * matrix) for matrix in matrices]
    totals = lax.psum(
        (squares[0], squares[1], squares[2], squares[3], squares[4], squares[5], squares[6]),
        ("dp", "tensor"),
    )
    current = [matrix / (jnp.sqrt(summed) + 1e-07) for matrix, summed in zip(matrices, totals)]
    for repeat in range(NS_STEPS):
        rounded = [matrix.astype(jnp.bfloat16) for matrix in current]
        gathered = (
            lax.all_gather(rounded[0], "dp", axis=0, tiled=True),
            lax.all_gather(rounded[1], "dp", axis=0, tiled=True),
            lax.all_gather(rounded[2], "dp", axis=0, tiled=True),
            lax.all_gather(rounded[3], "dp", axis=0, tiled=True),
            lax.all_gather(rounded[4], "dp", axis=0, tiled=True),
            lax.all_gather(rounded[5], "dp", axis=0, tiled=True),
            lax.all_gather(rounded[6], "dp", axis=0, tiled=True),
        )
        partial_value = [
            jnp.einsum("rc,dc->rd", local_rows, entire, preferred_element_type=jnp.float32)
            for local_rows, entire in zip(rounded, gathered)
        ]
        gram_sums = (
            lax.psum(partial_value[0].astype(jnp.bfloat16), "tensor").astype(jnp.float32),
            lax.psum(partial_value[1].astype(jnp.bfloat16), "tensor").astype(jnp.float32),
            lax.psum(partial_value[2].astype(jnp.bfloat16), "tensor").astype(jnp.float32),
            lax.psum(partial_value[3].astype(jnp.bfloat16), "tensor").astype(jnp.float32),
            lax.psum(partial_value[4].astype(jnp.bfloat16), "tensor").astype(jnp.float32),
            lax.psum(partial_value[5].astype(jnp.bfloat16), "tensor").astype(jnp.float32),
            lax.psum(partial_value[6].astype(jnp.bfloat16), "tensor").astype(jnp.float32),
        )
        gram_low = [product.astype(jnp.bfloat16) for product in gram_sums]
        images = [
            jnp.dot(product, entire, preferred_element_type=jnp.float32)
            for product, entire in zip(gram_low, gathered)
        ]
        images_low = [matrix.astype(jnp.bfloat16) for matrix in images]
        spread = (
            lax.all_gather(images_low[0], "dp", axis=0, tiled=True),
            lax.all_gather(images_low[1], "dp", axis=0, tiled=True),
            lax.all_gather(images_low[2], "dp", axis=0, tiled=True),
            lax.all_gather(images_low[3], "dp", axis=0, tiled=True),
            lax.all_gather(images_low[4], "dp", axis=0, tiled=True),
            lax.all_gather(images_low[5], "dp", axis=0, tiled=True),
            lax.all_gather(images_low[6], "dp", axis=0, tiled=True),
        )
        squared = [
            jnp.dot(product, entire, preferred_element_type=jnp.float32)
            for product, entire in zip(gram_low, spread)
        ]
        current = [
            COEF_ONE * start_term + COEF_TWO * image_term + COEF_THREE * square_term
            for start_term, image_term, square_term in zip(current, images, squared)
        ]

    def step_scale(matrix):
        return 0.15 * 0.2 * math.sqrt(max(model_width, matrix.shape[1] * tp_size))

    new_query = w_query - step_scale(current[0]) * current[0]
    new_keyval = w_keyval - jnp.stack(
        [step_scale(current[1]) * current[1], step_scale(current[2]) * current[2]]
    )
    new_output = w_output - step_scale(current[3]) * current[3].T
    new_gateup = w_gateup - jnp.stack(
        [step_scale(current[4]) * current[4], step_scale(current[5]) * current[5]]
    )
    new_down = w_down - step_scale(current[6]) * current[6].T
    gain_rate = 2.0 / math.sqrt(tok_rows * dp_size)
    next_gain_moms = 0.9 * gain_moms + 0.1 * gains_red
    new_norm_gains = norm_gains - gain_rate * next_gain_moms
    next_qk_moms = 0.9 * qk_moms + 0.1 * qk_red
    new_qk_gains = qk_gains - gain_rate * next_qk_moms
    return (
        block_out,
        input_grad,
        new_query,
        new_keyval,
        new_output,
        new_gateup,
        new_down,
        next_query,
        next_keyval,
        next_output,
        next_gateup,
        next_down,
        new_norm_gains,
        next_gain_moms,
        new_qk_gains,
        next_qk_moms,
    )


def solution(mesh):
    return jax.shard_map(
        local,
        mesh=mesh,
        in_specs=(
            P("dp", None),
            P("dp", None),
            P("dp"),
            P("dp", "tensor"),
            P(None, "dp", "tensor"),
            P("tensor", "dp"),
            P(None, "dp", "tensor"),
            P("tensor", "dp"),
            P(None, "dp"),
            P(None, ("dp", "tensor")),
            P("dp", "tensor"),
            P(None, "dp", "tensor"),
            P("tensor", "dp"),
            P(None, "dp", "tensor"),
            P("tensor", "dp"),
            P(None, "dp"),
            P(None, ("dp", "tensor")),
        ),
        out_specs=(
            P("dp", None),
            P("dp", None),
            P("dp", "tensor"),
            P(None, "dp", "tensor"),
            P("tensor", "dp"),
            P(None, "dp", "tensor"),
            P("tensor", "dp"),
            P("dp", "tensor"),
            P(None, "dp", "tensor"),
            P("tensor", "dp"),
            P(None, "dp", "tensor"),
            P("tensor", "dp"),
            P(None, "dp"),
            P(None, "dp"),
            P(None, ("dp", "tensor")),
            P(None, ("dp", "tensor")),
        ),
        check_vma=False,
    )
```

profile of v0, /device:TPU:1, one launch (start us, length us, event | category | flops | bytes accessed | tf_op | source)
XLA Modules:
  0.0 2201.5 jit_solution(15602695407172509913)
XLA Ops:
  27.8 27.0 %all-gather.4 = bf16[32,36,4]{1,2,0:T(4,128)(2,1)S(1)} all-gather(bf16[1,36,4]{1,2,0:T(4,128)(2,1)S(1)} %convert_bitcast_fusion.38), channel_id=1, replica_groups=mesh['dp'=32,'tensor'=4] {'dp'}, dimensions={0}, use_global_device_ids=true | all-gather | bytes 9504 | tf_op jit(solution)/shard_map/all_gather | solution.py:91
  158.6 38.3 %all-reduce.29.cloned.1.call-done = bf16[256,1152]{1,0:T(8,128)(2,1)} async-done(((bf16[256,1152]{1,0:T(8,128)(2,1)}), bf16[256,1152]{1,0:T(8,128)(2,1)}) %all-reduce.29.cloned.1.call-update) | async-done | bytes 589840 | tf_op jit(solution)/shard_map/psum | solution.py:49
  201.8 47.8 %all-gather.78.cloned.1.call-done = bf16[32,36,1728]{2,1,0:T(8,128)(2,1)} async-done(((bf16[1,36,1728]{2,1,0:T(8,128)(2,1)}), bf16[32,36,1728]{2,1,0:T(8,128)(2,1)}) %all-gather.78.cloned.1.call-update) | async-done | bytes 3981328 | tf_op jit(solution)/shard_map/all_gather | solution.py:90
  256.9 47.5 %all-gather.72.cloned.1.call-done = bf16[2,1152,1728]{2,0,1:T(2,128)(2,1)} async-done(((bf16[2,36,1728]{2,0,1:T(2,128)(2,1)}), bf16[2,1152,1728]{2,0,1:T(2,128)(2,1)}) %all-gather.72.cloned.1.call-update) | async-done | bytes 7962640 | tf_op jit(solution)/shard_map/all_gather | solution.py:89
  317.5 40.5 %all-reduce.31.cloned.1.call-done = bf16[256,1152]{1,0:T(8,128)(2,1)} async-done(((bf16[256,1152]{1,0:T(8,128)(2,1)}), bf16[256,1152]{1,0:T(8,128)(2,1)}) %all-reduce.31.cloned.1.call-update) | async-done | bytes 589840 | tf_op jit(solution)/shard_map/psum | solution.py:49
  373.4 44.1 %all-reduce.33.cloned.1.call-done = bf16[256,1152]{1,0:T(8,128)(2,1)} async-done(((bf16[256,1152]{1,0:T(8,128)(2,1)}), bf16[256,1152]{1,0:T(8,128)(2,1)}) %all-reduce.33.cloned.1.call-update) | async-done | bytes 589840 | tf_op jit(solution)/shard_map/psum | solution.py:49
  476.8 30.2 %all-reduce.35.cloned.1.call-done = bf16[2,256,256]{1,2,0:T(8,128)(2,1)} async-done(((bf16[2,256,256]{1,2,0:T(8,128)(2,1)}), bf16[2,256,256]{1,2,0:T(8,128)(2,1)}) %all-reduce.35.cloned.1.call-update) | async-done | bytes 262160 | tf_op jit(solution)/shard_map/psum | solution.py:215
  516.3 74.6 %fusion.210 = (bf16[40,256]{1,0:T(8,128)(2,1)S(1)}, bf16[256,40]{0,1:T(8,128)(2,1)S(1)}) fusion(bf16[1152,256]{1,0:T(8,128)(2,1)S(1)} %convolution_convert_fusion.3, bf16[256,1152]{0,1:T(8,128)(2,1)S(1)} %convolution_convert_fusion.2), kind=kCustom, calls=%all-reduce-scatter.2 | all-reduce-scatter fusion | flops 655361 | bytes 1221120
  613.7 37.9 %all-reduce.37.cloned.1.call-done = (bf16[2,1152,64]{2,0,1:T(2,128)(2,1)}, bf16[2,1152,1728]{2,0,1:T(2,128)(2,1)}, bf16[1728,1152]{1,0:T(8,128)(2,1)}) async-done(((bf16[2,1152,64]{2,0,1:T(2,128)(2,1)}, bf16[2,1152,1728]{2,0,1:T(2,128)(2,1)}, bf16[1728,1152]{1,0:T(8,128)(2,1)}), (bf16[2,1152,64]{2,0,1:T(2,128)(2,1)}, bf16[2,1152,1728]{2,0,1:T(2,128)(2,1)}, ...) | async-done | bytes 12238864
  658.2 65.7 %all-reduce.13 = (f32[]{:T(128)}, f32[]{:T(128)}, f32[]{:T(128)}, f32[]{:T(128)}, f32[]{:T(128)}, /*index=5*/f32[]{:T(128)}, f32[]{:T(128)}) all-reduce(f32[]{:T(128)} %get-tuple-element.166, f32[]{:T(128)} %get-tuple-element.111, f32[]{:T(128)} %get-tuple-element.110, ...), channel_id=1, replica_groups=mesh['dp'=32,'tensor'=4] {'dp','tensor'}, use_global_device_ids=true, to_apply=%region_22.23 | all-reduce | flops 7 | bytes 56 | tf_op jit(solution)/shard_map/psum | solution.py:275
  894.7 41.6 %all-reduce.43.cloned.1.call-done = (bf16[36,1152]{1,0:T(8,128)(2,1)}, bf16[36,1152]{1,0:T(8,128)(2,1)}, bf16[36,1152]{1,0:T(8,128)(2,1)}, bf16[36,1152]{1,0:T(8...) async-done(((bf16[36,1152]{1,0:T(8,128)(2,1)}, bf16[36,1152]{1,0:T(8,128)(2,1)}, bf16[36,1152]{1,0:T(8,128)(2,1)}, ...) | async-done | bytes 580624 | tf_op jit(solution)/shard_map/psum | solution.py:296
  948.8 41.5 %all-gather.90.cloned.1.call-done = bf16[32,36,1728]{2,1,0:T(8,128)(2,1)} async-done(((bf16[1,36,1728]{2,1,0:T(8,128)(2,1)}), bf16[32,36,1728]{2,1,0:T(8,128)(2,1)}) %all-gather.90.cloned.1.call-update) | async-done | bytes 3981328 | tf_op jit(solution)/shard_map/all_gather | solution.py:316
  1001.4 38.2 %all-gather.80.cloned.1.call-done = bf16[32,36,1728]{2,1,0:T(8,128)(2,1)} async-done(((bf16[1,36,1728]{2,1,0:T(8,128)(2,1)}), bf16[32,36,1728]{2,1,0:T(8,128)(2,1)}) %all-gather.80.cloned.1.call-update) | async-done | bytes 3981328 | tf_op jit(solution)/shard_map/all_gather | solution.py:315
  1050.6 37.7 %all-gather.102.cloned.1.call-done = bf16[32,36,1728]{2,1,0:T(8,128)(2,1)} async-done(((bf16[1,36,1728]{2,1,0:T(8,128)(2,1)}), bf16[32,36,1728]{2,1,0:T(8,128)(2,1)}) %all-gather.102.cloned.1.call-update) | async-done | bytes 3981328 | tf_op jit(solution)/shard_map/all_gather | solution.py:317
  1215.3 26.7 %all-gather.16 = bf16[32,36,64]{2,1,0:T(8,128)(2,1)} all-gather(bf16[1,36,64]{2,1,0:T(8,128)(2,1)S(1)} %convert_bitcast_fusion.31), channel_id=1, replica_groups=mesh['dp'=32,'tensor'=4] {'dp'}, dimensions={0}, use_global_device_ids=true | all-gather | bytes 152064 | tf_op jit(solution)/shard_map/all_gather | solution.py:312
  1273.1 26.6 %all-gather.27 = bf16[32,36,256]{2,1,0:T(8,128)(2,1)} all-gather(bf16[1,36,256]{2,1,0:T(8,128)(2,1)S(1)} %convert_bitcast_fusion.18), channel_id=1, replica_groups=mesh['dp'=32,'tensor'=4] {'dp'}, dimensions={0}, use_global_device_ids=true | all-gather | bytes 608256 | tf_op jit(solution)/shard_map/all_gather | solution.py:314
  1368.8 41.4 %all-reduce.41.cloned.1.call-done = (bf16[36,1152]{1,0:T(8,128)(2,1)}, bf16[36,1152]{1,0:T(8,128)(2,1)}, bf16[36,1152]{1,0:T(8,128)(2,1)}, bf16[36,1152]{1,0:T(8...) async-done(((bf16[36,1152]{1,0:T(8,128)(2,1)}, bf16[36,1152]{1,0:T(8,128)(2,1)}, bf16[36,1152]{1,0:T(8,128)(2,1)}, ...) | async-done | bytes 580624 | tf_op jit(solution)/shard_map/psum | solution.py:296
  1421.3 42.3 %all-gather.94.cloned.1.call-done = bf16[32,36,1728]{2,1,0:T(8,128)(2,1)} async-done(((bf16[1,36,1728]{2,1,0:T(8,128)(2,1)}), bf16[32,36,1728]{2,1,0:T(8,128)(2,1)}) %all-gather.94.cloned.1.call-update) | async-done | bytes 3981328 | tf_op jit(solution)/shard_map/all_gather | solution.py:316
  1474.6 37.8 %all-gather.84.cloned.1.call-done = bf16[32,36,1728]{2,1,0:T(8,128)(2,1)} async-done(((bf16[1,36,1728]{2,1,0:T(8,128)(2,1)}), bf16[32,36,1728]{2,1,0:T(8,128)(2,1)}) %all-gather.84.cloned.1.call-update) | async-done | bytes 3981328 | tf_op jit(solution)/shard_map/all_gather | solution.py:315
  1523.7 37.7 %all-gather.106.cloned.1.call-done = bf16[32,36,1728]{2,1,0:T(8,128)(2,1)} async-done(((bf16[1,36,1728]{2,1,0:T(8,128)(2,1)}), bf16[32,36,1728]{2,1,0:T(8,128)(2,1)}) %all-gather.106.cloned.1.call-update) | async-done | bytes 3981328 | tf_op jit(solution)/shard_map/all_gather | solution.py:317
  1575.2 26.8 %all-gather.13 = bf16[32,36,256]{2,1,0:T(8,128)(2,1)} all-gather(bf16[1,36,256]{2,1,0:T(8,128)(2,1)S(1)} %convert_bitcast_fusion.20), channel_id=1, replica_groups=mesh['dp'=32,'tensor'=4] {'dp'}, dimensions={0}, use_global_device_ids=true | all-gather | bytes 608256 | tf_op jit(solution)/shard_map/all_gather | solution.py:311
  1838.6 45.6 %all-reduce.39.cloned.1.call-done = (bf16[256,1152]{1,0:T(8,128)(2,1)}, bf16[36,1152]{1,0:T(8,128)(2,1)}, bf16[36,1152]{1,0:T(8,128)(2,1)}, bf16[36,1152]{1,0:T(...) async-done(((bf16[256,1152]{1,0:T(8,128)(2,1)}, bf16[36,1152]{1,0:T(8,128)(2,1)}, ...) | async-done | bytes 1170448 | tf_op jit(solution)/shard_map/psum | solution.py:49
  1910.7 30.5 %all-gather.15 = bf16[32,36,256]{2,1,0:T(8,128)(2,1)} all-gather(bf16[1,36,256]{2,1,0:T(8,128)(2,1)S(1)} %convert_bitcast_fusion.19), channel_id=1, replica_groups=mesh['dp'=32,'tensor'=4] {'dp'}, dimensions={0}, use_global_device_ids=true | all-gather | bytes 608256 | tf_op jit(solution)/shard_map/all_gather | solution.py:311
  2029.1 121.5 %all-reduce.14 = (bf16[4,1152]{1,0:T(4,128)(2,1)S(1)}, bf16[2,256]{1,0:T(2,128)(2,1)S(1)}) all-reduce(bf16[4,1152]{1,0:T(4,128)(2,1)S(1)} %pad_maximum_fusion.10, bf16[2,256]{1,0:T(2,128)(2,1)} %pad_maximum_fusion.11), channel_id=11, replica_groups=mesh['dp'=32,'tensor'=4] {'dp'}, use_global_device_ids=true, to_apply=%region_64.65.clone | all-reduce | flops 5120 | bytes 20480
  (749 shorter events, 1127.8 us)
Async XLA Ops:
  7.2 131.8 %all-gather.70.cloned.1.call-start = ((), (), s32[]{:S(2)}) async-start(), calls=%async_computation | async-start | bytes 1216512 | tf_op jit(solution)/shard_map/all_gather | solution.py:87
  7.9 140.6 %collective-permute-start.3 = (bf16[256]{0:T(256)(128)(2,1)S(1)}, bf16[256]{0:T(256)(128)(2,1)S(1)}, u32[]{:S(2)}, u32[]{:S(2)}) collective-permute-start(bf16[256]{0:T(256)(128)(2,1)S(1)} %get-tuple-element.172), channel_id=1, source_target_pairs={{0,4},{4,8},{8,12},{12,16},{16,20},{20,24},{24,28},{28,32},{32,36}... | collective-permute-start | bytes 1544 | tf_op jit(solution)/shard_map/ppermute | solution.py:21
  12.4 136.1 %collective-permute-start.2 = (bf16[256]{0:T(256)(128)(2,1)S(1)}, bf16[256]{0:T(256)(128)(2,1)S(1)}, u32[]{:S(2)}, u32[]{:S(2)}) collective-permute-start(bf16[256]{0:T(256)(128)(2,1)S(1)} %get-tuple-element.172), channel_id=1, source_target_pairs={{0,8},{4,12},{8,16},{12,20},{16,24},{20,28},{24,32},{28,36},{32,40... | collective-permute-start | bytes 1544 | tf_op jit(solution)/shard_map/ppermute | solution.py:21
  27.1 169.7 %all-reduce.29.cloned.1.call-start = ((), (), s32[]{:S(2)}) async-start(), calls=%async_computation.1 | async-start | bytes 1179648 | tf_op jit(solution)/shard_map/psum | solution.py:49
  157.4 147.0 %all-gather.72.cloned.1.call-start = ((), (), s32[]{:S(2)}) async-start(), calls=%async_computation.2 | async-start | bytes 8515584 | tf_op jit(solution)/shard_map/all_gather | solution.py:89
  158.3 199.7 %all-reduce.31.cloned.1.call-start = ((), (), s32[]{:S(2)}) async-start(), calls=%async_computation.3 | async-start | bytes 1179648 | tf_op jit(solution)/shard_map/psum | solution.py:49
  373.4 133.6 %all-reduce.35.cloned.1.call-start = ((), (), s32[]{:S(2)}) async-start(), calls=%async_computation.5 | async-start | bytes 524288 | tf_op jit(solution)/shard_map/psum | solution.py:215
  465.6 186.0 %all-reduce.37.cloned.1.call-start = ((), (), s32[]{:S(2)}) async-start(), calls=%async_computation.25 | async-start | bytes 25657344
  511.1 329.2 %all-gather.76.cloned.1.call-start = ((), (), s32[]{:S(2)}) async-start(), calls=%async_computation.7 | async-start | bytes 8515584 | tf_op jit(solution)/shard_map/all_gather | solution.py:288
  727.2 156.0 %all-gather.100.cloned.1.call-start = ((), (), s32[]{:S(2)}) async-start(), calls=%async_computation.19 | async-start | bytes 4730880 | tf_op jit(solution)/shard_map/all_gather | solution.py:289
  728.7 207.6 %all-reduce.43.cloned.1.call-start = ((), (), s32[]{:S(2)}) async-start(), calls=%async_computation.28 | async-start | bytes 1290240 | tf_op jit(solution)/shard_map/psum | solution.py:296
  944.9 143.4 %all-gather.102.cloned.1.call-start = ((), (), s32[]{:S(2)}) async-start(), calls=%async_computation.20 | async-start | bytes 4730880 | tf_op jit(solution)/shard_map/all_gather | solution.py:317
  948.5 387.9 %all-gather.92.cloned.1.call-start = ((), (), s32[]{:S(2)}) async-start(), calls=%async_computation.15 | async-start | bytes 4730880 | tf_op jit(solution)/shard_map/all_gather | solution.py:288
  1001.3 342.4 %all-gather.82.cloned.1.call-start = ((), (), s32[]{:S(2)}) async-start(), calls=%async_computation.10 | async-start | bytes 4730880 | tf_op jit(solution)/shard_map/all_gather | solution.py:287
  1050.6 306.7 %all-gather.104.cloned.1.call-start = ((), (), s32[]{:S(2)}) async-start(), calls=%async_computation.21 | async-start | bytes 4730880 | tf_op jit(solution)/shard_map/all_gather | solution.py:289
  1100.2 310.0 %all-reduce.41.cloned.1.call-start = ((), (), s32[]{:S(2)}) async-start(), calls=%async_computation.27 | async-start | bytes 1290240 | tf_op jit(solution)/shard_map/psum | solution.py:296
  1417.6 143.8 %all-gather.106.cloned.1.call-start = ((), (), s32[]{:S(2)}) async-start(), calls=%async_computation.22 | async-start | bytes 4730880 | tf_op jit(solution)/shard_map/all_gather | solution.py:317
  1421.2 384.9 %all-gather.96.cloned.1.call-start = ((), (), s32[]{:S(2)}) async-start(), calls=%async_computation.17 | async-start | bytes 4730880 | tf_op jit(solution)/shard_map/all_gather | solution.py:288
  1474.5 338.8 %all-gather.86.cloned.1.call-start = ((), (), s32[]{:S(2)}) async-start(), calls=%async_computation.12 | async-start | bytes 4730880 | tf_op jit(solution)/shard_map/all_gather | solution.py:287
  1523.5 303.6 %all-gather.108.cloned.1.call-start = ((), (), s32[]{:S(2)}) async-start(), calls=%async_computation.23 | async-start | bytes 4730880 | tf_op jit(solution)/shard_map/all_gather | solution.py:289
  1572.5 311.7 %all-reduce.39.cloned.1.call-start = ((), (), s32[]{:S(2)}) async-start(), calls=%async_computation.26 | async-start | bytes 2469888 | tf_op jit(solution)/shard_map/psum | solution.py:49
  1838.5 322.1 %all-gather.98.cloned.1.call-start = ((), (), s32[]{:S(2)}) async-start(), calls=%async_computation.18 | async-start | bytes 4730880 | tf_op jit(solution)/shard_map/all_gather | solution.py:316
  1888.6 282.7 %all-gather.88.cloned.1.call-start = ((), (), s32[]{:S(2)}) async-start(), calls=%async_computation.13 | async-start | bytes 4730880 | tf_op jit(solution)/shard_map/all_gather | solution.py:315
  1893.0 290.3 %all-gather.110.cloned.1.call-start = ((), (), s32[]{:S(2)}) async-start(), calls=%async_computation.24 | async-start | bytes 4730880 | tf_op jit(solution)/shard_map/all_gather | solution.py:317
  (191 other events, 9009.1 us)
Sparse Core Ops, SparseCore 0:
  27.2 46.1 all-gather.69
  199.7 49.8 all-gather.77
  252.3 51.9 all-gather.71
  373.5 44.0 all-reduce.32
  511.4 140.1 all-reduce.36
  726.4 50.2 all-gather.75
  779.7 54.2 all-gather.73
  836.6 46.5 all-gather.99
  940.7 49.5 all-gather.89
  993.3 46.2 all-gather.79
  1042.0 46.2 all-gather.101
  1090.7 46.3 all-gather.91
  1139.5 46.8 all-gather.81
  1188.9 46.3 all-gather.103
  1414.0 49.5 all-gather.93
  1466.2 46.2 all-gather.83
  1515.0 46.2 all-gather.105
  1564.0 46.3 all-gather.95
  1612.8 46.6 all-gather.85
  1662.0 45.9 all-gather.107
  1838.6 45.5 all-reduce.38
  1888.7 48.8 all-gather.97
  1939.9 46.6 all-gather.87
  1989.0 46.2 all-gather.109
  (5 shorter events, 205.3 us)
where the time goes:
time: 2220 us; the launch traced here: 2200 us
  blocking collectives  997 us (45%)
  waiting for transfers between devices  657 us (30%)
  local copies, waits for them, and re-layouts  260 us (12%)
  matrix products  171 us (8%)
  other arithmetic  53.2 us (2%)
  starting transfers between devices  39.4 us (2%)
  between operations  24.1 us (1%)
    unnamed x2, blocking collectives  196 us
    unnamed x398, local copies, waits for them, and re-layouts  185 us
    psum x4, waiting for transfers between devices, tensor_total(): lax.psum(partial_value.astype(jnp.bfloat16), 'tensor').astype(jnp.float32)  169 us
    all_gather x3, blocking collectives, local(): lax.all_gather(images_low[0], 'dp', axis=0, tiled=True)  84 us
    all_gather x3, waiting for transfers between devices, local(): lax.all_gather(images_low[5], 'dp', axis=0, tiled=True)  83.8 us
    psum x2, waiting for transfers between devices, local(): lax.psum(partial_value[0].astype(jnp.bfloat16), 'tensor')  83 us
    dot_general x42, matrix products, local(): jnp.dot(product, entire, preferred_element_type=jnp.float32)  80.4 us
    all_gather x3, blocking collectives, local(): lax.all_gather(images_low[2], 'dp', axis=0, tiled=True)  77.1 us
  transfers between devices with their start and end apart: 43, of which 18 were waited for; matrix products, arithmetic and copies ran while one was open for 20% of the time, Pallas kernels for 0%

commit v1 on v0

v1 whole, which is shorter than its diff:
```python
import functools
import math

import jax
import jax.numpy as jnp
import numpy as np
from jax import lax
from jax.experimental import pallas as pl
from jax.experimental.pallas import tpu as pltpu
from jax.sharding import PartitionSpec as P

WINDOW = 512
EPSILON = 1e-06
COEF_ONE = 3.4445
COEF_TWO = -4.775
COEF_THREE = 2.0315

D = 1152
HD = 256
TOK = 256
QTOK = 64
ROWS = 36
FFT = 1728
FFP = 1792
HALF = 896
BLK = 224
BF = jnp.bfloat16
F32 = jnp.float32
MESH = pl.DeviceIdType.MESH

SIZES = {"z": 4, "x": 4, "c": 2, "y": 4}


def place():
    dp = lax.axis_index("dp")
    return {"z": dp // 8, "x": (dp // 2) % 4, "c": dp % 2, "y": lax.axis_index("tensor")}


def rank(at, axes):
    r = 0
    for a in axes:
        r = r * SIZES[a] + at[a]
    return r


def count(axes):
    return math.prod(SIZES[a] for a in axes)


def decode(p, axes):
    out = {}
    for a in reversed(axes):
        out[a] = p % SIZES[a]
        p = p // SIZES[a]
    return out


def moved(at, off, sign):
    return {a: (at[a] + (off[a] if sign > 0 else SIZES[a] - off[a])) % SIZES[a] if a in off else at[a] for a in at}


def device(at):
    return {"dp": at["z"] * 8 + at["x"] * 2 + at["c"], "tensor": at["y"]}


def slot(ref, mode, axes, target):
    if mode == "ag":
        return ref
    if mode == "a2a":
        return ref.at[rank(target, axes)]
    return ref.at[rank(target, mode[1])]


def exchange_body(axes, modes, *refs):
    k = len(modes)
    n = count(axes)
    ins, outs = refs[:k], refs[k : 2 * k]
    send_sem, recv_sem, local_sem = refs[2 * k :]
    me = place()
    barrier = pltpu.get_barrier_semaphore()

    def greet(p, carry):
        pl.semaphore_signal(barrier, inc=1, device_id=device(moved(me, decode(p, axes), -1)), device_id_type=MESH)
        return carry

    def copies(p):
        off = decode(p, axes)
        target = moved(me, off, 1)
        return [
            pltpu.make_async_remote_copy(
                src_ref=slot(ins[i], modes[i], axes, target),
                dst_ref=outs[i].at[rank(me, axes)],
                send_sem=send_sem.at[i, p],
                recv_sem=recv_sem.at[i, p],
                device_id=device(target),
                device_id_type=MESH,
            )
            for i in range(k)
        ]

    def arrivals(p):
        off = decode(p, axes)
        target = moved(me, off, 1)
        source = moved(me, off, -1)
        return [
            pltpu.make_async_remote_copy(
                src_ref=slot(ins[i], modes[i], axes, target),
                dst_ref=outs[i].at[rank(source, axes)],
                send_sem=send_sem.at[i, p],
                recv_sem=recv_sem.at[i, p],
                device_id=device(target),
                device_id_type=MESH,
            )
            for i in range(k)
        ]

    def launch(p, carry):
        for copy in copies(p):
            copy.start()
        return carry

    def finish(p, carry):
        for copy in arrivals(p):
            copy.wait()
        return carry

    own = [
        pltpu.make_async_copy(slot(ins[i], modes[i], axes, me), outs[i].at[rank(me, axes)], local_sem.at[i])
        for i in range(k)
    ]
    lax.fori_loop(1, n, greet, 0)
    for copy in own:
        copy.start()
    pl.semaphore_wait(barrier, n - 1)
    lax.fori_loop(1, n, launch, 0)
    for copy in own:
        copy.wait()
    lax.fori_loop(1, n, finish, 0)


def exchange(items, axes, cid):
    arrays = [a for a, _ in items]
    modes = [m for _, m in items]
    n = count(axes)
    shapes = [a.shape if m == "ag" else a.shape[1:] for a, m in items]
    k = len(items)
    out = pl.pallas_call(
        functools.partial(exchange_body, axes, modes),
        out_shape=[jax.ShapeDtypeStruct((n,) + s, a.dtype) for s, a in zip(shapes, arrays)],
        in_specs=[pl.BlockSpec(memory_space=pl.ANY)] * k,
        out_specs=[pl.BlockSpec(memory_space=pl.ANY)] * k,
        scratch_shapes=[
            pltpu.SemaphoreType.DMA((k, n)),
            pltpu.SemaphoreType.DMA((k, n)),
            pltpu.SemaphoreType.DMA((k,)),
        ],
        compiler_params=pltpu.CompilerParams(collective_id=cid, has_side_effects=True),
    )(*arrays)
    return out


def halo_body(sign, kinds, *refs):
    k = len(kinds)
    ins, outs = refs[:k], refs[k : 2 * k]
    send_sem, recv_sem, local_sem = refs[2 * k :]
    dp = lax.axis_index("dp")
    y = lax.axis_index("tensor")
    barrier = pltpu.get_barrier_semaphore()
    offs = [(d, t) for d in range(3) for t in range(4)]

    def dev(d, t, way):
        shift = d if way > 0 else 32 - d
        return {"dp": (dp + shift) % 32, "tensor": (y + (t if way > 0 else 4 - t)) % 4}

    for d, t in offs[1:]:
        back = dev(d, t, -1) if sign > 0 else {"dp": (dp + d) % 32, "tensor": (y + 4 - t) % 4}
        pl.semaphore_signal(barrier, inc=1, device_id=back, device_id_type=MESH)
    own = []
    copies = []
    for i, kind in enumerate(kinds):
        for p, (d, t) in enumerate(offs):
            if kind == "near" and d > 0:
                continue
            ty = (y + t) % 4
            sy = (y + 4 - t) % 4
            src = ins[i].at[d, ty] if kind == "split" else ins[i]
            tdp = (dp + d) % 32 if sign > 0 else (dp + 32 - d) % 32
            if kind == "near":
                to, frm = outs[i].at[y], outs[i].at[sy]
            else:
                to, frm = outs[i].at[d, y], outs[i].at[d, sy]
            if p == 0:
                own.append(pltpu.make_async_copy(src, to, local_sem.at[i]))
                continue
            args = dict(send_sem=send_sem.at[i, p], recv_sem=recv_sem.at[i, p], device_id={"dp": tdp, "tensor": ty}, device_id_type=MESH)
            copies.append(
                (
                    pltpu.make_async_remote_copy(src_ref=src, dst_ref=to, **args),
                    pltpu.make_async_remote_copy(src_ref=src, dst_ref=frm, **args),
                )
            )
    for copy in own:
        copy.start()
    pl.semaphore_wait(barrier, len(offs) - 1)
    for out_copy, _ in copies:
        out_copy.start()
    for copy in own:
        copy.wait()
    for _, in_copy in copies:
        in_copy.wait()


def halo(items, sign, cid):
    arrays = [a for a, _ in items]
    kinds = [m for _, m in items]
    shapes = []
    for a, m in items:
        shapes.append((4,) + a.shape if m == "near" else (3, 4) + (a.shape[2:] if m == "split" else a.shape))
    k = len(items)
    return pl.pallas_call(
        functools.partial(halo_body, sign, kinds),
        out_shape=[jax.ShapeDtypeStruct(s, a.dtype) for s, a in zip(shapes, arrays)],
        in_specs=[pl.BlockSpec(memory_space=pl.ANY)] * k,
        out_specs=[pl.BlockSpec(memory_space=pl.ANY)] * k,
        scratch_shapes=[
            pltpu.SemaphoreType.DMA((k, 12)),
            pltpu.SemaphoreType.DMA((k, 12)),
            pltpu.SemaphoreType.DMA((k,)),
        ],
        compiler_params=pltpu.CompilerParams(collective_id=cid, has_side_effects=True),
    )(*arrays)


def sum_body(fn, rs_axes, ag_axes, n_extra, n_local, n_ag, *refs):
    parts = refs[0]
    extras = refs[1 : 1 + n_extra]
    locals_ = refs[1 + n_extra : 1 + n_extra + n_local]
    gathers = refs[1 + n_extra + n_local : 1 + n_extra + n_local + n_ag]
    recv, agbuf, rs_send, rs_recv, ag_send, ag_recv, local_sem = refs[1 + n_extra + n_local + n_ag :]
    me = place()
    union = rs_axes if len(rs_axes) >= len(ag_axes) else ag_axes
    barrier = pltpu.get_barrier_semaphore()
    for p in range(1, count(union)):
        pl.semaphore_signal(barrier, inc=1, device_id=device(moved(me, decode(p, union), -1)), device_id_type=MESH)
    own = pltpu.make_async_copy(parts.at[rank(me, rs_axes)], recv.at[rank(me, rs_axes)], local_sem.at[0])
    own.start()
    pl.semaphore_wait(barrier, count(union) - 1)

    def send(p, axes, src, dst, send_sem, recv_sem):
        off = decode(p, axes)
        target, source = moved(me, off, 1), moved(me, off, -1)
        source_ref = src(target)
        args = dict(send_sem=send_sem, recv_sem=recv_sem, device_id=device(target), device_id_type=MESH)
        out_copy = pltpu.make_async_remote_copy(src_ref=source_ref, dst_ref=dst.at[rank(me, axes)], **args)
        in_copy = pltpu.make_async_remote_copy(src_ref=source_ref, dst_ref=dst.at[rank(source, axes)], **args)
        return out_copy, in_copy

    moves = [
        send(p, rs_axes, lambda t: parts.at[rank(t, rs_axes)], recv, rs_send.at[p], rs_recv.at[p])
        for p in range(1, count(rs_axes))
    ]
    for out_copy, _ in moves:
        out_copy.start()
    own.wait()
    for _, in_copy in moves:
        in_copy.wait()
    total = recv[0].astype(F32)
    for i in range(1, count(rs_axes)):
        total = total + recv[i].astype(F32)
    local_vals, ag_vals = fn(total, *[e[...] for e in extras])
    for i, value in enumerate(ag_vals):
        agbuf[i] = value.astype(BF)
    moves = []
    own = []
    for i in range(n_ag):
        own.append(pltpu.make_async_copy(agbuf.at[i], gathers[i].at[rank(me, ag_axes)], local_sem.at[1 + i]))
        for p in range(1, count(ag_axes)):
            moves.append(send(p, ag_axes, lambda t, i=i: agbuf.at[i], gathers[i], ag_send.at[i, p], ag_recv.at[i, p]))
    for out_copy, _ in moves:
        out_copy.start()
    for copy in own:
        copy.start()
    for ref, value in zip(locals_, local_vals):
        ref[...] = value
    for copy in own:
        copy.wait()
    for _, in_copy in moves:
        in_copy.wait()


def sum_then_gather(fn, parts, extras, local_shapes, n_ag, rs_axes, ag_axes, cid):
    n_rs, n_g = count(rs_axes), count(ag_axes)
    rows = parts.shape[1:]
    vmem = pl.BlockSpec(memory_space=pltpu.VMEM)
    hbm = pl.BlockSpec(memory_space=pl.ANY)
    return pl.pallas_call(
        functools.partial(sum_body, fn, rs_axes, ag_axes, len(extras), len(local_shapes), n_ag),
        out_shape=[jax.ShapeDtypeStruct(s, F32) for s in local_shapes]
        + [jax.ShapeDtypeStruct((n_g,) + rows, BF)] * n_ag,
        in_specs=[hbm] + [vmem] * len(extras),
        out_specs=[vmem] * len(local_shapes) + [hbm] * n_ag,
        scratch_shapes=[
            pltpu.VMEM((n_rs,) + rows, BF),
            pltpu.VMEM((n_ag,) + rows, BF),
            pltpu.SemaphoreType.DMA((n_rs,)),
            pltpu.SemaphoreType.DMA((n_rs,)),
            pltpu.SemaphoreType.DMA((n_ag, n_g)),
            pltpu.SemaphoreType.DMA((n_ag, n_g)),
            pltpu.SemaphoreType.DMA((1 + n_ag,)),
        ],
        compiler_params=pltpu.CompilerParams(
            collective_id=cid, has_side_effects=True, vmem_limit_bytes=32 * 1024 * 1024
        ),
    )(parts, *extras)


def inv_rms(values):
    return lax.rsqrt(jnp.mean(values * values, axis=-1, keepdims=True) + EPSILON)


def rms_back(values, gain, s, grad):
    scaled = gain * grad
    dv = s * scaled - values * (s * s * s * jnp.mean(scaled * values, axis=-1, keepdims=True))
    return dv, jnp.sum(grad * values * s, axis=0, keepdims=True)


def rot(values, cosine, sine):
    front, back = values[:, :128], values[:, 128:]
    return jnp.concatenate([front * cosine - back * sine, back * cosine + front * sine], axis=-1)


def unrot(values, cosine, sine):
    return rot(values, cosine, -sine)


def mid_fn(u, hidden, g1, g2):
    hmid = hidden + u * inv_rms(u) * g1
    return [u, hmid], [hmid * inv_rms(hmid) * g2]


def ffn_out_fn(f, hmid, out_grad, g3):
    s = inv_rms(f)
    block = hmid + f * s * g3
    df, dg3 = rms_back(f, g3, s, out_grad)
    return [block, dg3], [df]


def ffn_in_fn(dbin, hmid, u, out_grad, g1, g2):
    dm, dg2 = rms_back(hmid, g2, inv_rms(hmid), dbin)
    dhmid = out_grad + dm
    du, dg1 = rms_back(u, g1, inv_rms(u), dhmid)
    return [dhmid, dg1, dg2], [du]


def last_fn(da, hidden, dhmid, block, g0):
    dh, dg0 = rms_back(hidden, g0, inv_rms(hidden), da)
    return [dg0], [dhmid + dh, block]


def dot(a, b, dims):
    return lax.dot_general(a, b, (dims, ((), ())), preferred_element_type=F32)


NN = ((1,), (0,))
NT = ((1,), (1,))
TN = ((0,), (0,))


def rope_tables():
    freqs = 10000.0 ** (-np.arange(128, dtype=np.float64) * 2.0 / 256)
    base = (np.arange(32, dtype=np.float64) - 2)[:, None] * 256 * freqs[None]
    step = np.arange(768, dtype=np.float64)[:, None] * freqs[None]
    return [t.astype(np.float32) for t in (np.cos(base), np.sin(base), np.cos(step), np.sin(step))]


def to_columns(ffn, attn):
    big = jnp.pad(ffn, ((0, 0), (0, 0), (0, FFP - FFT))).reshape(3, ROWS, 2, 4, BLK)
    big = big.transpose(0, 3, 2, 1, 4).reshape(24, ROWS, BLK)
    small = []
    for piece in attn:
        half = piece.shape[1] // 2
        piece = piece.reshape(ROWS, 2, half).transpose(1, 0, 2)
        small.append(jnp.pad(piece, ((0, 0), (0, 0), (0, BLK - half))))
    return jnp.concatenate([big] + small, axis=0)


def from_columns(blocks):
    big = blocks[:24].reshape(3, 4, 2, ROWS, BLK).transpose(0, 3, 2, 1, 4).reshape(3, ROWS, FFP)[:, :, :FFT]
    small = []
    for i, half in enumerate((128, 128, 32, 32)):
        piece = blocks[24 + 2 * i : 26 + 2 * i, :, :half]
        small.append(piece.transpose(1, 0, 2).reshape(ROWS, 2 * half))
    return big, small


def orthogonal(gram, columns):
    diag = jnp.sum(jnp.where(jnp.eye(D, dtype=bool), gram.astype(F32), 0.0))
    inv = 1.0 / (jnp.sqrt(diag) + 1e-07)
    a = (gram.astype(F32) * inv * inv).astype(BF)
    x = columns * inv
    for i in range(3):
        r = (COEF_TWO * a.astype(F32) + COEF_THREE * dot(a, a, NN)).astype(BF)
        x = COEF_ONE * x + dot(x.astype(BF), r, NN)
        if i < 2:
            t = (COEF_ONE * a.astype(F32) + dot(a, r, NN)).astype(BF)
            a = (COEF_ONE * t.astype(F32) + dot(t, r, NN)).astype(BF)
    return x


def local(
    hidden_in,
    out_grad,
    segment_ids,
    w_query,
    w_keyval,
    w_output,
    w_gateup,
    w_down,
    norm_gains,
    qk_gains,
    mom_query,
    mom_keyval,
    mom_output,
    mom_gateup,
    mom_down,
    gain_moms,
    qk_moms,
):
    dp = lax.axis_index("dp")
    y = lax.axis_index("tensor")
    z, x, c = dp // 8, (dp // 2) % 4, dp % 2

    attn_w = jnp.concatenate(
        [
            w_query,
            w_output.T,
            w_keyval[0],
            w_keyval[1],
            norm_gains.T,
            jnp.broadcast_to(qk_gains.reshape(1, 4), (ROWS, 4)),
            jnp.zeros((ROWS, 120), F32),
        ],
        axis=1,
    ).astype(BF)
    segs = segment_ids.reshape(2, 128)
    attn_all, segs_all = exchange([(attn_w, "ag"), (segs, "ag")], ("z", "x", "c"), 1)
    weights = attn_all.reshape(D, 768)
    wq, woT, wkv = weights[:, :256], weights[:, 256:512], weights[:, 512:640]
    gains = weights[:, 640:644].T.astype(F32)
    g0, g1, g2, g3 = (gains[i : i + 1] for i in range(4))
    qk_mine = jnp.pad(attn_all[:, 0, 644:648].reshape(32, 2, 2).transpose(1, 0, 2).reshape(2, 64), ((0, 14), (0, 64)))

    ffn_w = jnp.concatenate([w_gateup, w_down.T[None]], axis=0).astype(BF)
    ffn_w = jnp.pad(ffn_w, ((0, 0), (0, 0), (0, FFP - FFT))).reshape(3, ROWS, 2, HALF).transpose(2, 0, 1, 3)
    moms = to_columns(
        jnp.concatenate([mom_gateup, mom_down.T[None]], axis=0).astype(BF),
        [m.astype(BF) for m in (mom_query, mom_output.T, mom_keyval[0], mom_keyval[1])],
    )

    cos_b, sin_b, cos_s, sin_s = (jnp.asarray(t) for t in rope_tables())
    cb = lax.dynamic_slice_in_dim(cos_b, dp, 1, 0)
    sb = lax.dynamic_slice_in_dim(sin_b, dp, 1, 0)
    cosine = cb * cos_s - sb * sin_s
    sine = sb * cos_s + cb * sin_s
    cos_q, sin_q = cosine[512:], sine[512:]

    normed = (hidden_in * inv_rms(hidden_in) * g0).astype(BF)
    proj = dot(normed, jnp.concatenate([wq, wkv], axis=1), NN)
    q_raw = proj[:, :256]
    kv_all, qk_all = halo([(proj[:, 256:].astype(BF), "all"), (qk_mine, "near")], 1, 2)
    qk_full = qk_all[:, :2, :64].reshape(4, 2, 32, 2).transpose(1, 2, 0, 3).reshape(2, HD).astype(F32)
    gq, gk = qk_full[0:1], qk_full[1:2]
    kv_all = kv_all[::-1].reshape(3, 4, TOK, 2, 64).transpose(3, 0, 2, 1, 4).reshape(2, 3 * TOK, HD)
    k_raw = kv_all[0].astype(F32)
    vb = kv_all[1]
    q_s = inv_rms(q_raw)
    qr = rot(q_raw * q_s * gq, cos_q, sin_q).astype(BF)
    kr = rot(k_raw * inv_rms(k_raw) * gk, cosine, sine).astype(BF)
    first = jnp.maximum(dp - 2, 0)
    seg_rows = lax.dynamic_slice_in_dim(segs_all.reshape(32, TOK), first, 3, 0)
    seg_keys = jnp.where(
        dp >= 2, seg_rows, jnp.where(dp == 1, jnp.roll(seg_rows, 1, axis=0), jnp.roll(seg_rows, 2, axis=0))
    ).reshape(3 * TOK)
    key_no = jnp.arange(3 * TOK, dtype=jnp.int32)
    gap = (jnp.arange(TOK, dtype=jnp.int32) + 2 * TOK)[:, None] - key_no[None, :]
    allowed = (
        (segment_ids[:, None] == seg_keys[None, :])
        & (gap >= 0)
        & (gap < WINDOW)
        & (key_no + (dp - 2) * TOK >= 0)[None, :]
    )
    scale = HD ** (-0.5)
    scores = jnp.where(allowed, dot(qr, kr, NT) * scale, -1e30)
    top = jnp.max(scores, axis=-1, keepdims=True)
    exps = jnp.exp(scores - top)
    probs = exps / jnp.sum(exps, axis=-1, keepdims=True)
    pb = probs.astype(BF)
    ob = dot(pb, vb, NN).astype(BF)
    u_part = dot(ob, woT, NT).astype(BF).reshape(4, QTOK, D)
    hidden_q = lax.dynamic_slice_in_dim(hidden_in, y * QTOK, QTOK, 0)
    grad_q = lax.dynamic_slice_in_dim(out_grad, y * QTOK, QTOK, 0)
    u, hmid, bin_all = sum_then_gather(
        mid_fn, u_part, [hidden_q, g1, g2], [(QTOK, D)] * 2, 1, ("y",), ("c", "y"), 3
    )

    ffn_all, moms_all = exchange([(ffn_w, ("by", ("c",))), (moms, "a2a")], ("z", "x", "c"), 4)
    ffn_full = ffn_all.transpose(1, 0, 2, 3).reshape(3, D, HALF)
    wg, wu, wdT = ffn_full[0], ffn_full[1], ffn_full[2]
    bin_low = bin_all.reshape(512, D)
    gate = dot(bin_low, wg, NN)
    up = dot(bin_low, wu, NN)
    inner = math.sqrt(2.0 / math.pi)
    th = jnp.tanh(inner * (gate + 0.044715 * gate * gate * gate))
    gelu = 0.5 * gate * (1.0 + th)
    gelu_d = 0.5 * (1.0 + th) + 0.5 * gate * (1.0 - th * th) * inner * (1.0 + 3 * 0.044715 * gate * gate)
    mixed = (gelu * up).astype(BF)
    f_part = dot(mixed, wdT, NT).astype(BF).reshape(8, QTOK, D)
    block, dg3, df_all = sum_then_gather(
        ffn_out_fn, f_part, [hmid, grad_q, g3], [(QTOK, D), (1, D)], 1, ("c", "y"), ("c", "y"), 5
    )
    dfb = df_all.reshape(512, D)
    dz = dot(dfb, wdT, NN)
    dgate = (dz * up * gelu_d).astype(BF)
    dup = (dz * gelu).astype(BF)
    dbin_part = (dot(dgate, wg, NT) + dot(dup, wu, NT)).astype(BF).reshape(8, QTOK, D)
    dhmid, dg1, dg2, du_all = sum_then_gather(
        ffn_in_fn,
        dbin_part,
        [hmid, u, grad_q, g1, g2],
        [(QTOK, D), (1, D), (1, D)],
        1,
        ("c", "y"),
        ("c", "y"),
        6,
    )

    dub_all = du_all.reshape(512, D)
    dub = lax.dynamic_slice_in_dim(dub_all, c * TOK, TOK, 0)
    dob = dot(dub, woT, NN).astype(BF)
    dP = dot(dob, vb, NT)
    ds = (probs * (dP - jnp.sum(probs * dP, axis=-1, keepdims=True))).astype(BF)
    dqr = dot(ds, kr, NN) * scale
    dkr = dot(ds, qr, TN) * scale
    dv = dot(pb, dob, TN)
    dkv_part = jnp.concatenate([dkr, dv], axis=1).astype(BF).reshape(3, 4, QTOK, 512)[::-1]
    (dkv_got,) = halo([(dkv_part, "split")], -1, 7)
    dkv_sum = jnp.sum(dkv_got.reshape(12, QTOK, 512).astype(F32), axis=0)
    k_own = lax.dynamic_slice_in_dim(k_raw, 2 * TOK + y * QTOK, QTOK, 0)
    cos_k = lax.dynamic_slice_in_dim(cos_q, y * QTOK, QTOK, 0)
    sin_k = lax.dynamic_slice_in_dim(sin_q, y * QTOK, QTOK, 0)
    dk, dgk = rms_back(k_own, gk, inv_rms(k_own), unrot(dkv_sum[:, :256], cos_k, sin_k))
    dq, dgq = rms_back(q_raw, gq, q_s, unrot(dqr, cos_q, sin_q))
    dkvb = jnp.concatenate([dk, dkv_sum[:, 256:]], axis=1).astype(BF)
    dqb = dq.astype(BF)
    (dkv_all,) = exchange([(dkvb, "ag")], ("c", "y"), 8)
    pair, = exchange([(jnp.concatenate([normed, ob, dqb], axis=1), "ag")], ("c",), 9)
    pair = pair.reshape(512, D + 512)
    dkv_all = dkv_all.reshape(512, 2, 4, 64)
    dkv_cols = lax.dynamic_slice_in_dim(dkv_all, y, 1, 2).reshape(512, 128)
    da_part = (
        dot(
            jnp.concatenate([dqb, lax.dynamic_slice_in_dim(dkv_cols, c * TOK, TOK, 0)], axis=1),
            jnp.concatenate([wq, wkv], axis=1),
            NT,
        )
        .astype(BF)
        .reshape(4, QTOK, D)
    )
    dg0, last_in, last_out = sum_then_gather(
        last_fn, da_part, [hidden_q, dhmid, block, g0], [(1, D)], 2, ("y",), ("y",), 10
    )
    input_grad = last_in.reshape(TOK, D).astype(F32)
    block_out = last_out.reshape(TOK, D).astype(F32)

    qk_row = jnp.concatenate([dgq, dgk, jnp.zeros((1, D - 2 * HD), F32)], axis=1)
    gain_sum = lax.psum(jnp.concatenate([dg0, dg1, dg2, dg3, qk_row], axis=0), ("dp", "tensor"))
    gains_red = lax.dynamic_slice(gain_sum, (0, dp * ROWS), (4, ROWS))
    qk_red = lax.dynamic_slice_in_dim(gain_sum[4, : 2 * HD].reshape(2, HD), (dp * 4 + y) * 2, 2, 1)
    gain_rate = 2.0 / math.sqrt(8192)
    next_gain_moms = 0.9 * gain_moms + 0.1 * gains_red
    new_norm_gains = norm_gains - gain_rate * next_gain_moms
    next_qk_moms = 0.9 * qk_moms + 0.1 * qk_red
    new_qk_gains = qk_gains - gain_rate * next_qk_moms

    a_all, ob_all, dq_all = pair[:, :D], pair[:, D : D + 256], pair[:, D + 256 :]
    ob_cols = lax.dynamic_slice_in_dim(ob_all, c * 128, 128, 1)
    dq_cols = lax.dynamic_slice_in_dim(dq_all, c * 128, 128, 1)
    dk_cols = lax.dynamic_slice_in_dim(dkv_cols, c * 32, 32, 1)
    dv_cols = lax.dynamic_slice_in_dim(dkv_cols, 64 + c * 32, 32, 1)
    d_gate = dot(dgate, bin_low, TN).astype(BF)
    d_up = dot(dup, bin_low, TN).astype(BF)
    d_down = dot(mixed, dfb, TN).astype(BF)
    d_q = dot(dq_cols, a_all, TN).astype(BF)
    d_kv = dot(jnp.concatenate([dk_cols, dv_cols], axis=1), a_all, TN).astype(BF)
    d_o = dot(ob_cols, dub_all, TN).astype(BF)
    wgrads = jnp.concatenate(
        [
            d_gate.reshape(4, BLK, D),
            d_up.reshape(4, BLK, D),
            d_down.reshape(4, BLK, D),
            jnp.pad(d_q, ((0, BLK - 128), (0, 0)))[None],
            jnp.pad(d_o, ((0, BLK - 128), (0, 0)))[None],
            jnp.pad(d_kv[:32], ((0, BLK - 32), (0, 0)))[None],
            jnp.pad(d_kv[32:], ((0, BLK - 32), (0, 0)))[None],
        ],
        axis=0,
    )
    (wgrads_got,) = exchange([(wgrads, "a2a")], ("z", "x"), 11)
    wgrad = jnp.sum(wgrads_got.astype(F32), axis=0)

    mom = 0.95 * moms_all.reshape(D, BLK).T.astype(F32) + wgrad
    mom_low = mom.astype(BF)
    gram_part = dot(mom_low, mom_low, TN).astype(BF).reshape(32, ROWS, D)
    (gram_got,) = exchange([(gram_part, "a2a")], ("x", "y", "c"), 12)
    by_x = jnp.sum(gram_got.reshape(4, 8, ROWS, D).astype(F32), axis=1)
    by_x = jnp.where(z < 3, jnp.sum(by_x, axis=0, keepdims=True), by_x).astype(BF)
    (gram,) = exchange([(by_x, ("by", ("x",)))], ("x", "y", "c"), 13)
    ortho = orthogonal(gram.reshape(D, D), mom)
    back = jnp.concatenate([ortho.astype(BF), wgrad.astype(BF)], axis=0).T.reshape(32, ROWS, 2 * BLK)
    (back_got,) = exchange([(back, "a2a")], ("z", "x", "c"), 14)
    o_big, o_small = from_columns(back_got[:, :, :BLK].astype(F32))
    w_big, w_small = from_columns(back_got[:, :, BLK:].astype(F32))

    def step(columns):
        return 0.15 * 0.2 * math.sqrt(max(D, columns))

    new_query = w_query - step(1024) * o_small[0]
    new_output = w_output - step(1024) * o_small[1].T
    new_keyval = w_keyval - step(256) * jnp.stack(o_small[2:])
    new_gateup = w_gateup - step(6912) * o_big[:2]
    new_down = w_down - step(6912) * o_big[2].T
    next_query = 0.95 * mom_query + w_small[0]
    next_output = 0.95 * mom_output + w_small[1].T
    next_keyval = 0.95 * mom_keyval + jnp.stack(w_small[2:])
    next_gateup = 0.95 * mom_gateup + w_big[:2]
    next_down = 0.95 * mom_down + w_big[2].T
    return (
        block_out,
        input_grad,
        new_query,
        new_keyval,
        new_output,
        new_gateup,
        new_down,
        next_query,
        next_keyval,
        next_output,
        next_gateup,
        next_down,
        new_norm_gains,
        next_gain_moms,
        new_qk_gains,
        next_qk_moms,
    )


def solution(mesh):
    return jax.shard_map(
        local,
        mesh=mesh,
        in_specs=(
            P("dp", None),
            P("dp", None),
            P("dp"),
            P("dp", "tensor"),
            P(None, "dp", "tensor"),
            P("tensor", "dp"),
            P(None, "dp", "tensor"),
            P("tensor", "dp"),
            P(None, "dp"),
            P(None, ("dp", "tensor")),
            P("dp", "tensor"),
            P(None, "dp", "tensor"),
            P("tensor", "dp"),
            P(None, "dp", "tensor"),
            P("tensor", "dp"),
            P(None, "dp"),
            P(None, ("dp", "tensor")),
        ),
        out_specs=(
            P("dp", None),
            P("dp", None),
            P("dp", "tensor"),
            P(None, "dp", "tensor"),
            P("tensor", "dp"),
            P(None, "dp", "tensor"),
            P("tensor", "dp"),
            P("dp", "tensor"),
            P(None, "dp", "tensor"),
            P("tensor", "dp"),
            P(None, "dp", "tensor"),
            P("tensor", "dp"),
            P(None, "dp"),
            P(None, "dp"),
            P(None, ("dp", "tensor")),
            P(None, ("dp", "tensor")),
        ),
        check_vma=False,
    )
```

time: 2220 us -> 936 us (0.42)
  blocking collectives: 997 us -> 65.8 us
  waiting for transfers between devices: 657 us -> 0 us
  Pallas kernels: 0 us -> 627 us
  local copies, waits for them, and re-layouts: 260 us -> 91.2 us
  matrix products: 171 us -> 79.5 us
  starting transfers between devices: 39.4 us -> 0 us
    all_gather x30 -> x0, blocking collectives: 727 us -> none  [the longest x3 84 us: local(): lax.all_gather(images_low[0], 'dp', axis=0, tiled=True)]
    pallas_call x0 -> x14, Pallas kernels: none -> 627 us  [the longest x8 481 us: exchange(): pl.pallas_call(functools.partial(exchange_body, axes, modes), out_shape=[...]
    all_gather x21 -> x0, waiting for transfers between devices: 332 us -> none  [the longest x3 83.8 us: local(): lax.all_gather(images_low[5], 'dp', axis=0, tiled=True)]
    psum x7 -> x0, waiting for transfers between devices: 282 us -> none  [the longest x4 169 us: tensor_total(): lax.psum(partial_value.astype(jnp.bfloat16), 'tensor').astype(jnp.float32)]
    unnamed x2 -> x0, blocking collectives: 196 us -> none
    unnamed x398 -> x182, local copies, waits for them, and re-layouts: 185 us -> 22.4 us
    dot_general x84 -> x32, matrix products: 171 us -> 79.5 us  [dot(): return lax.dot_general(a, b, (dims, ((), ())), preferred_element_type=F32)]
    unnamed x38 -> x0, waiting for transfers between devices: 38.4 us -> none
  transfers between devices with their start and end apart: 43 -> 0, of which waited for: 18 -> 0; matrix products, arithmetic and copies ran while one was open for 20% -> 0% of each run, Pallas kernels for 0% -> 0%
where the time goes in v1:
time: 936 us; the launch traced here: 925 us
  Pallas kernels  627 us (67%)
  local copies, waits for them, and re-layouts  91.2 us (10%)
  matrix products  79.5 us (8%)
  blocking collectives  65.8 us (7%)
  other arithmetic  58.8 us (6%)
    pallas_call x8, Pallas kernels, exchange(): pl.pallas_call(functools.partial(exchange_body, axes, modes), out_shape=[...  481 us
    pallas_call x4, Pallas kernels, sum_then_gather(): pl.pallas_call(functools.partial(sum_body, fn, rs_axes, ag_axes, len(extr...  116 us
    dot_general x32, matrix products, dot(): return lax.dot_general(a, b, (dims, ((), ())), preferred_element_type=F32)  79.5 us
    psum x1, blocking collectives, local(): lax.psum(jnp.concatenate([dg0, dg1, dg2, dg3, qk_row], axis=0), ('dp', 't...  65.8 us
    pallas_call x2, Pallas kernels, halo(): pl.pallas_call(functools.partial(halo_body, sign, kinds), out_shape=[jax....  29.5 us
    unnamed x182, local copies, waits for them, and re-layouts  22.4 us

profile of v1, /device:TPU:1, one launch (start us, length us, event | category | flops | bytes accessed | tf_op | source)
XLA Modules:
  0.0 925.2 jit_solution(1563543313931988499)
XLA Ops:
  5.3 39.7 %shard_map.324 = (bf16[32,36,768]{2,1,0:T(8,128)(2,1)}, s32[32,2,128]{2,1,0:T(2,128)}) custom-call(bf16[36,768]{1,0:T(8,128)(2,1)} %concatenate.75.refs_0_, s32[2,128]{1,0:T(2,128)} %bitcast.263), custom_call_target="tpu_custom_call" | custom-call | tf_op jit(solution)/shard_map/pallas_call | solution.py:147
  54.3 19.1 %shard_map.325 = (bf16[3,4,256,128]{3,2,1,0:T(8,128)(2,1)}, bf16[4,16,128]{2,1,0:T(8,128)(2,1)}) custom-call(bf16[256,128]{1,0:T(8,128)(2,1)} %slice.394.refs_0_, bf16[16,128]{1,0:T(8,128)(2,1)} %pad.39.refs_1_), custom_call_target="tpu_custom_call" | custom-call | tf_op jit(solution)/shard_map/pallas_call | solution.py:220
  93.1 26.0 %shard_map.326 = (f32[64,1152]{1,0:T(8,128)S(1)}, f32[64,1152]{1,0:T(8,128)S(1)}, bf16[8,64,1152]{2,1,0:T(8,128)(2,1)S(1)}) custom-call(bf16[4,64,1152]{2,1,0:T(8,128)(2,1)S(1)} %bitcast.208, f32[64,1152]{1,0:T(8,128)S(1)} %get-tuple-element.169.refs_1_, f32[1,1152]{1,0:T(1,128)S(1)} %get-tuple-element.159.refs_2_.refs_4_, ...), custom_call_target="tpu_custom_call" | custom-call | tf_op jit(solution)/shard_map/pallas_call | solution.py:296
  134.2 128.9 %shard_map.327 = (bf16[32,3,36,896]{3,2,1,0:T(8,128)(2,1)}, bf16[32,36,224]{2,1,0:T(8,128)(2,1)}) custom-call(bf16[2,3,36,896]{3,2,1,0:T(8,128)(2,1)} %bitcast.234, bf16[32,36,224]{2,1,0:T(8,128)(2,1)} %pad_dynamic-update-slice_fusion.refs_1_), custom_call_target="tpu_custom_call" | custom-call | tf_op jit(solution)/shard_map/pallas_call | solution.py:147
  263.2 6.0 fusion.88
  281.5 5.3 multiply_convert_fusion.1
  294.2 32.3 %shard_map.328 = (f32[64,1152]{1,0:T(8,128)S(1)}, f32[1,1152]{1,0:T(1,128)S(1)}, bf16[8,64,1152]{2,1,0:T(8,128)(2,1)S(1)}) custom-call(bf16[8,64,1152]{2,1,0:T(8,128)(2,1)S(1)} %bitcast.212, f32[64,1152]{1,0:T(8,128)S(1)} %get-tuple-element.41.refs_1_, f32[64,1152]{1,0:T(8,128)S(1)} %get-tuple-element.168.refs_2_.refs_3_, ...), custom_call_target="tpu_custom_call" | custom-call | tf_op jit(solution)/shard_map/pallas_call | solution.py:296
  332.8 33.2 %shard_map.329 = (f32[64,1152]{1,0:T(8,128)S(1)}, f32[1,1152]{1,0:T(1,128)S(1)}, f32[1,1152]{1,0:T(1,128)S(1)}, bf16[8,64,1152]{2,1,0:T(8,128)(2,1)S(1)}) custom-call(bf16[8,64,1152]{2,1,0:T(8,128)(2,1)S(1)} %bitcast.209, f32[64,1152]{1,0:T(8,128)S(1)} %get-tuple-element.41.refs_1_, f32[64,1152]{1,0:T(8,128)S(1)} %get-tuple-element.43.refs_2_, ...), custom_call_target="tpu_custom_call" | custom-call | tf_op jit(solution)/shard_map/pallas_call | solution.py:296
  374.7 10.3 %shard_map.330 = bf16[3,4,64,512]{3,2,1,0:T(8,128)(2,1)} custom-call(bf16[3,4,64,512]{3,2,1,0:T(8,128)(2,1)} %rev.7.refs_0_), custom_call_target="tpu_custom_call" | custom-call | tf_op jit(solution)/shard_map/pallas_call | solution.py:220
  390.2 13.9 %shard_map.331 = bf16[8,64,512]{2,1,0:T(8,128)(2,1)} custom-call(bf16[64,512]{1,0:T(8,128)(2,1)} %pad_maximum_fusion.13.refs_0_), custom_call_target="tpu_custom_call" | custom-call | tf_op jit(solution)/shard_map/pallas_call | solution.py:147
  410.8 24.4 %shard_map.332 = (f32[1,1152]{1,0:T(1,128)S(1)}, bf16[4,64,1152]{2,1,0:T(8,128)(2,1)S(1)}, bf16[4,64,1152]{2,1,0:T(8,128)(2,1)S(1)}) custom-call(bf16[4,64,1152]{2,1,0:T(8,128)(2,1)S(1)} %bitcast.213, f32[64,1152]{1,0:T(8,128)S(1)} %get-tuple-element.169.refs_1_, f32[64,1152]{1,0:T(8,128)S(1)} %copy-done.1, f32[64,1152]{1,0:T(8,128)S(1)} %get-tuple-element.46.refs_3_, ...), custom_call_target="tpu_custom_call" | custom-call | tf_op jit(solution)/shard_map/pallas_call | solution.py:296
  435.3 65.8 %psum.7 = f32[5,1152]{1,0:T(8,128)S(1)} all-reduce(f32[5,1152]{1,0:T(8,128)S(1)} %concatenate.96), channel_id=1, replica_groups=mesh['dp'=32,'tensor'=4] {'dp','tensor'}, use_global_device_ids=true, to_apply=%region_16.17 | all-reduce | flops 5760 | bytes 46080 | tf_op jit(solution)/shard_map/psum | solution.py:576
  505.9 27.0 %shard_map.333 = bf16[2,256,1664]{2,1,0:T(8,128)(2,1)} custom-call(bf16[256,1664]{1,0:T(8,128)(2,1)} %pad_maximum_fusion.1.refs_0_), custom_call_target="tpu_custom_call" | custom-call | tf_op jit(solution)/shard_map/pallas_call | solution.py:147
  551.2 138.4 %shard_map.334 = bf16[16,224,1152]{2,1,0:T(8,128)(2,1)} custom-call(bf16[16,224,1152]{2,1,0:T(8,128)(2,1)} %bitcast_dynamic-update-slice_fusion.refs_0_), custom_call_target="tpu_custom_call" | custom-call | tf_op jit(solution)/shard_map/pallas_call | solution.py:147
  689.7 4.8 convert_reduce_fusion
  699.9 5.1 reshape.305.refs_0_
  705.0 52.6 %shard_map.335 = bf16[32,36,1152]{2,1,0:T(8,128)(2,1)} custom-call(bf16[32,36,1152]{2,1,0:T(8,128)(2,1)} %reshape.305.refs_0_), custom_call_target="tpu_custom_call" | custom-call | tf_op jit(solution)/shard_map/pallas_call | solution.py:147
  762.1 53.7 %shard_map.336 = bf16[32,36,1152]{2,1,0:T(8,128)(2,1)} custom-call(bf16[4,36,1152]{2,1,0:T(8,128)(2,1)} %select_convert_fusion.refs_0_), custom_call_target="tpu_custom_call" | custom-call | tf_op jit(solution)/shard_map/pallas_call | solution.py:147
  825.2 5.2 convert_element_type.292
  830.4 7.5 fusion.5
  850.3 4.6 fusion.8
  854.9 5.2 fusion.9
  862.0 9.1 fusion.14
  874.3 27.1 %shard_map.337 = bf16[32,36,448]{2,1,0:T(8,128)(2,1)} custom-call(bf16[32,36,448]{2,1,0:T(8,128)(2,1)} %reshape.306.refs_0_), custom_call_target="tpu_custom_call" | custom-call | tf_op jit(solution)/shard_map/pallas_call | solution.py:147
  (372 shorter events, 176.7 us)
Async XLA Ops:
  47.6 44.0 %copy-start.10 = (bf16[1152,768]{1,0:T(8,128)(2,1)}, bf16[1152,768]{1,0:T(8,128)(2,1)S(1)}, u32[]{:S(2)}) copy-start(bf16[1152,768]{1,0:T(8,128)(2,1)S(1)} %reshape.283) | copy-start | bytes 5308420
  86.7 285.8 %copy-start.57 = (f32[256]{0:T(256)}, f32[256]{0:T(256)S(1)}, u32[]{:S(2)}) copy-start(f32[256]{0:T(256)S(1)} %mul.563) | copy-start | bytes 3076
  86.9 285.7 %copy-start.59 = (f32[256]{0:T(256)}, f32[256]{0:T(256)S(1)}, u32[]{:S(2)}) copy-start(f32[256]{0:T(256)S(1)} %add_rsqrt_fusion.1) | copy-start | bytes 3076
  91.6 28.5 %copy-start.27 = (f32[1728,36]{0,1:T(8,128)S(1)}, f32[1728,36]{0,1:T(8,128)}, u32[]{:S(2)}) copy-start(f32[1728,36]{0,1:T(8,128)} %param.35) | copy-start | bytes 746500
  92.0 27.1 %copy-start.48 = (f32[2,36,64]{2,0,1:T(2,128)S(1)}, f32[2,36,64]{2,0,1:T(2,128)}, u32[]{:S(2)}) copy-start(f32[2,36,64]{2,0,1:T(2,128)} %param.32) | copy-start | bytes 55300
  119.1 162.3 %copy-start.6 = (bf16[8,64,1152]{2,1,0:T(8,128)(2,1)}, bf16[8,64,1152]{2,1,0:T(8,128)(2,1)S(1)}, u32[]{:S(2)}) copy-start(bf16[8,64,1152]{2,1,0:T(8,128)(2,1)S(1)} %get-tuple-element.39) | copy-start | bytes 3538948
  121.6 8.7 copy-start.29
  123.0 7.6 copy-start.22
  290.7 35.8 %copy-start.25 = (bf16[1152,896]{1,0:T(8,128)(2,1)S(1)}, bf16[1152,896]{1,0:T(8,128)(2,1)}, u32[]{:S(2)}) copy-start(bf16[1152,896]{1,0:T(8,128)(2,1)} %squeeze.32) | copy-start | bytes 6193156
  290.7 35.8 %copy-start.72 = (f32[512,896]{1,0:T(8,128)S(1)}, f32[512,896]{1,0:T(8,128)}, u32[]{:S(2)}) copy-start(f32[512,896]{1,0:T(8,128)} %fusion.94) | copy-start | bytes 5505028
  290.7 35.9 %copy-start.73 = (f32[512,896]{1,0:T(8,128)S(1)}, f32[512,896]{1,0:T(8,128)}, u32[]{:S(2)}) copy-start(f32[512,896]{1,0:T(8,128)} %get-tuple-element.163) | copy-start | bytes 5505028
  332.8 36.5 %copy-start.38 = (bf16[32,8,3,256]{3,1,2,0:T(8,128)(2,1)S(1)}, bf16[32,8,3,256]{3,1,2,0:T(8,128)(2,1)}, u32[]{:S(2)}) copy-start(bf16[32,8,3,256]{3,1,2,0:T(8,128)(2,1)} %copy-done.37) | copy-start | bytes 1179652
  332.8 36.5 %copy-start.66 = (f32[256]{0:T(256)S(1)}, f32[256]{0:T(256)}, u32[]{:S(2)}) copy-start(f32[256]{0:T(256)} %copy-done.65) | copy-start | bytes 3076
  332.8 36.5 %copy-start.68 = (f32[256]{0:T(256)S(1)}, f32[256]{0:T(256)}, u32[]{:S(2)}) copy-start(f32[256]{0:T(256)} %copy-done.67) | copy-start | bytes 3076
  373.7 13.6 %copy-start.62 = (f32[256]{0:T(256)S(1)}, f32[256]{0:T(256)}, u32[]{:S(2)}) copy-start(f32[256]{0:T(256)} %copy-done.61) | copy-start | bytes 3076
  373.7 14.7 %copy-start.64 = (f32[256]{0:T(256)S(1)}, f32[256]{0:T(256)}, u32[]{:S(2)}) copy-start(f32[256]{0:T(256)} %copy-done.63) | copy-start | bytes 3076
  373.7 14.7 %copy-start.58 = (f32[256]{0:T(256)S(1)}, f32[256]{0:T(256)}, u32[]{:S(2)}) copy-start(f32[256]{0:T(256)} %copy-done.57) | copy-start | bytes 3076
  373.7 14.7 %copy-start.60 = (f32[256]{0:T(256)S(1)}, f32[256]{0:T(256)}, u32[]{:S(2)}) copy-start(f32[256]{0:T(256)} %copy-done.59) | copy-start | bytes 3076
  388.6 20.5 %copy-start.36 = (bf16[256,256]{1,0:T(8,128)(2,1)}, bf16[256,256]{1,0:T(8,128)(2,1)S(1)}, u32[]{:S(2)}) copy-start(bf16[256,256]{1,0:T(8,128)(2,1)S(1)} %subtract_convert_fusion.1) | copy-start | bytes 393220
  408.9 26.3 %copy-start.3 = (f32[1,1152]{1,0:T(1,128)S(1)}, f32[1,1152]{1,0:T(1,128)}, u32[]{:S(2)}) copy-start(f32[1,1152]{1,0:T(1,128)} %copy-done.2) | copy-start | bytes 13828
  408.9 26.3 %copy-start.5 = (f32[1,1152]{1,0:T(1,128)S(1)}, f32[1,1152]{1,0:T(1,128)}, u32[]{:S(2)}) copy-start(f32[1,1152]{1,0:T(1,128)} %copy-done.4) | copy-start | bytes 13828
  408.9 94.9 %copy-start.35 = (bf16[256,256]{1,0:T(8,128)(2,1)S(1)}, bf16[256,256]{1,0:T(8,128)(2,1)}, u32[]{:S(2)}) copy-start(bf16[256,256]{1,0:T(8,128)(2,1)} %copy-done.34) | copy-start | bytes 393220
  830.4 7.5 copy-start.20
  914.8 7.3 copy-start.47
  (53 other events, 147.6 us)

commit v2 on v1

--- a/solution.py
+++ b/solution.py
@@ -71,7 +71,7 @@
     return ref.at[rank(target, mode[1])]
 
 
-def exchange_body(axes, modes, *refs):
+def exchange_body(axes, modes, subs, *refs):
     k = len(modes)
     n = count(axes)
     ins, outs = refs[:k], refs[k : 2 * k]
@@ -83,80 +83,471 @@
         pl.semaphore_signal(barrier, inc=1, device_id=device(moved(me, decode(p, axes), -1)), device_id_type=MESH)
         return carry
 
-    def copies(p):
+    def copies(p, arriving, items):
         off = decode(p, axes)
         target = moved(me, off, 1)
+        place_of = moved(me, off, -1) if arriving else me
         return [
             pltpu.make_async_remote_copy(
                 src_ref=slot(ins[i], modes[i], axes, target),
-                dst_ref=outs[i].at[rank(me, axes)],
+                dst_ref=outs[i].at[rank(place_of, subs[i])],
                 send_sem=send_sem.at[i, p],
                 recv_sem=recv_sem.at[i, p],
                 device_id=device(target),
                 device_id_type=MESH,
             )
-            for i in range(k)
+            for i in items
         ]
 
-    def arrivals(p):
-        off = decode(p, axes)
-        target = moved(me, off, 1)
-        source = moved(me, off, -1)
-        return [
-            pltpu.make_async_remote_copy(
-                src_ref=slot(ins[i], modes[i], axes, target),
-                dst_ref=outs[i].at[rank(source, axes)],
-                send_sem=send_sem.at[i, p],
-                recv_sem=recv_sem.at[i, p],
-                device_id=device(target),
-                device_id_type=MESH,
-            )
-            for i in range(k)
-        ]
-
-    def launch(p, carry):
-        for copy in copies(p):
-            copy.start()
-        return carry
-
-    def finish(p, carry):
-        for copy in arrivals(p):
-            copy.wait()
-        return carry
-
     own = [
-        pltpu.make_async_copy(slot(ins[i], modes[i], axes, me), outs[i].at[rank(me, axes)], local_sem.at[i])
+        pltpu.make_async_copy(slot(ins[i], modes[i], axes, me), outs[i].at[rank(me, subs[i])], local_sem.at[i])
         for i in range(k)
     ]
     lax.fori_loop(1, n, greet, 0)
     for copy in own:
         copy.start()
     pl.semaphore_wait(barrier, n - 1)
-    lax.fori_loop(1, n, launch, 0)
+    if all(s == axes for s in subs):
+
+        def launch(p, carry):
+            for copy in copies(p, False, range(k)):
+                copy.start()
+            return carry
+
+        def finish(p, carry):
+            for copy in copies(p, True, range(k)):
+                copy.wait()
+            return carry
+
+        lax.fori_loop(1, n, launch, 0)
+        for copy in own:
+            copy.wait()
+        lax.fori_loop(1, n, finish, 0)
+        return
+    items = []
+    for p in range(1, n):
+        off = decode(p, axes)
+        items.append((p, [i for i in range(k) if all(off[ax] == 0 for ax in axes if ax not in subs[i])]))
+    for p, mine in items:
+        for copy in copies(p, False, mine):
+            copy.start()
     for copy in own:
         copy.wait()
-    lax.fori_loop(1, n, finish, 0)
+    for p, mine in items:
+        for copy in copies(p, True, mine):
+            copy.wait()
 
 
 def exchange(items, axes, cid):
-    arrays = [a for a, _ in items]
-    modes = [m for _, m in items]
-    n = count(axes)
-    shapes = [a.shape if m == "ag" else a.shape[1:] for a, m in items]
-    k = len(items)
-    out = pl.pallas_call(
-        functools.partial(exchange_body, axes, modes),
-        out_shape=[jax.ShapeDtypeStruct((n,) + s, a.dtype) for s, a in zip(shapes, arrays)],
-        in_specs=[pl.BlockSpec(memory_space=pl.ANY)] * k,
-        out_specs=[pl.BlockSpec(memory_space=pl.ANY)] * k,
+    arrays = [i[0] for i in items]
+    modes = [i[1] for i in items]
+    subs = [i[2] if len(i) > 2 else axes for i in items]
+    shapes = [
+        (count(sub),) + (a.shape if m == "ag" else a.shape[1:]) for a, m, sub in zip(arrays, modes, subs)
+    ]
+    k, n = len(items), count(axes)
+    vmem = pl.BlockSpec(memory_space=pltpu.VMEM)
+    return pl.pallas_call(
+        functools.partial(exchange_body, axes, modes, subs),
+        out_shape=[jax.ShapeDtypeStruct(s, a.dtype) for s, a in zip(shapes, arrays)],
+        in_specs=[vmem] * k,
+        out_specs=[vmem] * k,
         scratch_shapes=[
             pltpu.SemaphoreType.DMA((k, n)),
             pltpu.SemaphoreType.DMA((k, n)),
             pltpu.SemaphoreType.DMA((k,)),
         ],
+        compiler_params=pltpu.CompilerParams(
+            collective_id=cid, has_side_effects=True, vmem_limit_bytes=32 * 1024 * 1024
+        ),
+    )(*arrays)
+
+
+def virtual(me, p, q):
+    c = me["c"]
+    first = {"a": jnp.where(c == 0, me[p], me[q]), "b": jnp.where(c == 0, me[q], me[p])}
+
+    def to(av, bv):
+        return {**me, p: jnp.where(c == 0, av, bv), q: jnp.where(c == 0, bv, av)}
+
+    return first["a"], first["b"], to
+
+
+def remote(src, dst, send_sem, recv_sem, at):
+    return pltpu.make_async_remote_copy(
+        src_ref=src, dst_ref=dst, send_sem=send_sem, recv_sem=recv_sem, device_id=device(at), device_id_type=MESH
+    )
+
+
+def greet_all(places):
+    barrier = pltpu.get_barrier_semaphore()
+    for at in places:
+        pl.semaphore_signal(barrier, inc=1, device_id=device(at), device_id_type=MESH)
+    return barrier
+
+
+def gather_body(block, ffn, out, near, send_sem, recv_sem, local_sem):
+    me = place()
+    a, b, to = virtual(me, "z", "x")
+    twin = {**me, "c": 1 - me["c"]}
+    a_next, a_last, a_far = (a + 1) % 4, (a + 3) % 4, (a + 2) % 4
+    b_next, b_last = (b + 1) % 4, (b + 3) % 4
+    barrier = greet_all([to(a_next, b), to(a_last, b), to(a, b_next), to(a, b_last)] + [twin])
+
+    def spot(av, bv):
+        at = to(av, bv)
+        return out.at[me["c"], at["z"], at["x"]]
+
+    here = spot(a, b)
+    mine = near.at[a, pl.ds(me["c"] * 3, 3)]
+    theirs = near.at[a, pl.ds((1 - me["c"]) * 3, 3)]
+    own = pltpu.make_async_copy(block, here, local_sem.at[0])
+    own.start()
+    keep = pltpu.make_async_copy(ffn.at[me["c"]], mine, local_sem.at[1])
+    keep.start()
+    pl.semaphore_wait(barrier, 5)
+
+    def sent(src, dst_here, sem, at):
+        remote(src, src, send_sem.at[sem], recv_sem.at[sem], at).start()
+        return remote(src, dst_here, send_sem.at[sem], recv_sem.at[sem], at)
+
+    own.wait()
+    up, down = to(a_next, b), to(a_last, b)
+    first = [sent(here, spot(a_last, b), 1, up), sent(here, spot(a_next, b), 2, down)]
+    there = near.at[b, pl.ds(me["c"] * 3, 3)]
+    remote(ffn.at[1 - me["c"]], there, send_sem.at[0], recv_sem.at[0], twin).start()
+    keep.wait()
+    remote(ffn.at[1 - me["c"]], theirs, send_sem.at[0], recv_sem.at[0], twin).wait()
+    ffn_first = [sent(near.at[a], near.at[a_last], 17, up), sent(near.at[a], near.at[a_next], 18, down)]
+    for w in first:
+        w.wait()
+    left, right, far = spot(a_last, b), spot(a_next, b), spot(a_far, b)
+    for w in [sent(left.at[0], far.at[0], 3, up), sent(right.at[1], far.at[1], 4, down)]:
+        w.wait()
+    up2, down2 = to(a, b_next), to(a, b_last)
+    waits = [
+        (sent(spot(i, b), spot(i, b_last), 5 + 2 * i, up2), sent(spot(i, b), spot(i, b_next), 6 + 2 * i, down2))
+        for i in range(4)
+    ]
+    for w in ffn_first:
+        w.wait()
+    lo, hi = pl.ds(0, 3), pl.ds(3, 3)
+    late = [
+        sent(near.at[a_last, lo], near.at[a_far, lo], 19, up),
+        sent(near.at[a_next, hi], near.at[a_far, hi], 20, down),
+    ]
+    for i in range(4):
+        w_last, w_next = waits[i]
+        far = spot(i, (b + 2) % 4)
+        if i < 2:
+            w_last.wait()
+            late += [sent(spot(i, b_last), far, 13 + i, up2), w_next]
+        else:
+            w_next.wait()
+            late += [sent(spot(i, b_next), far, 13 + i, down2), w_last]
+    for w in late:
+        w.wait()
+    remote(out.at[me["c"]], out.at[me["c"]], send_sem.at[21], recv_sem.at[21], twin).start()
+    remote(out.at[me["c"]], out.at[1 - me["c"]], send_sem.at[21], recv_sem.at[21], twin).wait()
+
+
+def gather_plane(block, ffn, cid):
+    hbm = pl.BlockSpec(memory_space=pl.ANY)
+    return pl.pallas_call(
+        gather_body,
+        out_shape=[
+            jax.ShapeDtypeStruct((2, 4, 4) + block.shape, block.dtype),
+            jax.ShapeDtypeStruct((4, 6) + ffn.shape[2:], ffn.dtype),
+        ],
+        in_specs=[hbm, hbm],
+        out_specs=[hbm, hbm],
+        scratch_shapes=[
+            pltpu.SemaphoreType.DMA((22,)),
+            pltpu.SemaphoreType.DMA((22,)),
+            pltpu.SemaphoreType.DMA((2,)),
+        ],
         compiler_params=pltpu.CompilerParams(collective_id=cid, has_side_effects=True),
-    )(*arrays)
-    return out
+    )(block, ffn)
+
+
+class SideGather:
+    sems = 16
+
+    def shape(self, near):
+        return jax.ShapeDtypeStruct((4, 4) + near.shape[1:], near.dtype)
+
+    def places(self, me):
+        a, b, to = virtual(me, "z", "x")
+        return [to(a, (b + 1) % 4), to(a, (b + 3) % 4)]
+
+    def start(self, me, near, out, send_sem, recv_sem):
+        a, b, to = virtual(me, "z", "x")
+        b_next, b_last = (b + 1) % 4, (b + 3) % 4
+        up, down = to(a, b_next), to(a, b_last)
+
+        def spot(av, bv):
+            at = to(av, bv)
+            return out.at[at["z"], at["x"]]
+
+        def sent(src, dst, dst_here, sem, at):
+            remote(src, dst, send_sem.at[sem], recv_sem.at[sem], at).start()
+            return remote(src, dst_here, send_sem.at[sem], recv_sem.at[sem], at)
+
+        self.waits = []
+        for i in range(4):
+            self.waits.append(
+                (
+                    sent(near.at[i], spot(i, b), spot(i, b_last), 2 * i, up),
+                    sent(near.at[i], spot(i, b), spot(i, b_next), 2 * i + 1, down),
+                )
+            )
+        self.late = []
+        for i in range(4):
+            copy = pltpu.make_async_copy(near.at[i], spot(i, b), recv_sem.at[12 + i])
+            copy.start()
+            self.late.append(copy)
+
+        def middle():
+            for i in range(4):
+                w_last, w_next = self.waits[i]
+                far = spot(i, (b + 2) % 4)
+                if i < 2:
+                    w_last.wait()
+                    src = spot(i, b_last)
+                    self.late += [sent(src, src, far, 8 + i, up), w_next]
+                else:
+                    w_next.wait()
+                    src = spot(i, b_next)
+                    self.late += [sent(src, src, far, 8 + i, down), w_last]
+
+        self.middle = middle
+
+    def finish(self):
+        for w in self.late:
+            w.wait()
+
+
+class SideSwap:
+    sems = 33
+    axes = ("z", "x", "c")
+
+    def shape(self, parts):
+        return jax.ShapeDtypeStruct(parts.shape, parts.dtype)
+
+    def places(self, me):
+        return [moved(me, decode(p, self.axes), -1) for p in range(1, 32)]
+
+    def start(self, me, parts, out, send_sem, recv_sem):
+        def copies(p, arriving):
+            off = decode(p, self.axes)
+            target = moved(me, off, 1)
+            spot = moved(me, off, -1) if arriving else me
+            return remote(
+                parts.at[rank(target, self.axes)],
+                out.at[rank(spot, self.axes)],
+                send_sem.at[p],
+                recv_sem.at[p],
+                target,
+            )
+
+        def launch(p, carry):
+            copies(p, False).start()
+            return carry
+
+        def finish(p, carry):
+            copies(p, True).wait()
+            return carry
+
+        lax.fori_loop(1, 32, launch, 0)
+        mine = rank(me, self.axes)
+        copy = pltpu.make_async_copy(parts.at[mine], out.at[mine], recv_sem.at[32])
+        copy.start()
+        copy.wait()
+        self.finish = lambda: lax.fori_loop(1, 32, finish, 0)
+        self.middle = lambda: None
+
+
+def reduce_body(parts, total, p, r1, r2, q, r3, r4, send_sem, recv_sem, local_sem):
+    me = place()
+    a, b, to = virtual(me, "z", "x")
+    a_next, a_last, a_far = (a + 1) % 4, (a + 3) % 4, (a + 2) % 4
+    b_next, b_last, b_far = (b + 1) % 4, (b + 3) % 4, (b + 2) % 4
+    up, down = to(a_next, b), to(a_last, b)
+    up2, down2 = to(a, b_next), to(a, b_last)
+    barrier = greet_all([up, down, up2, down2])
+
+    def at(ref, av, bv):
+        w = to(av, bv)
+        return ref.at[w["z"], w["x"]]
+
+    load = pltpu.make_async_copy(parts, p, local_sem.at[0])
+    load.start()
+    pl.semaphore_wait(barrier, 4)
+    first = []
+    for i in range(4):
+        first.append(remote(at(parts, a_far, i), r1.at[i], send_sem.at[i], recv_sem.at[i], up if i < 2 else down))
+        first[-1].start()
+    second = []
+
+    def onward(i, way, src):
+        sem = 4 + 2 * i + way
+        copy = remote(src, r2.at[way, i], send_sem.at[sem], recv_sem.at[sem], down if way else up)
+        copy.start()
+        second.append(copy)
+
+    for i in range(4):
+        onward(i, 1 if i < 2 else 0, at(parts, a_last if i < 2 else a_next, i))
+    load.wait()
+    for i in range(4):
+        first[i].wait()
+        dest = at(p, a_next if i < 2 else a_last, i)
+        dest[...] = (dest[...].astype(F32) + r1[i].astype(F32)).astype(BF)
+        onward(i, 0 if i < 2 else 1, dest)
+    for copy in second:
+        copy.wait()
+    for i in range(4):
+        q[i] = (at(p, a, i)[...].astype(F32) + r2[0, i].astype(F32) + r2[1, i].astype(F32)).astype(BF)
+    lo, hi = pl.ds(0, BLK // 2), pl.ds(BLK // 2, BLK // 2)
+    one = remote(q.at[b_far, lo], r3.at[0], send_sem.at[12], recv_sem.at[12], up2)
+    two = remote(q.at[b_far, hi], r3.at[1], send_sem.at[13], recv_sem.at[13], down2)
+    one.start()
+    two.start()
+    three = remote(q.at[b_next, hi], r4.at[0, hi], send_sem.at[14], recv_sem.at[14], up2)
+    four = remote(q.at[b_last, lo], r4.at[1, lo], send_sem.at[15], recv_sem.at[15], down2)
+    three.start()
+    four.start()
+    one.wait()
+    dest = q.at[b_next, lo]
+    dest[...] = (dest[...].astype(F32) + r3[0].astype(F32)).astype(BF)
+    five = remote(q.at[b_next, lo], r4.at[0, lo], send_sem.at[16], recv_sem.at[16], up2)
+    five.start()
+    two.wait()
+    dest = q.at[b_last, hi]
+    dest[...] = (dest[...].astype(F32) + r3[1].astype(F32)).astype(BF)
+    six = remote(q.at[b_last, hi], r4.at[1, hi], send_sem.at[17], recv_sem.at[17], down2)
+    six.start()
+    for copy in (three, four, five, six):
+        copy.wait()
+    total[...] = q[b].astype(F32) + r4[0].astype(F32) + r4[1].astype(F32)
+
+
+def reduce_plane(parts, cid):
+    block = parts.shape[2:]
+    return pl.pallas_call(
+        reduce_body,
+        out_shape=jax.ShapeDtypeStruct(block, F32),
+        in_specs=[pl.BlockSpec(memory_space=pl.ANY)],
+        out_specs=pl.BlockSpec(memory_space=pltpu.VMEM),
+        scratch_shapes=[
+            pltpu.VMEM((4, 4) + block, BF),
+            pltpu.VMEM((4,) + block, BF),
+            pltpu.VMEM((2, 4) + block, BF),
+            pltpu.VMEM((4,) + block, BF),
+            pltpu.VMEM((2, BLK // 2, D), BF),
+            pltpu.VMEM((2,) + block, BF),
+            pltpu.SemaphoreType.DMA((18,)),
+            pltpu.SemaphoreType.DMA((18,)),
+            pltpu.SemaphoreType.DMA((1,)),
+        ],
+        compiler_params=pltpu.CompilerParams(
+            collective_id=cid, has_side_effects=True, vmem_limit_bytes=48 * 1024 * 1024
+        ),
+    )(parts)
+
+
+def gram_body(parts, extra, gram, extras, p, got, mine, bx, send_sem, recv_sem, local_sem):
+    me = place()
+    c, z = me["c"], me["z"]
+    axes = ("x", "y")
+    twin = {**me, "c": 1 - c}
+    barrier = pltpu.get_barrier_semaphore()
+    for i in range(1, 16):
+        pl.semaphore_signal(barrier, inc=1, device_id=device(moved(me, decode(i, axes), -1)), device_id_type=MESH)
+    for i in range(4):
+        pl.semaphore_signal(barrier, inc=1, device_id=device({**twin, "y": (me["y"] + i) % 4}), device_id_type=MESH)
+    load = pltpu.make_async_copy(parts.at[c], p, local_sem.at[0])
+    load.start()
+    keep = pltpu.make_async_copy(extra, extras.at[rank(me, ("c", "y"))], local_sem.at[1])
+    keep.start()
+    pl.semaphore_wait(barrier, 19)
+    swap = remote(parts.at[1 - c], got, send_sem.at[0, 0], recv_sem.at[0, 0], twin)
+    swap.start()
+    extra_waits = []
+    for i in range(1, 8):
+        off = decode(i, ("c", "y"))
+        target, source = moved(me, off, 1), moved(me, off, -1)
+        sems = (send_sem.at[3, i], recv_sem.at[3, i])
+        remote(extra, extras.at[rank(me, ("c", "y"))], *sems, target).start()
+        extra_waits.append(remote(extra, extras.at[rank(source, ("c", "y"))], *sems, target))
+    load.wait()
+    swap.wait()
+    for i in range(16):
+        p[i] = (p[i].astype(F32) + got[i].astype(F32)).astype(BF)
+    waits = []
+    for i in range(1, 16):
+        off = decode(i, axes)
+        target, source = moved(me, off, 1), moved(me, off, -1)
+        sems = (send_sem.at[1, i], recv_sem.at[1, i])
+        remote(p.at[rank(target, axes)], mine.at[rank(me, axes)], *sems, target).start()
+        waits.append(remote(p.at[rank(target, axes)], mine.at[rank(source, axes)], *sems, target))
+    own = pltpu.make_async_copy(p.at[rank(me, axes)], mine.at[rank(me, axes)], local_sem.at[0])
+    own.start()
+    own.wait()
+    for w in waits:
+        w.wait()
+    sums = []
+    for i in range(4):
+        part = mine[4 * i].astype(F32)
+        for j in range(1, 4):
+            part = part + mine[4 * i + j].astype(F32)
+        sums.append(part)
+    whole = sums[0] + sums[1] + sums[2] + sums[3]
+    for i in range(4):
+        bx[i] = jnp.where(z < 3, whole, sums[i]).astype(BF)
+    waits = []
+    spot = gram.at[c]
+    for i in range(1, 16):
+        off = decode(i, axes)
+        target, source = moved(me, off, 1), moved(me, off, -1)
+        sems = (send_sem.at[2, i], recv_sem.at[2, i])
+        remote(bx.at[target["x"]], spot.at[rank(me, axes)], *sems, target).start()
+        waits.append(remote(bx.at[target["x"]], spot.at[rank(source, axes)], *sems, target))
+    own = pltpu.make_async_copy(bx.at[me["x"]], spot.at[rank(me, axes)], local_sem.at[0])
+    own.start()
+    own.wait()
+    for w in waits:
+        w.wait()
+    remote(gram.at[c], gram.at[c], send_sem.at[2, 0], recv_sem.at[2, 0], twin).start()
+    remote(gram.at[c], gram.at[1 - c], send_sem.at[2, 0], recv_sem.at[2, 0], twin).wait()
+    keep.wait()
+    for w in extra_waits:
+        w.wait()
+
+
+def gram_sum(parts, extra, cid):
+    vmem = pl.BlockSpec(memory_space=pltpu.VMEM)
+    half = parts.shape[1:]
+    return pl.pallas_call(
+        gram_body,
+        out_shape=[
+            jax.ShapeDtypeStruct(parts.shape, BF),
+            jax.ShapeDtypeStruct((8,) + extra.shape, extra.dtype),
+        ],
+        in_specs=[vmem, vmem],
+        out_specs=[vmem, vmem],
+        scratch_shapes=[
+            pltpu.VMEM(half, BF),
+            pltpu.VMEM(half, BF),
+            pltpu.VMEM(half, BF),
+            pltpu.VMEM((4,) + half[1:], BF),
+            pltpu.SemaphoreType.DMA((4, 16)),
+            pltpu.SemaphoreType.DMA((4, 16)),
+            pltpu.SemaphoreType.DMA((2,)),
+        ],
+        compiler_params=pltpu.CompilerParams(
+            collective_id=cid, has_side_effects=True, vmem_limit_bytes=48 * 1024 * 1024
+        ),
+    )(parts, extra)
 
 
 def halo_body(sign, kinds, *refs):
@@ -231,87 +622,103 @@
     )(*arrays)
 
 
-def sum_body(fn, rs_axes, ag_axes, n_extra, n_local, n_ag, *refs):
+def sum_body(fn, both, spread, side, n_extra, n_local, n_ag, *refs):
+    if side is not None:
+        side_in, side_out, side_send, side_recv = refs[0], refs[1 + 1 + n_extra + n_local + n_ag], refs[-2], refs[-1]
+        refs = refs[1 : 2 + n_extra + n_local + n_ag] + refs[3 + n_extra + n_local + n_ag : -2]
     parts = refs[0]
     extras = refs[1 : 1 + n_extra]
     locals_ = refs[1 + n_extra : 1 + n_extra + n_local]
     gathers = refs[1 + n_extra + n_local : 1 + n_extra + n_local + n_ag]
-    recv, agbuf, rs_send, rs_recv, ag_send, ag_recv, local_sem = refs[1 + n_extra + n_local + n_ag :]
+    pre, recv, agbuf, send_sem, recv_sem, local_sem = refs[1 + n_extra + n_local + n_ag :]
     me = place()
-    union = rs_axes if len(rs_axes) >= len(ag_axes) else ag_axes
-    barrier = pltpu.get_barrier_semaphore()
-    for p in range(1, count(union)):
-        pl.semaphore_signal(barrier, inc=1, device_id=device(moved(me, decode(p, union), -1)), device_id_type=MESH)
-    own = pltpu.make_async_copy(parts.at[rank(me, rs_axes)], recv.at[rank(me, rs_axes)], local_sem.at[0])
-    own.start()
-    pl.semaphore_wait(barrier, count(union) - 1)
-
-    def send(p, axes, src, dst, send_sem, recv_sem):
-        off = decode(p, axes)
-        target, source = moved(me, off, 1), moved(me, off, -1)
-        source_ref = src(target)
-        args = dict(send_sem=send_sem, recv_sem=recv_sem, device_id=device(target), device_id_type=MESH)
-        out_copy = pltpu.make_async_remote_copy(src_ref=source_ref, dst_ref=dst.at[rank(me, axes)], **args)
-        in_copy = pltpu.make_async_remote_copy(src_ref=source_ref, dst_ref=dst.at[rank(source, axes)], **args)
-        return out_copy, in_copy
-
-    moves = [
-        send(p, rs_axes, lambda t: parts.at[rank(t, rs_axes)], recv, rs_send.at[p], rs_recv.at[p])
-        for p in range(1, count(rs_axes))
-    ]
-    for out_copy, _ in moves:
-        out_copy.start()
-    own.wait()
-    for _, in_copy in moves:
-        in_copy.wait()
-    total = recv[0].astype(F32)
-    for i in range(1, count(rs_axes)):
+    c, y = me["c"], me["y"]
+    twin = {**me, "c": 1 - c}
+    near = [(moved(me, {"y": i}, 1), moved(me, {"y": i}, -1)) for i in range(1, 4)]
+    use_twin = both or spread
+    places = [source for _, source in near] + ([twin] if use_twin else [])
+    if side is not None:
+        places += side.places(me)
+    barrier = greet_all(places)
+    pl.semaphore_wait(barrier, len(places))
+    if both:
+        swap = remote(parts.at[1 - c], pre, send_sem.at[0], recv_sem.at[0], twin)
+        swap.start()
+        if side is not None:
+            side.start(me, side_in, side_out, side_send, side_recv)
+        swap.wait()
+        for i in range(4):
+            pre[i] = (pre[i].astype(F32) + parts[c, i].astype(F32)).astype(BF)
+        mine = pre
+    else:
+        mine = parts
+    waits = []
+    for i, (target, source) in enumerate(near):
+        sems = (send_sem.at[1 + i], recv_sem.at[1 + i])
+        remote(mine.at[target["y"]], recv.at[i], *sems, target).start()
+        waits.append(remote(mine.at[target["y"]], recv.at[i], *sems, target))
+    if side is not None and not both:
+        side.start(me, side_in, side_out, side_send, side_recv)
+    total = mine[y].astype(F32)
+    for i in range(3):
+        waits[i].wait()
         total = total + recv[i].astype(F32)
     local_vals, ag_vals = fn(total, *[e[...] for e in extras])
     for i, value in enumerate(ag_vals):
         agbuf[i] = value.astype(BF)
-    moves = []
-    own = []
-    for i in range(n_ag):
-        own.append(pltpu.make_async_copy(agbuf.at[i], gathers[i].at[rank(me, ag_axes)], local_sem.at[1 + i]))
-        for p in range(1, count(ag_axes)):
-            moves.append(send(p, ag_axes, lambda t, i=i: agbuf.at[i], gathers[i], ag_send.at[i, p], ag_recv.at[i, p]))
-    for out_copy, _ in moves:
-        out_copy.start()
-    for copy in own:
-        copy.start()
+    waits, own = [], []
+    for j in range(n_ag):
+        out = gathers[j].at[c] if spread else gathers[j]
+        for i, (target, source) in enumerate(near):
+            sems = (send_sem.at[4 + 3 * j + i], recv_sem.at[4 + 3 * j + i])
+            remote(agbuf.at[j], out.at[y], *sems, target).start()
+            waits.append(remote(agbuf.at[j], out.at[source["y"]], *sems, target))
+        own.append(pltpu.make_async_copy(agbuf.at[j], out.at[y], local_sem.at[j]))
+        own[-1].start()
     for ref, value in zip(locals_, local_vals):
         ref[...] = value
-    for copy in own:
+    if side is not None:
+        side.middle()
+    for copy in own + waits:
         copy.wait()
-    for _, in_copy in moves:
-        in_copy.wait()
-
-
-def sum_then_gather(fn, parts, extras, local_shapes, n_ag, rs_axes, ag_axes, cid):
-    n_rs, n_g = count(rs_axes), count(ag_axes)
-    rows = parts.shape[1:]
+    if spread:
+        for j in range(n_ag):
+            g = gathers[j]
+            sems = (send_sem.at[4 + 3 * n_ag + j], recv_sem.at[4 + 3 * n_ag + j])
+            remote(g.at[c], g.at[c], *sems, twin).start()
+            remote(g.at[c], g.at[1 - c], *sems, twin).wait()
+    if side is not None:
+        side.finish()
+
+
+def sum_then_gather(fn, parts, extras, local_shapes, n_ag, spread, cid, side=None, side_in=None):
+    both = parts.ndim == 4
+    rows = parts.shape[-2:]
     vmem = pl.BlockSpec(memory_space=pltpu.VMEM)
+    gathered = ((2, 4) if spread else (4,)) + rows
+    n_sem = 4 + 4 * n_ag
     hbm = pl.BlockSpec(memory_space=pl.ANY)
+    more = side is not None
     return pl.pallas_call(
-        functools.partial(sum_body, fn, rs_axes, ag_axes, len(extras), len(local_shapes), n_ag),
+        functools.partial(sum_body, fn, both, spread, side, len(extras), len(local_shapes), n_ag),
         out_shape=[jax.ShapeDtypeStruct(s, F32) for s in local_shapes]
-        + [jax.ShapeDtypeStruct((n_g,) + rows, BF)] * n_ag,
-        in_specs=[hbm] + [vmem] * len(extras),
-        out_specs=[vmem] * len(local_shapes) + [hbm] * n_ag,
+        + [jax.ShapeDtypeStruct(gathered, BF)] * n_ag
+        + ([side.shape(side_in)] if more else []),
+        in_specs=[hbm] * more + [vmem] * (1 + len(extras)),
+        out_specs=[vmem] * (len(local_shapes) + n_ag) + [hbm] * more,
         scratch_shapes=[
-            pltpu.VMEM((n_rs,) + rows, BF),
+            pltpu.VMEM((4,) + rows, BF),
+            pltpu.VMEM((3,) + rows, BF),
             pltpu.VMEM((n_ag,) + rows, BF),
-            pltpu.SemaphoreType.DMA((n_rs,)),
-            pltpu.SemaphoreType.DMA((n_rs,)),
-            pltpu.SemaphoreType.DMA((n_ag, n_g)),
-            pltpu.SemaphoreType.DMA((n_ag, n_g)),
-            pltpu.SemaphoreType.DMA((1 + n_ag,)),
-        ],
+            pltpu.SemaphoreType.DMA((n_sem,)),
+            pltpu.SemaphoreType.DMA((n_sem,)),
+            pltpu.SemaphoreType.DMA((n_ag,)),
+        ]
+        + ([pltpu.SemaphoreType.DMA((side.sems,))] * 2 if more else []),
         compiler_params=pltpu.CompilerParams(
             collective_id=cid, has_side_effects=True, vmem_limit_bytes=32 * 1024 * 1024
         ),
-    )(parts, *extras)
+    )(*([side_in] if more else []), parts, *extras)
 
 
 def inv_rms(values):
@@ -430,26 +837,6 @@
     y = lax.axis_index("tensor")
     z, x, c = dp // 8, (dp // 2) % 4, dp % 2
 
-    attn_w = jnp.concatenate(
-        [
-            w_query,
-            w_output.T,
-            w_keyval[0],
-            w_keyval[1],
-            norm_gains.T,
-            jnp.broadcast_to(qk_gains.reshape(1, 4), (ROWS, 4)),
-            jnp.zeros((ROWS, 120), F32),
-        ],
-        axis=1,
-    ).astype(BF)
-    segs = segment_ids.reshape(2, 128)
-    attn_all, segs_all = exchange([(attn_w, "ag"), (segs, "ag")], ("z", "x", "c"), 1)
-    weights = attn_all.reshape(D, 768)
-    wq, woT, wkv = weights[:, :256], weights[:, 256:512], weights[:, 512:640]
-    gains = weights[:, 640:644].T.astype(F32)
-    g0, g1, g2, g3 = (gains[i : i + 1] for i in range(4))
-    qk_mine = jnp.pad(attn_all[:, 0, 644:648].reshape(32, 2, 2).transpose(1, 0, 2).reshape(2, 64), ((0, 14), (0, 64)))
-
     ffn_w = jnp.concatenate([w_gateup, w_down.T[None]], axis=0).astype(BF)
     ffn_w = jnp.pad(ffn_w, ((0, 0), (0, 0), (0, FFP - FFT))).reshape(3, ROWS, 2, HALF).transpose(2, 0, 1, 3)
     moms = to_columns(
@@ -457,6 +844,33 @@
         [m.astype(BF) for m in (mom_query, mom_output.T, mom_keyval[0], mom_keyval[1])],
     )
 
+    segs = jnp.pad(segment_ids.astype(F32).reshape(4, 64), ((0, ROWS - 4), (0, 0)))
+    attn_w = jnp.stack(
+        [
+            jnp.concatenate([w_query, w_keyval[0], w_keyval[1]], axis=1),
+            jnp.concatenate(
+                [
+                    w_output.T,
+                    norm_gains.T,
+                    jnp.broadcast_to(qk_gains.reshape(1, 4), (ROWS, 4)),
+                    segs,
+                    jnp.zeros((ROWS, 56), F32),
+                ],
+                axis=1,
+            ),
+        ]
+    ).astype(BF)
+    attn_got, ffn_near = gather_plane(attn_w, ffn_w, 1)
+    attn_all = attn_got.transpose(3, 1, 2, 0, 4, 5).reshape(2, 32, ROWS, 384)
+    w_qkv = attn_all[0].reshape(D, 384)
+    wq, wkv = w_qkv[:, :256], w_qkv[:, 256:]
+    woT = attn_all[1, :, :, :256].reshape(D, 256)
+    gains = attn_all[1, :, :, 256:260].reshape(D, 4).T.astype(F32)
+    g0, g1, g2, g3 = (gains[i : i + 1] for i in range(4))
+    qk_mine = attn_all[1, :, 0, 260:264].reshape(32, 2, 2).transpose(1, 0, 2).reshape(2, 64)
+    qk_mine = jnp.pad(qk_mine, ((0, 14), (0, 64)))
+    segs_all = attn_all[1, :, :4, 264:328].reshape(32, TOK).astype(jnp.int32)
+
     cos_b, sin_b, cos_s, sin_s = (jnp.asarray(t) for t in rope_tables())
     cb = lax.dynamic_slice_in_dim(cos_b, dp, 1, 0)
     sb = lax.dynamic_slice_in_dim(sin_b, dp, 1, 0)
@@ -465,7 +879,7 @@
     cos_q, sin_q = cosine[512:], sine[512:]
 
     normed = (hidden_in * inv_rms(hidden_in) * g0).astype(BF)
-    proj = dot(normed, jnp.concatenate([wq, wkv], axis=1), NN)
+    proj = dot(normed, w_qkv, NN)
     q_raw = proj[:, :256]
     kv_all, qk_all = halo([(proj[:, 256:].astype(BF), "all"), (qk_mine, "near")], 1, 2)
     qk_full = qk_all[:, :2, :64].reshape(4, 2, 32, 2).transpose(1, 2, 0, 3).reshape(2, HD).astype(F32)
@@ -477,7 +891,7 @@
     qr = rot(q_raw * q_s * gq, cos_q, sin_q).astype(BF)
     kr = rot(k_raw * inv_rms(k_raw) * gk, cosine, sine).astype(BF)
     first = jnp.maximum(dp - 2, 0)
-    seg_rows = lax.dynamic_slice_in_dim(segs_all.reshape(32, TOK), first, 3, 0)
+    seg_rows = lax.dynamic_slice_in_dim(segs_all, first, 3, 0)
     seg_keys = jnp.where(
         dp >= 2, seg_rows, jnp.where(dp == 1, jnp.roll(seg_rows, 1, axis=0), jnp.roll(seg_rows, 2, axis=0))
     ).reshape(3 * TOK)
@@ -499,12 +913,11 @@
     u_part = dot(ob, woT, NT).astype(BF).reshape(4, QTOK, D)
     hidden_q = lax.dynamic_slice_in_dim(hidden_in, y * QTOK, QTOK, 0)
     grad_q = lax.dynamic_slice_in_dim(out_grad, y * QTOK, QTOK, 0)
-    u, hmid, bin_all = sum_then_gather(
-        mid_fn, u_part, [hidden_q, g1, g2], [(QTOK, D)] * 2, 1, ("y",), ("c", "y"), 3
+    u, hmid, bin_all, ffn_all = sum_then_gather(
+        mid_fn, u_part, [hidden_q, g1, g2], [(QTOK, D)] * 2, 1, True, 3, SideGather(), ffn_near
     )
 
-    ffn_all, moms_all = exchange([(ffn_w, ("by", ("c",))), (moms, "a2a")], ("z", "x", "c"), 4)
-    ffn_full = ffn_all.transpose(1, 0, 2, 3).reshape(3, D, HALF)
+    ffn_full = ffn_all.reshape(32, 3, ROWS, HALF).transpose(1, 0, 2, 3).reshape(3, D, HALF)
     wg, wu, wdT = ffn_full[0], ffn_full[1], ffn_full[2]
     bin_low = bin_all.reshape(512, D)
     gate = dot(bin_low, wg, NN)
@@ -514,23 +927,22 @@
     gelu = 0.5 * gate * (1.0 + th)
     gelu_d = 0.5 * (1.0 + th) + 0.5 * gate * (1.0 - th * th) * inner * (1.0 + 3 * 0.044715 * gate * gate)
     mixed = (gelu * up).astype(BF)
-    f_part = dot(mixed, wdT, NT).astype(BF).reshape(8, QTOK, D)
-    block, dg3, df_all = sum_then_gather(
-        ffn_out_fn, f_part, [hmid, grad_q, g3], [(QTOK, D), (1, D)], 1, ("c", "y"), ("c", "y"), 5
+    f_part = dot(mixed, wdT, NT).astype(BF).reshape(2, 4, QTOK, D)
+    block, dg3, df_all, moms_all = sum_then_gather(
+        ffn_out_fn, f_part, [hmid, grad_q, g3], [(QTOK, D), (1, D)], 1, True, 5, SideSwap(), moms
     )
     dfb = df_all.reshape(512, D)
     dz = dot(dfb, wdT, NN)
     dgate = (dz * up * gelu_d).astype(BF)
     dup = (dz * gelu).astype(BF)
-    dbin_part = (dot(dgate, wg, NT) + dot(dup, wu, NT)).astype(BF).reshape(8, QTOK, D)
+    dbin_part = (dot(dgate, wg, NT) + dot(dup, wu, NT)).astype(BF).reshape(2, 4, QTOK, D)
     dhmid, dg1, dg2, du_all = sum_then_gather(
         ffn_in_fn,
         dbin_part,
         [hmid, u, grad_q, g1, g2],
         [(QTOK, D), (1, D), (1, D)],
         1,
-        ("c", "y"),
-        ("c", "y"),
+        True,
         6,
     )
 
@@ -552,35 +964,29 @@
     dq, dgq = rms_back(q_raw, gq, q_s, unrot(dqr, cos_q, sin_q))
     dkvb = jnp.concatenate([dk, dkv_sum[:, 256:]], axis=1).astype(BF)
     dqb = dq.astype(BF)
-    (dkv_all,) = exchange([(dkvb, "ag")], ("c", "y"), 8)
-    pair, = exchange([(jnp.concatenate([normed, ob, dqb], axis=1), "ag")], ("c",), 9)
+    pair = jnp.concatenate([normed, ob, dqb], axis=1)
+    dkv_all, pair = exchange([(dkvb, "ag"), (pair, "ag", ("c",))], ("c", "y"), 8)
     pair = pair.reshape(512, D + 512)
     dkv_all = dkv_all.reshape(512, 2, 4, 64)
     dkv_cols = lax.dynamic_slice_in_dim(dkv_all, y, 1, 2).reshape(512, 128)
     da_part = (
         dot(
             jnp.concatenate([dqb, lax.dynamic_slice_in_dim(dkv_cols, c * TOK, TOK, 0)], axis=1),
-            jnp.concatenate([wq, wkv], axis=1),
+            w_qkv,
             NT,
         )
         .astype(BF)
         .reshape(4, QTOK, D)
     )
     dg0, last_in, last_out = sum_then_gather(
-        last_fn, da_part, [hidden_q, dhmid, block, g0], [(1, D)], 2, ("y",), ("y",), 10
+        last_fn, da_part, [hidden_q, dhmid, block, g0], [(1, D)], 2, False, 10
     )
     input_grad = last_in.reshape(TOK, D).astype(F32)
     block_out = last_out.reshape(TOK, D).astype(F32)
 
-    qk_row = jnp.concatenate([dgq, dgk, jnp.zeros((1, D - 2 * HD), F32)], axis=1)
-    gain_sum = lax.psum(jnp.concatenate([dg0, dg1, dg2, dg3, qk_row], axis=0), ("dp", "tensor"))
-    gains_red = lax.dynamic_slice(gain_sum, (0, dp * ROWS), (4, ROWS))
-    qk_red = lax.dynamic_slice_in_dim(gain_sum[4, : 2 * HD].reshape(2, HD), (dp * 4 + y) * 2, 2, 1)
-    gain_rate = 2.0 / math.sqrt(8192)
-    next_gain_moms = 0.9 * gain_moms + 0.1 * gains_red
-    new_norm_gains = norm_gains - gain_rate * next_gain_moms
-    next_qk_moms = 0.9 * qk_moms + 0.1 * qk_red
-    new_qk_gains = qk_gains - gain_rate * next_qk_moms
+    gain_rows = jnp.concatenate(
+        [dg0, dg1, dg2, dg3, jnp.concatenate([dgq, dgk, jnp.zeros((1, D - 2 * HD), F32)], axis=1)], axis=0
+    ).astype(BF)
 
     a_all, ob_all, dq_all = pair[:, :D], pair[:, D : D + 256], pair[:, D + 256 :]
     ob_cols = lax.dynamic_slice_in_dim(ob_all, c * 128, 128, 1)
@@ -601,25 +1007,42 @@
             jnp.pad(d_q, ((0, BLK - 128), (0, 0)))[None],
             jnp.pad(d_o, ((0, BLK - 128), (0, 0)))[None],
             jnp.pad(d_kv[:32], ((0, BLK - 32), (0, 0)))[None],
-            jnp.pad(d_kv[32:], ((0, BLK - 32), (0, 0)))[None],
+            jnp.concatenate([d_kv[32:], gain_rows, jnp.zeros((BLK - 37, D), BF)], axis=0)[None],
         ],
         axis=0,
     )
-    (wgrads_got,) = exchange([(wgrads, "a2a")], ("z", "x"), 11)
-    wgrad = jnp.sum(wgrads_got.astype(F32), axis=0)
+    wgrad = reduce_plane(wgrads.reshape(4, 4, BLK, D), 11)
 
     mom = 0.95 * moms_all.reshape(D, BLK).T.astype(F32) + wgrad
+    kept = jnp.where((z == 3) & (x == 3), 32, BLK)
+    mom = jnp.where(jnp.arange(BLK)[:, None] < kept, mom, 0.0)
     mom_low = mom.astype(BF)
-    gram_part = dot(mom_low, mom_low, TN).astype(BF).reshape(32, ROWS, D)
-    (gram_got,) = exchange([(gram_part, "a2a")], ("x", "y", "c"), 12)
-    by_x = jnp.sum(gram_got.reshape(4, 8, ROWS, D).astype(F32), axis=1)
-    by_x = jnp.where(z < 3, jnp.sum(by_x, axis=0, keepdims=True), by_x).astype(BF)
-    (gram,) = exchange([(by_x, ("by", ("x",)))], ("x", "y", "c"), 13)
+    gram_part = dot(mom_low, mom_low, TN).astype(BF).reshape(2, 16, ROWS, D)
+    gram, gains_got = gram_sum(gram_part, wgrad[32:48].astype(BF), 13)
     ortho = orthogonal(gram.reshape(D, D), mom)
+    gain_sum = jnp.sum(gains_got[:, :5].astype(F32), axis=0)
+    gain_cols = jnp.concatenate(
+        [
+            gain_sum[:4].T.reshape(32, ROWS, 4),
+            jnp.pad(
+                gain_sum[4, : 2 * HD].reshape(2, 32, 4, 2)[:, :, y].transpose(1, 0, 2).reshape(32, 1, 4),
+                ((0, 0), (0, ROWS - 1), (0, 0)),
+            ),
+        ],
+        axis=2,
+    )
     back = jnp.concatenate([ortho.astype(BF), wgrad.astype(BF)], axis=0).T.reshape(32, ROWS, 2 * BLK)
+    back = jnp.concatenate([back, gain_cols.astype(BF), jnp.zeros((32, ROWS, 56), BF)], axis=2)
     (back_got,) = exchange([(back, "a2a")], ("z", "x", "c"), 14)
     o_big, o_small = from_columns(back_got[:, :, :BLK].astype(F32))
-    w_big, w_small = from_columns(back_got[:, :, BLK:].astype(F32))
+    w_big, w_small = from_columns(back_got[:, :, BLK : 2 * BLK].astype(F32))
+    gains_red = back_got[30, :, 448:452].T.astype(F32)
+    qk_red = back_got[30, 0, 452:456].reshape(2, 2).astype(F32)
+    gain_rate = 2.0 / math.sqrt(8192)
+    next_gain_moms = 0.9 * gain_moms + 0.1 * gains_red
+    new_norm_gains = norm_gains - gain_rate * next_gain_moms
+    next_qk_moms = 0.9 * qk_moms + 0.1 * qk_red
+    new_qk_gains = qk_gains - gain_rate * next_qk_moms
 
     def step(columns):
         return 0.15 * 0.2 * math.sqrt(max(D, columns))

time: 936 us -> 561 us (0.60)
  Pallas kernels: 627 us -> 320 us
  blocking collectives: 65.8 us -> 0 us
  local copies, waits for them, and re-layouts: 91.2 us -> 106 us
  other arithmetic: 58.8 us -> 47.1 us
    pallas_call x12 -> x9, Pallas kernels: 597 us -> 289 us  [the longest x4 107 us: sum_then_gather(): pl.pallas_call(functools.partial(sum_body, fn, both, spread, side, len(ex...]
    psum x1 -> x0, blocking collectives: 65.8 us -> none  [local(): lax.psum(jnp.concatenate([dg0, dg1, dg2, dg3, qk_row], axis=0), ('dp', 't...]
    unnamed x182 -> x193, local copies, waits for them, and re-layouts: 22.4 us -> 21.9 us
where the time goes in v2:
time: 561 us; the launch traced here: 555 us
  Pallas kernels  320 us (57%)
  local copies, waits for them, and re-layouts  106 us (19%)
  matrix products  78.1 us (14%)
  other arithmetic  47.1 us (8%)
    pallas_call x4, Pallas kernels, sum_then_gather(): pl.pallas_call(functools.partial(sum_body, fn, both, spread, side, len(ex...  107 us
    dot_general x32, matrix products, dot(): return lax.dot_general(a, b, (dims, ((), ())), preferred_element_type=F32)  78.1 us
    pallas_call x1, Pallas kernels, gram_sum(): pl.pallas_call(gram_body, out_shape=[jax.ShapeDtypeStruct(parts.shape, BF...  60.3 us
    pallas_call x1, Pallas kernels, reduce_plane(): pl.pallas_call(reduce_body, out_shape=jax.ShapeDtypeStruct(block, F32), i...  50.7 us
    pallas_call x2, Pallas kernels, exchange(): pl.pallas_call(functools.partial(exchange_body, axes, modes, subs), out_s...  36.6 us
    pallas_call x1, Pallas kernels, gather_plane(): pl.pallas_call(gather_body, out_shape=[jax.ShapeDtypeStruct((2, 4, 4) + b...  34.6 us
    pallas_call x2, Pallas kernels, halo(): pl.pallas_call(functools.partial(halo_body, sign, kinds), out_shape=[jax....  31.3 us
    unnamed x193, local copies, waits for them, and re-layouts  21.9 us

profile of v2, /device:TPU:1, one launch (start us, length us, event | category | flops | bytes accessed | tf_op | source)
XLA Modules:
  0.0 554.9 jit_solution(13204668091706509777)
XLA Ops:
  10.3 34.6 %shard_map.324 = (bf16[2,4,4,2,36,384]{5,4,3,2,1,0:T(8,128)(2,1)}, bf16[4,6,36,896]{3,2,1,0:T(8,128)(2,1)}) custom-call(bf16[2,36,384]{2,1,0:T(8,128)(2,1)} %pad_maximum_fusion.11.block, bf16[2,3,36,896]{3,2,1,0:T(8,128)(2,1)} %bitcast.260), custom_call_target="tpu_custom_call" | custom-call | tf_op jit(solution)/shard_map/pallas_call | solution.py:256
  59.3 18.4 %shard_map.325 = (bf16[3,4,256,128]{3,2,1,0:T(8,128)(2,1)}, bf16[4,16,128]{2,1,0:T(8,128)(2,1)}) custom-call(bf16[256,128]{1,0:T(8,128)(2,1)} %slice.425.refs_0_, bf16[16,128]{1,0:T(8,128)(2,1)} %pad.48.refs_1_), custom_call_target="tpu_custom_call" | custom-call | tf_op jit(solution)/shard_map/pallas_call | solution.py:611
  101.8 4.4 slice_reduce_fusion
  110.0 31.9 %shard_map.326 = (f32[64,1152]{1,0:T(8,128)S(1)}, f32[64,1152]{1,0:T(8,128)S(1)}, bf16[2,4,64,1152]{3,2,1,0:T(8,128)(2,1)S(1)}, bf16[4,4,6,36,896]{4,3,2,1,0:T(8,128)(2,1)S(1)}) custom-call(bf16[4,6,36,896]{3,2,1,0:T(8,128)(2,1)S(1)} %copy-done.2, bf16[4,64,1152]{2,1,0:T(8,128)(2,1)S(1)} %bitcast.230, f32[64,1152]{1,0:T(8,128)S(1)} %get-tuple-element.177.refs_2_.refs_1_, ...), custom_call_target="tpu_custom_call" | custom-call | tf_op jit(solution)/shard_map/pallas_call | solution.py:702
  145.3 6.1 %fusion.89 = (bf16[1,32,36,896]{3,2,1,0:T(8,128)(2,1)}, bf16[1,32,36,896]{3,2,1,0:T(8,128)(2,1)}, bf16[1,32,36,896]{3,2,1,0:T(8,128)(2,1)}) fusion(bf16[3,32,36,896]{3,2,1,0:T(8,128)(2,1)} %bitcast.242), kind=kLoop, calls=%fused_computation.262 | loop fusion | bytes 12386304 | tf_op jit(solution)/shard_map/slice | solution.py:921
  155.4 4.4 fusion.96
  163.7 5.2 multiply_convert_fusion.1
  180.2 26.5 %shard_map.327 = (f32[64,1152]{1,0:T(8,128)S(1)}, f32[1,1152]{1,0:T(1,128)S(1)}, bf16[2,4,64,1152]{3,2,1,0:T(8,128)(2,1)S(1)}, bf16[32,36,224]{2,1,0:T(8,128)(2,1)S(1)}) custom-call(bf16[32,36,224]{2,1,0:T(8,128)(2,1)S(1)} %pad_dynamic-update-slice_fusion.refs_0_, bf16[2,4,64,1152]{3,2,1,0:T(8,128)(2,1)S(1)} %bitcast.235, ...), custom_call_target="tpu_custom_call" | custom-call | tf_op jit(solution)/shard_map/pallas_call | solution.py:702
  206.7 5.2 multiply_convert_fusion
  215.8 23.9 %shard_map.328 = (f32[64,1152]{1,0:T(8,128)S(1)}, f32[1,1152]{1,0:T(1,128)S(1)}, f32[1,1152]{1,0:T(1,128)S(1)}, bf16[2,4,64,1152]{3,2,1,0:T(8,128)(2,1)S(1)}) custom-call(bf16[2,4,64,1152]{3,2,1,0:T(8,128)(2,1)S(1)} %bitcast.234, f32[64,1152]{1,0:T(8,128)S(1)} %get-tuple-element.45.refs_2_.refs_1_, f32[64,1152]{1,0:T(8,128)S(1)} %get-tuple-element.47.refs_2_, ...), custom_call_target="tpu_custom_call" | custom-call | tf_op jit(solution)/shard_map/pallas_call | solution.py:702
  246.9 12.9 %shard_map.329 = bf16[3,4,64,512]{3,2,1,0:T(8,128)(2,1)} custom-call(bf16[3,4,64,512]{3,2,1,0:T(8,128)(2,1)} %rev.7.refs_0_), custom_call_target="tpu_custom_call" | custom-call | tf_op jit(solution)/shard_map/pallas_call | solution.py:611
  265.5 12.5 %shard_map.330 = (bf16[8,64,512]{2,1,0:T(8,128)(2,1)S(1)}, bf16[2,256,1664]{2,1,0:T(8,128)(2,1)S(1)}) custom-call(bf16[64,512]{1,0:T(8,128)(2,1)S(1)} %pad_maximum_fusion.10.refs_0_, bf16[256,1664]{1,0:T(8,128)(2,1)S(1)} %pad_maximum_fusion.refs_1_), custom_call_target="tpu_custom_call" | custom-call | tf_op jit(solution)/shard_map/pallas_call | solution.py:150
  293.8 24.3 %shard_map.331 = (f32[1,1152]{1,0:T(1,128)S(1)}, bf16[4,64,1152]{2,1,0:T(8,128)(2,1)S(1)}, bf16[4,64,1152]{2,1,0:T(8,128)(2,1)S(1)}) custom-call(bf16[4,64,1152]{2,1,0:T(8,128)(2,1)S(1)} %bitcast.229, f32[64,1152]{1,0:T(8,128)S(1)} %get-tuple-element.177.refs_2_.refs_1_, f32[64,1152]{1,0:T(8,128)S(1)} %copy-done.13, f32[64,1152]{1,0:T(8,128)S(1)} %copy-done.11, ...), custom_call_target="tpu_custom_call" | custom-call | tf_op jit(solution)/shard_map/pallas_call | solution.py:702
  320.7 4.1 concatenate.104
  337.5 50.7 %shard_map.332 = f32[224,1152]{1,0:T(8,128)S(1)} custom-call(bf16[4,4,224,1152]{3,2,1,0:T(8,128)(2,1)} %bitcast.243), custom_call_target="tpu_custom_call" | custom-call | tf_op jit(solution)/shard_map/pallas_call | solution.py:436
  391.5 5.1 reshape.335.parts
  396.7 60.3 %shard_map.333 = (bf16[2,16,36,1152]{3,2,1,0:T(8,128)(2,1)S(1)}, bf16[8,16,1152]{2,1,0:T(8,128)(2,1)S(1)}) custom-call(bf16[2,16,36,1152]{3,2,1,0:T(8,128)(2,1)} %reshape.335.parts, bf16[16,1152]{1,0:T(8,128)(2,1)S(1)} %slice.327.extra), custom_call_target="tpu_custom_call" | custom-call | tf_op jit(solution)/shard_map/pallas_call | solution.py:530
  467.1 4.1 fusion.5
  471.2 4.1 fusion.6
  479.5 4.1 fusion.4
  483.6 4.1 fusion.8
  487.8 5.4 fusion.9
  495.1 8.3 %fusion.16 = bf16[224,1152]{1,0:T(8,128)(2,1)S(1)} fusion(f32[224,1152]{1,0:T(8,128)S(1)} %convolution_add_fusion.6, bf16[1152,1152]{1,0:T(8,128)(2,1)} %fusion.9), kind=kOutput, calls=%fused_computation.46 | convolution fusion | flops 3659857920 | bytes 4202496 | tf_op jit(solution)/shard_map/dot_general | solution.py:768
  506.1 24.1 %shard_map.334 = bf16[32,36,512]{2,1,0:T(8,128)(2,1)S(1)} custom-call(bf16[32,36,512]{2,1,0:T(8,128)(2,1)S(1)} %fusion.25.refs_0_), custom_call_target="tpu_custom_call" | custom-call | tf_op jit(solution)/shard_map/pallas_call | solution.py:150
  (409 shorter events, 166.2 us)
Async XLA Ops:
  55.7 26.4 %copy-start.20 = (bf16[1152,384]{1,0:T(8,128)(2,1)}, bf16[1152,384]{1,0:T(8,128)(2,1)S(1)}, u32[]{:S(2)}) copy-start(bf16[1152,384]{1,0:T(8,128)(2,1)S(1)} %reshape_squeeze.15) | copy-start | bytes 2654212
  57.5 38.5 %copy-start.21 = (f32[256,384]{1,0:T(8,128)}, f32[256,384]{1,0:T(8,128)S(1)}, u32[]{:S(2)}) copy-start(f32[256,384]{1,0:T(8,128)S(1)} %fusion.95) | copy-start | bytes 1179652
  84.3 6.8 %copy-start.26 = (bf16[3,4,256,128]{2,3,1,0:T(8,128)(2,1)S(1)}, bf16[3,4,256,128]{2,3,1,0:T(8,128)(2,1)}, u32[]{:S(2)}) copy-start(bf16[3,4,256,128]{2,3,1,0:T(8,128)(2,1)} %copy.132) | copy-start | bytes 2359300
  91.1 171.7 %copy-start.63 = (f32[256]{0:T(256)}, f32[256]{0:T(256)S(1)}, u32[]{:S(2)}) copy-start(f32[256]{0:T(256)S(1)} %mul.583) | copy-start | bytes 3076
  180.2 26.5 %copy-start.40 = (bf16[1152,896]{1,0:T(8,128)(2,1)S(1)}, bf16[1152,896]{1,0:T(8,128)(2,1)}, u32[]{:S(2)}) copy-start(bf16[1152,896]{1,0:T(8,128)(2,1)} %squeeze.37) | copy-start | bytes 6193156
  215.8 24.6 %copy-start.25 = (bf16[1152,256]{1,0:T(8,128)(2,1)S(1)}, bf16[1152,256]{1,0:T(8,128)(2,1)}, u32[]{:S(2)}) copy-start(bf16[1152,256]{1,0:T(8,128)(2,1)} %copy-done.24) | copy-start | bytes 1769476
  215.8 25.0 %copy-start.69 = (f32[256]{0:T(256)S(1)}, f32[256]{0:T(256)}, u32[]{:S(2)}) copy-start(f32[256]{0:T(256)} %copy-done.68) | copy-start | bytes 3076
  245.9 18.0 %copy-start.66 = (f32[256]{0:T(256)S(1)}, f32[256]{0:T(256)}, u32[]{:S(2)}) copy-start(f32[256]{0:T(256)} %copy-done.65) | copy-start | bytes 3076
  246.9 17.2 %copy-start.23 = (bf16[256,1152]{1,0:T(8,128)(2,1)S(1)}, bf16[256,1152]{1,0:T(8,128)(2,1)}, u32[]{:S(2)}) copy-start(bf16[256,1152]{1,0:T(8,128)(2,1)} %multiply_convert_fusion.2) | copy-start | bytes 1769476
  246.9 17.2 %copy-start.47 = (bf16[256,256]{1,0:T(8,128)(2,1)S(1)}, bf16[256,256]{1,0:T(8,128)(2,1)}, u32[]{:S(2)}) copy-start(bf16[256,256]{1,0:T(8,128)(2,1)} %convolution_convert_fusion.11) | copy-start | bytes 393220
  264.1 17.6 %copy-start.42 = (bf16[256,256]{1,0:T(8,128)(2,1)}, bf16[256,256]{1,0:T(8,128)(2,1)S(1)}, u32[]{:S(2)}) copy-start(bf16[256,256]{1,0:T(8,128)(2,1)S(1)} %subtract_convert_fusion.1) | copy-start | bytes 393220
  337.5 50.7 %copy-start.4 = (bf16[32,36,224]{2,1,0:T(8,128)(2,1)S(1)}, bf16[32,36,224]{2,1,0:T(8,128)(2,1)}, u32[]{:S(2)}) copy-start(bf16[32,36,224]{2,1,0:T(8,128)(2,1)} %copy-done.3) | copy-start | bytes 1548292
  388.2 8.4 %copy-start = (f32[224,1152]{1,0:T(8,128)}, f32[224,1152]{1,0:T(8,128)S(1)}, u32[]{:S(2)}) copy-start(f32[224,1152]{1,0:T(8,128)S(1)} %shard_map.332) | copy-start | bytes 3096580
  396.7 60.3 %copy-start.35 = (bf16[224,1152]{1,0:T(8,128)(2,1)}, bf16[224,1152]{1,0:T(8,128)(2,1)S(1)}, u32[]{:S(2)}) copy-start(bf16[224,1152]{1,0:T(8,128)(2,1)S(1)} %convert.159) | copy-start | bytes 1548292
  495.1 8.3 %copy-start.36 = (bf16[224,1152]{1,0:T(8,128)(2,1)S(1)}, bf16[224,1152]{1,0:T(8,128)(2,1)}, u32[]{:S(2)}) copy-start(bf16[224,1152]{1,0:T(8,128)(2,1)} %copy-done.35) | copy-start | bytes 1548292
  540.0 7.7 %copy-start.53 = (f32[256,36]{0,1:T(8,128)S(1)}, f32[256,36]{0,1:T(8,128)}, u32[]{:S(2)}) copy-start(f32[256,36]{0,1:T(8,128)} %param.26) | copy-start | bytes 110596
  541.1 7.3 %copy-start.54 = (f32[36,256]{1,0:T(8,128)S(1)}, f32[36,256]{1,0:T(8,128)}, u32[]{:S(2)}) copy-start(f32[36,256]{1,0:T(8,128)} %param.31) | copy-start | bytes 110596
  541.1 8.0 %copy-start.55 = (f32[36,256]{1,0:T(8,128)S(1)}, f32[36,256]{1,0:T(8,128)}, u32[]{:S(2)}) copy-start(f32[36,256]{1,0:T(8,128)} %param.24) | copy-start | bytes 110596
  541.1 8.7 %copy-start.67 = (f32[4,36]{1,0:T(4,128)S(1)}, f32[4,36]{1,0:T(4,128)}, u32[]{:S(2)}) copy-start(f32[4,36]{1,0:T(4,128)} %param.29) | copy-start | bytes 1732
  541.1 11.0 %copy-start.8 = (bf16[4,64,1152]{2,1,0:T(8,128)(2,1)S(1)}, bf16[4,64,1152]{2,1,0:T(8,128)(2,1)}, u32[]{:S(2)}) copy-start(bf16[4,64,1152]{2,1,0:T(8,128)(2,1)} %copy-done.7) | copy-start | bytes 1769476
  541.9 7.8 %copy-start.72 = (f32[4,36]{1,0:T(4,128)S(1)}, f32[4,36]{1,0:T(4,128)}, u32[]{:S(2)}) copy-start(f32[4,36]{1,0:T(4,128)} %param.36) | copy-start | bytes 1732
  541.9 9.6 %copy-start.73 = (f32[2,2]{1,0:T(2,128)S(1)}, f32[2,2]{1,0:T(2,128)}, u32[]{:S(2)}) copy-start(f32[2,2]{1,0:T(2,128)} %param.30) | copy-start | bytes 52
  541.9 9.6 %copy-start.74 = (f32[2,2]{1,0:T(2,128)S(1)}, f32[2,2]{1,0:T(2,128)}, u32[]{:S(2)}) copy-start(f32[2,2]{1,0:T(2,128)} %param.37) | copy-start | bytes 52
  544.6 8.7 %copy-start.6 = (bf16[4,64,1152]{2,1,0:T(8,128)(2,1)S(1)}, bf16[4,64,1152]{2,1,0:T(8,128)(2,1)}, u32[]{:S(2)}) copy-start(bf16[4,64,1152]{2,1,0:T(8,128)(2,1)} %copy-done.5) | copy-start | bytes 1769476
  (57 other events, 158.5 us)

commit v3 on v2

--- a/solution.py
+++ b/solution.py
@@ -24,6 +24,7 @@
 FFP = 1792
 HALF = 896
 BLK = 224
+PART = 192
 BF = jnp.bfloat16
 F32 = jnp.float32
 MESH = pl.DeviceIdType.MESH
@@ -199,8 +200,8 @@
         return out.at[me["c"], at["z"], at["x"]]
 
     here = spot(a, b)
-    mine = near.at[a, pl.ds(me["c"] * 3, 3)]
-    theirs = near.at[a, pl.ds((1 - me["c"]) * 3, 3)]
+    mine = near.at[a, me["c"]]
+    theirs = near.at[a, 1 - me["c"]]
     own = pltpu.make_async_copy(block, here, local_sem.at[0])
     own.start()
     keep = pltpu.make_async_copy(ffn.at[me["c"]], mine, local_sem.at[1])
@@ -214,7 +215,7 @@
     own.wait()
     up, down = to(a_next, b), to(a_last, b)
     first = [sent(here, spot(a_last, b), 1, up), sent(here, spot(a_next, b), 2, down)]
-    there = near.at[b, pl.ds(me["c"] * 3, 3)]
+    there = near.at[b, me["c"]]
     remote(ffn.at[1 - me["c"]], there, send_sem.at[0], recv_sem.at[0], twin).start()
     keep.wait()
     remote(ffn.at[1 - me["c"]], theirs, send_sem.at[0], recv_sem.at[0], twin).wait()
@@ -231,10 +232,9 @@
     ]
     for w in ffn_first:
         w.wait()
-    lo, hi = pl.ds(0, 3), pl.ds(3, 3)
     late = [
-        sent(near.at[a_last, lo], near.at[a_far, lo], 19, up),
-        sent(near.at[a_next, hi], near.at[a_far, hi], 20, down),
+        sent(near.at[a_last, 0], near.at[a_far, 0], 19, up),
+        sent(near.at[a_next, 1], near.at[a_far, 1], 20, down),
     ]
     for i in range(4):
         w_last, w_next = waits[i]
@@ -257,7 +257,7 @@
         gather_body,
         out_shape=[
             jax.ShapeDtypeStruct((2, 4, 4) + block.shape, block.dtype),
-            jax.ShapeDtypeStruct((4, 6) + ffn.shape[2:], ffn.dtype),
+            jax.ShapeDtypeStruct((4, 2) + ffn.shape[1:], ffn.dtype),
         ],
         in_specs=[hbm, hbm],
         out_specs=[hbm, hbm],
@@ -367,7 +367,7 @@
         self.middle = lambda: None
 
 
-def reduce_body(parts, total, p, r1, r2, q, r3, r4, send_sem, recv_sem, local_sem):
+def reduce_body(by0, by1, by2, by3, total, p, r1, r2, q, r3, r4, send_sem, recv_sem, local_sem):
     me = place()
     a, b, to = virtual(me, "z", "x")
     a_next, a_last, a_far = (a + 1) % 4, (a + 3) % 4, (a + 2) % 4
@@ -380,12 +380,15 @@
         w = to(av, bv)
         return ref.at[w["z"], w["x"]]
 
-    load = pltpu.make_async_copy(parts, p, local_sem.at[0])
-    load.start()
+    loads = [pltpu.make_async_copy(by, p.at[i], local_sem.at[i]) for i, by in enumerate((by0, by1, by2, by3))]
+    for load in loads:
+        load.start()
     pl.semaphore_wait(barrier, 4)
+    for load in loads:
+        load.wait()
     first = []
     for i in range(4):
-        first.append(remote(at(parts, a_far, i), r1.at[i], send_sem.at[i], recv_sem.at[i], up if i < 2 else down))
+        first.append(remote(at(p, a_far, i), r1.at[i], send_sem.at[i], recv_sem.at[i], up if i < 2 else down))
         first[-1].start()
     second = []
 
@@ -396,8 +399,7 @@
         second.append(copy)
 
     for i in range(4):
-        onward(i, 1 if i < 2 else 0, at(parts, a_last if i < 2 else a_next, i))
-    load.wait()
+        onward(i, 1 if i < 2 else 0, at(p, a_last if i < 2 else a_next, i))
     for i in range(4):
         first[i].wait()
         dest = at(p, a_next if i < 2 else a_last, i)
@@ -432,11 +434,11 @@
 
 
 def reduce_plane(parts, cid):
-    block = parts.shape[2:]
+    block = parts[0].shape[1:]
     return pl.pallas_call(
         reduce_body,
         out_shape=jax.ShapeDtypeStruct(block, F32),
-        in_specs=[pl.BlockSpec(memory_space=pl.ANY)],
+        in_specs=[pl.BlockSpec(memory_space=pl.ANY)] * 4,
         out_specs=pl.BlockSpec(memory_space=pltpu.VMEM),
         scratch_shapes=[
             pltpu.VMEM((4, 4) + block, BF),
@@ -447,15 +449,15 @@
             pltpu.VMEM((2,) + block, BF),
             pltpu.SemaphoreType.DMA((18,)),
             pltpu.SemaphoreType.DMA((18,)),
-            pltpu.SemaphoreType.DMA((1,)),
+            pltpu.SemaphoreType.DMA((4,)),
         ],
         compiler_params=pltpu.CompilerParams(
             collective_id=cid, has_side_effects=True, vmem_limit_bytes=48 * 1024 * 1024
         ),
-    )(parts)
-
-
-def gram_body(parts, extra, gram, extras, p, got, mine, bx, send_sem, recv_sem, local_sem):
+    )(*parts)
+
+
+def gram_body(kept, moms, grad, extra, gram, extras, mom, flat, parts, p, got, mine, bx, send_sem, recv_sem, local_sem):
     me = place()
     c, z = me["c"], me["z"]
     axes = ("x", "y")
@@ -465,6 +467,23 @@
         pl.semaphore_signal(barrier, inc=1, device_id=device(moved(me, decode(i, axes), -1)), device_id_type=MESH)
     for i in range(4):
         pl.semaphore_signal(barrier, inc=1, device_id=device({**twin, "y": (me["y"] + i) % 4}), device_id_type=MESH)
+    new = 0.95 * moms[...].astype(F32) + grad[...]
+    new = jnp.where(lax.broadcasted_iota(jnp.int32, (BLK, 1), 0) < kept[...], new, 0.0)
+    mom[...] = new
+    flat[...] = new.astype(BF)
+    start = 0
+    for j in range(D // 128):
+        tall = 128 * (j + 1)
+        value = dot(flat[:, pl.ds(0, tall)], flat[:, pl.ds(128 * j, 128)], TN).astype(BF)
+        while tall:
+            part, row = divmod(start, PART)
+            size = min(tall, PART - row)
+            done = 128 * (j + 1) - tall
+            parts[part // 16, part % 16, pl.ds(row, size), :] = value[done : done + size]
+            start, tall = start + size, tall - size
+    for part in range(start // PART, 32):
+        row = start % PART if part == start // PART else 0
+        parts[part // 16, part % 16, pl.ds(row, PART - row), :] = jnp.zeros((PART - row, 128), BF)
     load = pltpu.make_async_copy(parts.at[c], p, local_sem.at[0])
     load.start()
     keep = pltpu.make_async_copy(extra, extras.at[rank(me, ("c", "y"))], local_sem.at[1])
@@ -524,18 +543,21 @@
         w.wait()
 
 
-def gram_sum(parts, extra, cid):
+def gram_sum(kept, moms, grad, extra, cid):
     vmem = pl.BlockSpec(memory_space=pltpu.VMEM)
-    half = parts.shape[1:]
+    half = (16, PART, 128)
     return pl.pallas_call(
         gram_body,
         out_shape=[
-            jax.ShapeDtypeStruct(parts.shape, BF),
+            jax.ShapeDtypeStruct((2,) + half, BF),
             jax.ShapeDtypeStruct((8,) + extra.shape, extra.dtype),
+            jax.ShapeDtypeStruct(grad.shape, F32),
         ],
-        in_specs=[vmem, vmem],
-        out_specs=[vmem, vmem],
+        in_specs=[vmem] * 4,
+        out_specs=[vmem] * 3,
         scratch_shapes=[
+            pltpu.VMEM(moms.shape, BF),
+            pltpu.VMEM((2,) + half, BF),
             pltpu.VMEM(half, BF),
             pltpu.VMEM(half, BF),
             pltpu.VMEM(half, BF),
@@ -547,7 +569,7 @@
         compiler_params=pltpu.CompilerParams(
             collective_id=cid, has_side_effects=True, vmem_limit_bytes=48 * 1024 * 1024
         ),
-    )(parts, extra)
+    )(kept, moms, grad, extra)
 
 
 def halo_body(sign, kinds, *refs):
@@ -574,10 +596,13 @@
                 continue
             ty = (y + t) % 4
             sy = (y + 4 - t) % 4
-            src = ins[i].at[d, ty] if kind == "split" else ins[i]
+            src = ins[i].at[pl.ds(pl.multiple_of((2 - d) * TOK + ty * QTOK, QTOK), QTOK)] if kind == "split" else ins[i]
             tdp = (dp + d) % 32 if sign > 0 else (dp + 32 - d) % 32
             if kind == "near":
                 to, frm = outs[i].at[y], outs[i].at[sy]
+            elif kind == "all":
+                rows = pl.ds((2 - d) * TOK, TOK)
+                to, frm = (outs[i].at[rows, pl.ds(pl.multiple_of(at * 128, 128), 128)] for at in (y, sy))
             else:
                 to, frm = outs[i].at[d, y], outs[i].at[d, sy]
             if p == 0:
@@ -606,7 +631,7 @@
     kinds = [m for _, m in items]
     shapes = []
     for a, m in items:
-        shapes.append((4,) + a.shape if m == "near" else (3, 4) + (a.shape[2:] if m == "split" else a.shape))
+        shapes.append({"near": (4,) + a.shape, "all": (3 * TOK, 512), "split": (3, 4, QTOK, 512)}[m])
     k = len(items)
     return pl.pallas_call(
         functools.partial(halo_body, sign, kinds),
@@ -773,6 +798,195 @@
 TN = ((0,), (0,))
 
 
+def ffn_body(blocks, tokens, dense, gate, up, mixed, f):
+    for k in range(32):
+        for m in range(3):
+            dense[m, pl.ds(ROWS * k, ROWS), :] = blocks[k, pl.ds(ROWS * m, ROWS), :]
+    inner = math.sqrt(2.0 / math.pi)
+
+    def body(i, carry):
+        rows = pl.ds(pl.multiple_of(i * TOK, TOK), TOK)
+        low = tokens[rows, :]
+        g = dot(low, dense[0], NN)
+        gate[rows, :] = g
+        u = dot(low, dense[1], NN)
+        up[rows, :] = u
+        th = jnp.tanh(inner * (g + 0.044715 * g * g * g))
+        z = (0.5 * g * (1.0 + th) * u).astype(BF)
+        mixed[rows, :] = z
+        f[rows, :] = dot(z, dense[2], NT).astype(BF)
+        return carry
+
+    lax.fori_loop(0, 2, body, 0)
+
+
+def ffn_forward(blocks, tokens):
+    vmem = pl.BlockSpec(memory_space=pltpu.VMEM)
+    return pl.pallas_call(
+        ffn_body,
+        out_shape=[
+            jax.ShapeDtypeStruct((3, D, HALF), BF),
+            jax.ShapeDtypeStruct((512, HALF), F32),
+            jax.ShapeDtypeStruct((512, HALF), F32),
+            jax.ShapeDtypeStruct((512, HALF), BF),
+            jax.ShapeDtypeStruct((512, D), BF),
+        ],
+        in_specs=[vmem] * 2,
+        out_specs=[vmem] * 5,
+        compiler_params=pltpu.CompilerParams(vmem_limit_bytes=48 * 1024 * 1024),
+    )(blocks, tokens)
+
+
+def attention_body(kv, sort, q_raw, gq, gk, cosine, sine, seg_q, seg_k, woT, qr, kr, vb, k_own, probs, ob, u):
+    sorted_kv = dot(kv[...], sort[...], NN)
+    k_raw = sorted_kv[:, :HD]
+    v = sorted_kv[:, HD:].astype(BF)
+    vb[...] = v
+    k_own[...] = k_raw[2 * TOK :]
+    k = rot(k_raw * inv_rms(k_raw) * gk[...], cosine[...], sine[...]).astype(BF)
+    kr[...] = k
+    raw = q_raw[...]
+    q = rot(raw * inv_rms(raw) * gq[...], cosine[pl.ds(2 * TOK, TOK), :], sine[pl.ds(2 * TOK, TOK), :]).astype(BF)
+    qr[...] = q
+    shape = (TOK, 3 * TOK)
+    gap = lax.broadcasted_iota(jnp.int32, shape, 0) + 2 * TOK - lax.broadcasted_iota(jnp.int32, shape, 1)
+    allowed = (seg_q[...] == seg_k[...]) & (gap >= 0) & (gap < WINDOW)
+    scores = jnp.where(allowed, dot(q, k, NT) * (HD**-0.5), -1e30)
+    exps = jnp.exp(scores - jnp.max(scores, axis=-1, keepdims=True))
+    p = exps / jnp.sum(exps, axis=-1, keepdims=True)
+    probs[...] = p
+    o = dot(p.astype(BF), v, NN).astype(BF)
+    ob[...] = o
+    u[...] = dot(o, woT[...], NT).astype(BF)
+
+
+def attention(*args):
+    vmem = pl.BlockSpec(memory_space=pltpu.VMEM)
+    wide = 3 * TOK
+    shapes = [
+        ((TOK, HD), BF),
+        ((wide, HD), BF),
+        ((wide, HD), BF),
+        ((TOK, HD), F32),
+        ((TOK, wide), F32),
+        ((TOK, HD), BF),
+        ((TOK, D), BF),
+    ]
+    return pl.pallas_call(
+        attention_body,
+        out_shape=[jax.ShapeDtypeStruct(s, t) for s, t in shapes],
+        in_specs=[vmem] * len(args),
+        out_specs=[vmem] * len(shapes),
+        compiler_params=pltpu.CompilerParams(vmem_limit_bytes=32 * 1024 * 1024),
+    )(*args)
+
+
+def attention_back_body(*refs):
+    du_all, woT, vb, probs, kr, qr, q_raw, gq, gk, cosine, sine, k_own, normed, ob = refs[:14]
+    dkv_all, a_all, ob_all, dq_all, dgq, dgk = refs[14:20]
+    part, got, dkvb, send_sem, recv_sem, local_sem = refs[20:]
+    me = place()
+    c, y, dp = me["c"], me["y"], lax.axis_index("dp")
+    twin = {**me, "c": 1 - c}
+
+    def along(d, t):
+        at = (dp + d + 32) % 32
+        return {"z": at // 8, "x": (at // 2) % 4, "c": at % 2, "y": (y + t + 4) % 4}
+
+    offs = [(d, t) for d in range(3) for t in range(4)][1:]
+    group = [decode(p, ("c", "y")) for p in range(1, 8)]
+    places = [along(d, -t) for d, t in offs] + [moved(me, off, -1) for off in group]
+    barrier = greet_all(places)
+    pl.semaphore_wait(barrier, len(places))
+    waits = []
+
+    def to_twin(src, out, sem):
+        remote(src, out.at[c], send_sem.at[sem], recv_sem.at[sem], twin).start()
+        waits.append(remote(src, out.at[1 - c], send_sem.at[sem], recv_sem.at[sem], twin))
+        own = pltpu.make_async_copy(src, out.at[c], local_sem.at[sem])
+        own.start()
+        waits.append(own)
+
+    to_twin(normed, a_all, 0)
+    to_twin(ob, ob_all, 1)
+    scale = HD**-0.5
+    dub = du_all[pl.ds(pl.multiple_of(c * TOK, TOK), TOK), :]
+    dob = dot(dub, woT[...], NN).astype(BF)
+    p = probs[...]
+    dp_ = dot(dob, vb[...], NT)
+    ds = (p * (dp_ - jnp.sum(p * dp_, axis=-1, keepdims=True))).astype(BF)
+    part[:, pl.ds(0, HD)] = (dot(ds, qr[...], TN) * scale).astype(BF)
+    part[:, pl.ds(HD, HD)] = dot(p.astype(BF), dob, TN).astype(BF)
+    own = pltpu.make_async_copy(part.at[pl.ds(pl.multiple_of(2 * TOK + y * QTOK, QTOK), QTOK)], got.at[0, y], local_sem.at[2])
+    own.start()
+    halo_waits = []
+    for i, (d, t) in enumerate(offs):
+        target = along(-d, t)
+        src = part.at[pl.ds(pl.multiple_of((2 - d) * TOK + target["y"] * QTOK, QTOK), QTOK)]
+        sems = (send_sem.at[3 + i], recv_sem.at[3 + i])
+        remote(src, got.at[d, y], *sems, target).start()
+        halo_waits.append(remote(src, got.at[d, (y + 4 - t) % 4], *sems, target))
+    raw = q_raw[...]
+    dqr = dot(ds, kr[...], NN) * scale
+    here = pl.ds(2 * TOK, TOK)
+    dq, dg = rms_back(raw, gq[...], inv_rms(raw), unrot(dqr, cosine[here, :], sine[here, :]))
+    dgq[...] = dg
+    dq_all[c] = dq.astype(BF)
+    remote(dq_all.at[c], dq_all.at[c], send_sem.at[2], recv_sem.at[2], twin).start()
+    waits.append(remote(dq_all.at[c], dq_all.at[1 - c], send_sem.at[2], recv_sem.at[2], twin))
+    own.wait()
+    for w in halo_waits:
+        w.wait()
+    total = got[0, 0].astype(F32)
+    for i in range(1, 12):
+        total = total + got[i // 4, i % 4].astype(F32)
+    k = k_own[pl.ds(pl.multiple_of(y * QTOK, QTOK), QTOK), :]
+    rows = pl.ds(pl.multiple_of(2 * TOK + y * QTOK, QTOK), QTOK)
+    dk, dg = rms_back(k, gk[...], inv_rms(k), unrot(total[:, :HD], cosine[rows, :], sine[rows, :]))
+    dgk[...] = dg
+    dkvb[:, pl.ds(0, HD)] = dk.astype(BF)
+    dkvb[:, pl.ds(HD, HD)] = total[:, HD:].astype(BF)
+    own = pltpu.make_async_copy(dkvb, dkv_all.at[c, y], local_sem.at[3])
+    own.start()
+    waits.append(own)
+    for i, off in enumerate(group):
+        target, source = moved(me, off, 1), moved(me, off, -1)
+        sems = (send_sem.at[14 + i], recv_sem.at[14 + i])
+        remote(dkvb, dkv_all.at[c, y], *sems, target).start()
+        waits.append(remote(dkvb, dkv_all.at[source["c"], source["y"]], *sems, target))
+    for w in waits:
+        w.wait()
+
+
+def attention_back(cid, *args):
+    vmem = pl.BlockSpec(memory_space=pltpu.VMEM)
+    shapes = [
+        ((2, 4, QTOK, 512), BF),
+        ((2, TOK, D), BF),
+        ((2, TOK, HD), BF),
+        ((2, TOK, HD), BF),
+        ((1, HD), F32),
+        ((1, HD), F32),
+    ]
+    return pl.pallas_call(
+        attention_back_body,
+        out_shape=[jax.ShapeDtypeStruct(s, t) for s, t in shapes],
+        in_specs=[vmem] * len(args),
+        out_specs=[vmem] * len(shapes),
+        scratch_shapes=[
+            pltpu.VMEM((3 * TOK, 512), BF),
+            pltpu.VMEM((3, 4, QTOK, 512), BF),
+            pltpu.VMEM((QTOK, 512), BF),
+            pltpu.SemaphoreType.DMA((21,)),
+            pltpu.SemaphoreType.DMA((21,)),
+            pltpu.SemaphoreType.DMA((4,)),
+        ],
+        compiler_params=pltpu.CompilerParams(
+            collective_id=cid, has_side_effects=True, vmem_limit_bytes=40 * 1024 * 1024
+        ),
+    )(*args)
+
+
 def rope_tables():
     freqs = 10000.0 ** (-np.arange(128, dtype=np.float64) * 2.0 / 256)
     base = (np.arange(32, dtype=np.float64) - 2)[:, None] * 256 * freqs[None]
@@ -800,18 +1014,73 @@
     return big, small
 
 
-def orthogonal(gram, columns):
-    diag = jnp.sum(jnp.where(jnp.eye(D, dtype=bool), gram.astype(F32), 0.0))
+def block_row(i, j):
+    return 128 * (j * (j + 1) // 2 + i)
+
+
+def chain_body(side, side_in, gram, mom, x, side_out, a, r, t, side_send, side_recv):
+    me = place()
+    places = side.places(me)
+    barrier = greet_all(places)
+    pl.semaphore_wait(barrier, len(places))
+    side.start(me, side_in, side_out, side_send, side_recv)
+    eye = lax.broadcasted_iota(jnp.int32, (128, 128), 0) == lax.broadcasted_iota(jnp.int32, (128, 128), 1)
+    total = jnp.zeros((128, 128), F32)
+    for i in range(D // 128):
+        total = total + jnp.where(eye, gram[pl.ds(block_row(i, i), 128), :].astype(F32), 0.0)
+    diag = jnp.sum(jnp.sum(total, axis=1, keepdims=True), axis=0, keepdims=True)
     inv = 1.0 / (jnp.sqrt(diag) + 1e-07)
-    a = (gram.astype(F32) * inv * inv).astype(BF)
-    x = columns * inv
+    step = 384
+
+    def by_rows(fn):
+        def body(i, carry):
+            fn(pl.ds(pl.multiple_of(i * step, step), step))
+            return carry
+
+        lax.fori_loop(0, D // step, body, 0)
+
+    def poly(rows):
+        low = a[rows, :]
+        r[rows, :] = (COEF_TWO * low.astype(F32) + COEF_THREE * dot(low, a[...], NN)).astype(BF)
+
+    def once(rows):
+        low = a[rows, :]
+        t[rows, :] = (COEF_ONE * low.astype(F32) + dot(low, r[...], NN)).astype(BF)
+
+    def twice(rows):
+        low = t[rows, :]
+        a[rows, :] = (COEF_ONE * low.astype(F32) + dot(low, r[...], NN)).astype(BF)
+
+    for j in range(D // 128):
+        for i in range(j + 1):
+            block = gram[pl.ds(block_row(i, j), 128), :].astype(F32) * (inv * inv)
+            a[pl.ds(128 * i, 128), pl.ds(128 * j, 128)] = block.astype(BF)
+            if i < j:
+                a[pl.ds(128 * j, 128), pl.ds(128 * i, 128)] = block.T.astype(BF)
+    x[...] = mom[...] * inv
     for i in range(3):
-        r = (COEF_TWO * a.astype(F32) + COEF_THREE * dot(a, a, NN)).astype(BF)
-        x = COEF_ONE * x + dot(x.astype(BF), r, NN)
+        by_rows(poly)
+        x[...] = COEF_ONE * x[...] + dot(x[...].astype(BF), r[...], NN)
         if i < 2:
-            t = (COEF_ONE * a.astype(F32) + dot(a, r, NN)).astype(BF)
-            a = (COEF_ONE * t.astype(F32) + dot(t, r, NN)).astype(BF)
-    return x
+            by_rows(once)
+            by_rows(twice)
+    side.finish()
+
+
+def orthogonal(gram, columns, side_in, cid):
+    side = SideSwap()
+    vmem = pl.BlockSpec(memory_space=pltpu.VMEM)
+    hbm = pl.BlockSpec(memory_space=pl.ANY)
+    return pl.pallas_call(
+        functools.partial(chain_body, side),
+        out_shape=[jax.ShapeDtypeStruct(columns.shape, F32), side.shape(side_in)],
+        in_specs=[hbm, vmem, vmem],
+        out_specs=[vmem, hbm],
+        scratch_shapes=[pltpu.VMEM((D, D), BF)] * 3 + [pltpu.SemaphoreType.DMA((side.sems,))] * 2,
+        compiler_params=pltpu.CompilerParams(
+            collective_id=cid, has_side_effects=True, vmem_limit_bytes=48 * 1024 * 1024
+        ),
+    )(side_in, gram, columns)
 
 
 def local(
@@ -839,6 +1108,7 @@
 
     ffn_w = jnp.concatenate([w_gateup, w_down.T[None]], axis=0).astype(BF)
     ffn_w = jnp.pad(ffn_w, ((0, 0), (0, 0), (0, FFP - FFT))).reshape(3, ROWS, 2, HALF).transpose(2, 0, 1, 3)
+    ffn_w = jnp.pad(ffn_w.reshape(2, 3 * ROWS, HALF), ((0, 0), (0, 4), (0, 0)))
     moms = to_columns(
         jnp.concatenate([mom_gateup, mom_down.T[None]], axis=0).astype(BF),
         [m.astype(BF) for m in (mom_query, mom_output.T, mom_keyval[0], mom_keyval[1])],
@@ -860,8 +1130,9 @@
             ),
         ]
     ).astype(BF)
+    attn_w = jnp.pad(attn_w, ((0, 0), (0, 12), (0, 0)))
     attn_got, ffn_near = gather_plane(attn_w, ffn_w, 1)
-    attn_all = attn_got.transpose(3, 1, 2, 0, 4, 5).reshape(2, 32, ROWS, 384)
+    attn_all = attn_got[..., :ROWS, :].transpose(3, 1, 2, 0, 4, 5).reshape(2, 32, ROWS, 384)
     w_qkv = attn_all[0].reshape(D, 384)
     wq, wkv = w_qkv[:, :256], w_qkv[:, 256:]
     woT = attn_all[1, :, :, :256].reshape(D, 256)
@@ -876,7 +1147,6 @@
     sb = lax.dynamic_slice_in_dim(sin_b, dp, 1, 0)
     cosine = cb * cos_s - sb * sin_s
     sine = sb * cos_s + cb * sin_s
-    cos_q, sin_q = cosine[512:], sine[512:]
 
     normed = (hidden_in * inv_rms(hidden_in) * g0).astype(BF)
     proj = dot(normed, w_qkv, NN)
@@ -884,53 +1154,37 @@
     kv_all, qk_all = halo([(proj[:, 256:].astype(BF), "all"), (qk_mine, "near")], 1, 2)
     qk_full = qk_all[:, :2, :64].reshape(4, 2, 32, 2).transpose(1, 2, 0, 3).reshape(2, HD).astype(F32)
     gq, gk = qk_full[0:1], qk_full[1:2]
-    kv_all = kv_all[::-1].reshape(3, 4, TOK, 2, 64).transpose(3, 0, 2, 1, 4).reshape(2, 3 * TOK, HD)
-    k_raw = kv_all[0].astype(F32)
-    vb = kv_all[1]
-    q_s = inv_rms(q_raw)
-    qr = rot(q_raw * q_s * gq, cos_q, sin_q).astype(BF)
-    kr = rot(k_raw * inv_rms(k_raw) * gk, cosine, sine).astype(BF)
+    order = np.arange(512)
+    sort = np.zeros((512, 512), np.float32)
+    sort[(order % 256) // 64 * 128 + order // 256 * 64 + order % 64, order] = 1.0
     first = jnp.maximum(dp - 2, 0)
     seg_rows = lax.dynamic_slice_in_dim(segs_all, first, 3, 0)
     seg_keys = jnp.where(
         dp >= 2, seg_rows, jnp.where(dp == 1, jnp.roll(seg_rows, 1, axis=0), jnp.roll(seg_rows, 2, axis=0))
     ).reshape(3 * TOK)
-    key_no = jnp.arange(3 * TOK, dtype=jnp.int32)
-    gap = (jnp.arange(TOK, dtype=jnp.int32) + 2 * TOK)[:, None] - key_no[None, :]
-    allowed = (
-        (segment_ids[:, None] == seg_keys[None, :])
-        & (gap >= 0)
-        & (gap < WINDOW)
-        & (key_no + (dp - 2) * TOK >= 0)[None, :]
+    seg_keys = jnp.where(jnp.arange(3 * TOK) >= (2 - dp) * TOK, seg_keys, -1)
+    qr, kr, vb, k_own, probs, ob, u_part = attention(
+        kv_all, jnp.asarray(sort, BF), q_raw, gq, gk, cosine, sine, segment_ids[:, None], seg_keys[None, :], woT
     )
-    scale = HD ** (-0.5)
-    scores = jnp.where(allowed, dot(qr, kr, NT) * scale, -1e30)
-    top = jnp.max(scores, axis=-1, keepdims=True)
-    exps = jnp.exp(scores - top)
-    probs = exps / jnp.sum(exps, axis=-1, keepdims=True)
-    pb = probs.astype(BF)
-    ob = dot(pb, vb, NN).astype(BF)
-    u_part = dot(ob, woT, NT).astype(BF).reshape(4, QTOK, D)
+    u_part = u_part.reshape(4, QTOK, D)
     hidden_q = lax.dynamic_slice_in_dim(hidden_in, y * QTOK, QTOK, 0)
     grad_q = lax.dynamic_slice_in_dim(out_grad, y * QTOK, QTOK, 0)
     u, hmid, bin_all, ffn_all = sum_then_gather(
         mid_fn, u_part, [hidden_q, g1, g2], [(QTOK, D)] * 2, 1, True, 3, SideGather(), ffn_near
     )
 
-    ffn_full = ffn_all.reshape(32, 3, ROWS, HALF).transpose(1, 0, 2, 3).reshape(3, D, HALF)
-    wg, wu, wdT = ffn_full[0], ffn_full[1], ffn_full[2]
     bin_low = bin_all.reshape(512, D)
-    gate = dot(bin_low, wg, NN)
-    up = dot(bin_low, wu, NN)
+    dense, gate, up, mixed, f_part = ffn_forward(ffn_all.reshape(32, 112, HALF), bin_low)
+    wg, wu, wdT = dense[0], dense[1], dense[2]
     inner = math.sqrt(2.0 / math.pi)
     th = jnp.tanh(inner * (gate + 0.044715 * gate * gate * gate))
     gelu = 0.5 * gate * (1.0 + th)
     gelu_d = 0.5 * (1.0 + th) + 0.5 * gate * (1.0 - th * th) * inner * (1.0 + 3 * 0.044715 * gate * gate)
-    mixed = (gelu * up).astype(BF)
-    f_part = dot(mixed, wdT, NT).astype(BF).reshape(2, 4, QTOK, D)
+    f_part = f_part.reshape(2, 4, QTOK, D)
     block, dg3, df_all, moms_all = sum_then_gather(
         ffn_out_fn, f_part, [hmid, grad_q, g3], [(QTOK, D), (1, D)], 1, True, 5, SideSwap(), moms
     )
+    moms_cols = moms_all.reshape(D, BLK).T
     dfb = df_all.reshape(512, D)
     dz = dot(dfb, wdT, NN)
     dgate = (dz * up * gelu_d).astype(BF)
@@ -947,31 +1201,22 @@
     )
 
     dub_all = du_all.reshape(512, D)
-    dub = lax.dynamic_slice_in_dim(dub_all, c * TOK, TOK, 0)
-    dob = dot(dub, woT, NN).astype(BF)
-    dP = dot(dob, vb, NT)
-    ds = (probs * (dP - jnp.sum(probs * dP, axis=-1, keepdims=True))).astype(BF)
-    dqr = dot(ds, kr, NN) * scale
-    dkr = dot(ds, qr, TN) * scale
-    dv = dot(pb, dob, TN)
-    dkv_part = jnp.concatenate([dkr, dv], axis=1).astype(BF).reshape(3, 4, QTOK, 512)[::-1]
-    (dkv_got,) = halo([(dkv_part, "split")], -1, 7)
-    dkv_sum = jnp.sum(dkv_got.reshape(12, QTOK, 512).astype(F32), axis=0)
-    k_own = lax.dynamic_slice_in_dim(k_raw, 2 * TOK + y * QTOK, QTOK, 0)
-    cos_k = lax.dynamic_slice_in_dim(cos_q, y * QTOK, QTOK, 0)
-    sin_k = lax.dynamic_slice_in_dim(sin_q, y * QTOK, QTOK, 0)
-    dk, dgk = rms_back(k_own, gk, inv_rms(k_own), unrot(dkv_sum[:, :256], cos_k, sin_k))
-    dq, dgq = rms_back(q_raw, gq, q_s, unrot(dqr, cos_q, sin_q))
-    dkvb = jnp.concatenate([dk, dkv_sum[:, 256:]], axis=1).astype(BF)
-    dqb = dq.astype(BF)
-    pair = jnp.concatenate([normed, ob, dqb], axis=1)
-    dkv_all, pair = exchange([(dkvb, "ag"), (pair, "ag", ("c",))], ("c", "y"), 8)
-    pair = pair.reshape(512, D + 512)
-    dkv_all = dkv_all.reshape(512, 2, 4, 64)
-    dkv_cols = lax.dynamic_slice_in_dim(dkv_all, y, 1, 2).reshape(512, 128)
+    dkv_all, a_all, ob_all, dq_all, dgq, dgk = attention_back(
+        7, dub_all, woT, vb, probs, kr, qr, q_raw, gq, gk, cosine, sine, k_own, normed, ob
+    )
+    dqb = lax.dynamic_slice_in_dim(dq_all, c, 1, 0)[0]
+    dkv_all = dkv_all.reshape(512, 512)
+    a_all, ob_all, dq_all = a_all.reshape(512, D), ob_all.reshape(512, HD), dq_all.reshape(512, HD)
+    src, col = jnp.arange(512)[:, None], jnp.arange(128)[None, :]
+    pick_y = (src == col // 64 * 256 + y * 64 + col % 64).astype(BF)
+    col = col[:, :64]
+    pick_c = (src == col // 32 * 256 + y * 64 + c * 32 + col % 32).astype(BF)
+    dkv_mine = lax.dynamic_slice_in_dim(dkv_all, c * TOK, TOK, 0)
+    dkv_y = dot(dkv_mine, pick_y, NN).astype(BF)
+    dkv_cols = dot(dkv_all, pick_c, NN).astype(BF)
     da_part = (
         dot(
-            jnp.concatenate([dqb, lax.dynamic_slice_in_dim(dkv_cols, c * TOK, TOK, 0)], axis=1),
+            jnp.concatenate([dqb, dkv_y], axis=1),
             w_qkv,
             NT,
         )
@@ -988,38 +1233,26 @@
         [dg0, dg1, dg2, dg3, jnp.concatenate([dgq, dgk, jnp.zeros((1, D - 2 * HD), F32)], axis=1)], axis=0
     ).astype(BF)
 
-    a_all, ob_all, dq_all = pair[:, :D], pair[:, D : D + 256], pair[:, D + 256 :]
     ob_cols = lax.dynamic_slice_in_dim(ob_all, c * 128, 128, 1)
     dq_cols = lax.dynamic_slice_in_dim(dq_all, c * 128, 128, 1)
-    dk_cols = lax.dynamic_slice_in_dim(dkv_cols, c * 32, 32, 1)
-    dv_cols = lax.dynamic_slice_in_dim(dkv_cols, 64 + c * 32, 32, 1)
     d_gate = dot(dgate, bin_low, TN).astype(BF)
     d_up = dot(dup, bin_low, TN).astype(BF)
     d_down = dot(mixed, dfb, TN).astype(BF)
     d_q = dot(dq_cols, a_all, TN).astype(BF)
-    d_kv = dot(jnp.concatenate([dk_cols, dv_cols], axis=1), a_all, TN).astype(BF)
+    d_kv = dot(dkv_cols, a_all, TN).astype(BF)
     d_o = dot(ob_cols, dub_all, TN).astype(BF)
-    wgrads = jnp.concatenate(
+    small = jnp.stack(
         [
-            d_gate.reshape(4, BLK, D),
-            d_up.reshape(4, BLK, D),
-            d_down.reshape(4, BLK, D),
-            jnp.pad(d_q, ((0, BLK - 128), (0, 0)))[None],
-            jnp.pad(d_o, ((0, BLK - 128), (0, 0)))[None],
-            jnp.pad(d_kv[:32], ((0, BLK - 32), (0, 0)))[None],
-            jnp.concatenate([d_kv[32:], gain_rows, jnp.zeros((BLK - 37, D), BF)], axis=0)[None],
-        ],
-        axis=0,
+            jnp.pad(d_q, ((0, BLK - 128), (0, 0))),
+            jnp.pad(d_o, ((0, BLK - 128), (0, 0))),
+            jnp.pad(d_kv[:32], ((0, BLK - 32), (0, 0))),
+            jnp.concatenate([d_kv[32:], gain_rows, jnp.zeros((BLK - 37, D), BF)], axis=0),
+        ]
     )
-    wgrad = reduce_plane(wgrads.reshape(4, 4, BLK, D), 11)
-
-    mom = 0.95 * moms_all.reshape(D, BLK).T.astype(F32) + wgrad
-    kept = jnp.where((z == 3) & (x == 3), 32, BLK)
-    mom = jnp.where(jnp.arange(BLK)[:, None] < kept, mom, 0.0)
-    mom_low = mom.astype(BF)
-    gram_part = dot(mom_low, mom_low, TN).astype(BF).reshape(2, 16, ROWS, D)
-    gram, gains_got = gram_sum(gram_part, wgrad[32:48].astype(BF), 13)
-    ortho = orthogonal(gram.reshape(D, D), mom)
+    wgrad = reduce_plane([d_gate.reshape(4, BLK, D), d_up.reshape(4, BLK, D), d_down.reshape(4, BLK, D), small], 11)
+
+    kept = jnp.where((z == 3) & (x == 3), 32, BLK).reshape(1, 1)
+    gram, gains_got, mom = gram_sum(kept, moms_cols, wgrad, wgrad[32:48].astype(BF), 13)
     gain_sum = jnp.sum(gains_got[:, :5].astype(F32), axis=0)
     gain_cols = jnp.concatenate(
         [
@@ -1031,13 +1264,16 @@
         ],
         axis=2,
     )
-    back = jnp.concatenate([ortho.astype(BF), wgrad.astype(BF)], axis=0).T.reshape(32, ROWS, 2 * BLK)
-    back = jnp.concatenate([back, gain_cols.astype(BF), jnp.zeros((32, ROWS, 56), BF)], axis=2)
-    (back_got,) = exchange([(back, "a2a")], ("z", "x", "c"), 14)
-    o_big, o_small = from_columns(back_got[:, :, :BLK].astype(F32))
-    w_big, w_small = from_columns(back_got[:, :, BLK : 2 * BLK].astype(F32))
-    gains_red = back_got[30, :, 448:452].T.astype(F32)
-    qk_red = back_got[30, 0, 452:456].reshape(2, 2).astype(F32)
+    w_back = jnp.concatenate(
+        [wgrad.astype(BF).T.reshape(32, ROWS, BLK), gain_cols.astype(BF), jnp.zeros((32, ROWS, 24), BF)], axis=2
+    )
+    ortho, w_got = orthogonal(gram.reshape(32 * PART, 128), mom, w_back, 12)
+    w_big, w_small = from_columns(w_got[:, :, :BLK].astype(F32))
+    gains_red = w_got[30, :, 224:228].T.astype(F32)
+    qk_red = w_got[30, 0, 228:232].reshape(2, 2).astype(F32)
+    o_back = ortho.astype(BF).T.reshape(32, ROWS, BLK)
+    (o_got,) = exchange([(o_back, "a2a")], ("z", "x", "c"), 14)
+    o_big, o_small = from_columns(o_got.astype(F32))
     gain_rate = 2.0 / math.sqrt(8192)
     next_gain_moms = 0.9 * gain_moms + 0.1 * gains_red
     new_norm_gains = norm_gains - gain_rate * next_gain_moms

time: 561 us -> 469 us (0.84)
  matrix products: 78.1 us -> 18.5 us
  local copies, waits for them, and re-layouts: 106 us -> 75.6 us
  other arithmetic: 47.1 us -> 30.8 us
  Pallas kernels: 320 us -> 335 us
    dot_general x32 -> x12, matrix products: 78.1 us -> 18.5 us  [dot(): return lax.dot_general(a, b, (dims, ((), ())), preferred_element_type=F32)]
    pallas_call x1 -> x5, Pallas kernels: 60.3 us -> 108 us  [the longest x1 36.8 us: orthogonal(): pl.pallas_call(functools.partial(chain_body, side), out_shape=[jax.ShapeD...]
    pallas_call x2 -> x1, Pallas kernels: 36.6 us -> 15.8 us  [exchange(): pl.pallas_call(functools.partial(exchange_body, axes, modes, subs), out_s...]
    unnamed x193 -> x219, local copies, waits for them, and re-layouts: 21.9 us -> 35.6 us
    pallas_call x2 -> x1, Pallas kernels: 31.3 us -> 18.4 us  [halo(): pl.pallas_call(functools.partial(halo_body, sign, kinds), out_shape=[jax....]
    squeeze x3 -> x1, local copies, waits for them, and re-layouts: 11.9 us -> 0.01 us  [local(): dqb = lax.dynamic_slice_in_dim(dq_all, c, 1, 0)[0]]
    convert_element_type x3 -> x1, local copies, waits for them, and re-layouts: 9.1 us -> 0.11 us  [local(): dkv_y = dot(dkv_mine, pick_y, NN).astype(BF)]
    reshape x4 -> x5, local copies, waits for them, and re-layouts: 11.7 us -> 2.83 us  [the longest x1 2.11 us: local(): wgrad.astype(BF).T.reshape(32, ROWS, BLK)]
where the time goes in v3:
time: 469 us; the launch traced here: 463 us
  Pallas kernels  335 us (71%)
  local copies, waits for them, and re-layouts  75.6 us (16%)
  other arithmetic  30.8 us (7%)
  matrix products  18.5 us (4%)
    pallas_call x4, Pallas kernels, sum_then_gather(): pl.pallas_call(functools.partial(sum_body, fn, both, spread, side, len(ex...  105 us
    pallas_call x1, Pallas kernels, reduce_plane(): pl.pallas_call(reduce_body, out_shape=jax.ShapeDtypeStruct(block, F32), i...  52.8 us
    pallas_call x1, Pallas kernels, orthogonal(): pl.pallas_call(functools.partial(chain_body, side), out_shape=[jax.ShapeD...  36.8 us
    pallas_call x1, Pallas kernels, gram_sum(): pl.pallas_call(gram_body, out_shape=[jax.ShapeDtypeStruct((2,) + half, BF...  36.5 us
    unnamed x219, local copies, waits for them, and re-layouts  35.6 us
    pallas_call x1, Pallas kernels, gather_plane(): pl.pallas_call(gather_body, out_shape=[jax.ShapeDtypeStruct((2, 4, 4) + b...  35.3 us
    pallas_call x1, Pallas kernels, attention_back(): pl.pallas_call(attention_back_body, out_shape=[jax.ShapeDtypeStruct(s, t)...  23.3 us
    dot_general x12, matrix products, dot(): return lax.dot_general(a, b, (dims, ((), ())), preferred_element_type=F32)  18.5 us

profile of v3, /device:TPU:1, one launch (start us, length us, event | category | flops | bytes accessed | tf_op | source)
XLA Modules:
  0.0 462.7 jit_solution(12180565884446966690)
XLA Ops:
  10.6 35.3 %shard_map.333 = (bf16[2,4,4,2,48,384]{5,4,3,2,1,0:T(8,128)(2,1)}, bf16[4,2,112,896]{3,2,1,0:T(8,128)(2,1)}) custom-call(bf16[2,48,384]{2,1,0:T(8,128)(2,1)} %fusion.41.block, bf16[2,112,896]{2,1,0:T(8,128)(2,1)} %pad.62.ffn), custom_call_target="tpu_custom_call" | custom-call | tf_op jit(solution)/shard_map/pallas_call | solution.py:256
  45.9 1.8 slice_bitcast_fusion
  53.0 2.0 slice.232
  62.8 18.4 %shard_map.334 = (bf16[768,512]{1,0:T(8,128)(2,1)}, bf16[4,16,128]{2,1,0:T(8,128)(2,1)}) custom-call(bf16[256,128]{1,0:T(8,128)(2,1)} %slice.321.refs_0_, bf16[16,128]{1,0:T(8,128)(2,1)} %pad.63.refs_1_), custom_call_target="tpu_custom_call" | custom-call | tf_op jit(solution)/shard_map/pallas_call | solution.py:636
  83.1 5.9 %slice_reduce_fusion = bf16[32,36,256]{2,1,0:T(8,128)(2,1)} fusion(bf16[2,32,36,384]{3,0,2,1:T(2,128)(2,1)} %bitcast.220), kind=kLoop, calls=%fused_computation.33 | loop fusion | bytes 1179648 | tf_op jit(solution)/shard_map/slice | solution.py:1138
  91.4 1.8 shard_map.335
  102.1 29.9 %shard_map.336 = (f32[64,1152]{1,0:T(8,128)S(1)}, f32[64,1152]{1,0:T(8,128)S(1)}, bf16[2,4,64,1152]{3,2,1,0:T(8,128)(2,1)S(1)}, bf16[4,4,2,112,896]{4,3,2,1,0:T(8,128)(2,1)S(1)}) custom-call(bf16[4,2,112,896]{3,2,1,0:T(8,128)(2,1)S(1)} %copy-done.9, bf16[4,64,1152]{2,1,0:T(8,128)(2,1)S(1)} %bitcast.212, f32[64,1152]{1,0:T(8,128)S(1)} %get-tuple-element.184.refs_2_.refs_1_, ...), custom_call_target="tpu_custom_call" | custom-call | tf_op jit(solution)/shard_map/pallas_call | solution.py:727
  132.1 2.6 copy-done
  134.7 9.3 %shard_map.337 = (bf16[3,1152,896]{2,1,0:T(8,128)(2,1)}, f32[512,896]{1,0:T(8,128)S(1)}, f32[512,896]{1,0:T(8,128)}, bf16[512,896]{1,0:T(8,128)(2,1)S(1)}, bf16[512,1152]{1,0:T(8,128)(2,1)S(1)}) custom-call(bf16[32,112,896]{2,1,0:T(8,128)(2,1)} %bitcast.195, bf16[512,1152]{1,0:T(8,128)(2,1)S(1)} %bitcast.209), custom_call_target="tpu_custom_call" | custom-call | tf_op jit(solution)/shard_map/pallas_call | solution.py:825
  150.9 2.7 reshape.316
  156.3 25.7 %shard_map.338 = (f32[64,1152]{1,0:T(8,128)S(1)}, f32[1,1152]{1,0:T(1,128)S(1)}, bf16[2,4,64,1152]{3,2,1,0:T(8,128)(2,1)S(1)}, bf16[32,36,224]{2,1,0:T(8,128)(2,1)S(1)}) custom-call(bf16[32,36,224]{2,1,0:T(8,128)(2,1)S(1)} %pad_dynamic-update-slice_fusion.refs_0_, bf16[2,4,64,1152]{3,2,1,0:T(8,128)(2,1)S(1)} %bitcast.206, ...), custom_call_target="tpu_custom_call" | custom-call | tf_op jit(solution)/shard_map/pallas_call | solution.py:727
  182.1 5.2 %multiply_convert_fusion = (bf16[512,896]{1,0:T(8,128)(2,1)S(1)}, bf16[512,896]{1,0:T(8,128)(2,1)S(1)}) fusion(f32[512,896]{1,0:T(8,128)S(1)} %copy-done.62, f32[512,896]{1,0:T(8,128)} %get-tuple-element.69, bf16[512,1152]{1,0:T(8,128)(2,1)S(1)} %bitcast.215, bf16[3,1152,896]{2,1,0:T(8,128)(2,1)} %get-tuple-element.68), kind=kOutput, calls=%fused_computation.30 | convolution fusion | flops 1067515904 | bytes 8749056 | tf_op jit(solution)/shard_map/dot_general | solution.py:793
  190.6 23.9 %shard_map.339 = (f32[64,1152]{1,0:T(8,128)S(1)}, f32[1,1152]{1,0:T(1,128)S(1)}, f32[1,1152]{1,0:T(1,128)S(1)}, bf16[2,4,64,1152]{3,2,1,0:T(8,128)(2,1)S(1)}) custom-call(bf16[2,4,64,1152]{3,2,1,0:T(8,128)(2,1)S(1)} %bitcast.205, f32[64,1152]{1,0:T(8,128)S(1)} %get-tuple-element.66.refs_2_.refs_1_, f32[64,1152]{1,0:T(8,128)S(1)} %get-tuple-element.71.refs_2_, ...), custom_call_target="tpu_custom_call" | custom-call | tf_op jit(solution)/shard_map/pallas_call | solution.py:727
  215.9 23.3 %shard_map.340 = (bf16[2,4,64,512]{3,2,1,0:T(8,128)(2,1)S(1)}, bf16[2,256,1152]{2,1,0:T(8,128)(2,1)S(1)}, bf16[2,256,256]{2,1,0:T(8,128)(2,1)S(1)}, bf16[2,256,2...) custom-call(bf16[512,1152]{1,0:T(8,128)(2,1)S(1)} %bitcast.196, ...), custom_call_target="tpu_custom_call" | custom-call | tf_op jit(solution)/shard_map/pallas_call | solution.py:971
  247.7 25.5 %shard_map.341 = (f32[1,1152]{1,0:T(1,128)S(1)}, bf16[4,64,1152]{2,1,0:T(8,128)(2,1)S(1)}, bf16[4,64,1152]{2,1,0:T(8,128)(2,1)S(1)}) custom-call(bf16[4,64,1152]{2,1,0:T(8,128)(2,1)S(1)} %bitcast.200, f32[64,1152]{1,0:T(8,128)S(1)} %copy-done.6, f32[64,1152]{1,0:T(8,128)S(1)} %copy-done.40, f32[64,1152]{1,0:T(8,128)S(1)} %copy-done.38, ...), custom_call_target="tpu_custom_call" | custom-call | tf_op jit(solution)/shard_map/pallas_call | solution.py:727
  278.3 2.7 convolution_convert_fusion
  283.8 52.8 %shard_map.342.grad = f32[224,1152]{1,0:T(8,128)S(1)} custom-call(bf16[4,224,1152]{2,1,0:T(8,128)(2,1)S(1)} %bitcast.203, bf16[4,224,1152]{2,1,0:T(8,128)(2,1)S(1)} %bitcast.202, bf16[4,224,1152]{2,1,0:T(8,128)(2,1)} %bitcast.223, bf16[4,224,1152]{2,1,0:T(8,128)(2,1)} %pad_maximum_fusion.by3), custom_call_target="tpu_custom_call" | custom-call | tf_op jit(solution)/shard_map/pallas_call | solution.py:438
  338.3 36.5 %shard_map.343 = (bf16[2,16,192,128]{3,2,1,0:T(8,128)(2,1)S(1)}, bf16[8,16,1152]{2,1,0:T(8,128)(2,1)S(1)}, f32[224,1152]{1,0:T(8,128)S(1)}) custom-call(s32[1,1]{1,0:T(1,128)} %bitcast.58.kept, bf16[224,1152]{1,0:T(8,128)(2,1)S(1)} %bitcast.201, f32[224,1152]{1,0:T(8,128)S(1)} %shard_map.342.grad, bf16[16,1152]{1,0:T(8,128)(2,1)S(1)} %slice.247.extra), custom_call_target="tpu_custom_call" | custom-call | tf_op jit(solution)/shard_map/pallas_call | solution.py:549
  377.9 2.1 reshape.297
  381.5 36.8 %shard_map.344 = (f32[224,1152]{1,0:T(8,128)S(1)}, bf16[32,36,256]{2,1,0:T(8,128)(2,1)S(1)}) custom-call(bf16[32,36,256]{2,1,0:T(8,128)(2,1)S(1)} %fusion.23.side_in, bf16[6144,128]{1,0:T(8,128)(2,1)S(1)} %bitcast.204, f32[224,1152]{1,0:T(8,128)S(1)} %copy-done.17), custom_call_target="tpu_custom_call" | custom-call | tf_op jit(solution)/shard_map/pallas_call | solution.py:1074
  421.8 15.8 %shard_map.345 = bf16[32,36,224]{2,1,0:T(8,128)(2,1)S(1)} custom-call(bf16[32,36,224]{2,1,0:T(8,128)(2,1)S(1)} %reshape.303.refs_0_), custom_call_target="tpu_custom_call" | custom-call | tf_op jit(solution)/shard_map/pallas_call | solution.py:151
  438.2 1.7 reshape.305
  444.7 1.7 reshape.309
  448.8 1.7 fusion.27
  (385 shorter events, 94.6 us)
Async XLA Ops:
  53.0 37.4 %copy-start.1 = (f32[768,128]{1,0:T(8,128)}, f32[768,128]{1,0:T(8,128)S(1)}, u32[]{:S(2)}) copy-start(f32[768,128]{1,0:T(8,128)S(1)} %get-tuple-element.164.sine.refs_10_) | copy-start | bytes 1179652
  53.0 37.4 %copy-start.3 = (f32[768,128]{1,0:T(8,128)}, f32[768,128]{1,0:T(8,128)S(1)}, u32[]{:S(2)}) copy-start(f32[768,128]{1,0:T(8,128)S(1)} %get-tuple-element.165.cosine.refs_9_) | copy-start | bytes 1179652
  60.0 23.1 %copy-start.68 = (bf16[1152,384]{1,0:T(8,128)(2,1)}, bf16[1152,384]{1,0:T(8,128)(2,1)S(1)}, u32[]{:S(2)}) copy-start(bf16[1152,384]{1,0:T(8,128)(2,1)S(1)} %reshape_squeeze.15) | copy-start | bytes 2654212
  83.1 10.2 %copy-start.7 = (f32[256,256]{1,0:T(8,128)}, f32[256,256]{1,0:T(8,128)S(1)}, u32[]{:S(2)}) copy-start(f32[256,256]{1,0:T(8,128)S(1)} %slice.237.q_raw.refs_6_) | copy-start | bytes 786436
  99.5 32.5 %copy-start.5 = (f32[64,1152]{1,0:T(8,128)}, f32[64,1152]{1,0:T(8,128)S(1)}, u32[]{:S(2)}) copy-start(f32[64,1152]{1,0:T(8,128)S(1)} %get-tuple-element.184.refs_2_.refs_1_) | copy-start | bytes 884740
  134.7 9.3 %copy-start.14 = (bf16[2,4,64,1152]{3,2,1,0:T(8,128)(2,1)}, bf16[2,4,64,1152]{3,2,1,0:T(8,128)(2,1)S(1)}, u32[]{:S(2)}) copy-start(bf16[2,4,64,1152]{3,2,1,0:T(8,128)(2,1)S(1)} %get-tuple-element.64) | copy-start | bytes 3538948
  134.7 11.4 %copy-start.83 = (f32[2,36,64]{2,0,1:T(2,128)S(1)}, f32[2,36,64]{2,0,1:T(2,128)}, u32[]{:S(2)}) copy-start(f32[2,36,64]{2,0,1:T(2,128)} %param.33) | copy-start | bytes 55300
  156.3 25.8 %copy-start.62 = (f32[512,896]{1,0:T(8,128)S(1)}, f32[512,896]{1,0:T(8,128)}, u32[]{:S(2)}) copy-start(f32[512,896]{1,0:T(8,128)} %copy-done.61) | copy-start | bytes 5505028
  156.3 31.1 %slice-start.1 = ((s8[6193152]{0:T(1024)(128)(4,1)}), s8[4194304]{0:T(1024)(128)(4,1)S(1)}, s32[]{:S(2)}) async-start(s8[6193152]{0:T(1024)(128)(4,1)} %bitcast.248), calls=%async_computation.1 | async-start | bytes 8388608
  189.0 26.8 %copy-start.34 = (bf16[768,256]{1,0:T(8,128)(2,1)S(1)}, bf16[768,256]{1,0:T(8,128)(2,1)}, u32[]{:S(2)}) copy-start(bf16[768,256]{1,0:T(8,128)(2,1)} %copy-done.33) | copy-start | bytes 1179652
  189.0 26.8 %copy-start.36 = (bf16[768,256]{1,0:T(8,128)(2,1)S(1)}, bf16[768,256]{1,0:T(8,128)(2,1)}, u32[]{:S(2)}) copy-start(bf16[768,256]{1,0:T(8,128)(2,1)} %copy-done.35) | copy-start | bytes 1179652
  189.0 26.8 %copy-start.42 = (f32[256,256]{1,0:T(8,128)S(1)}, f32[256,256]{1,0:T(8,128)}, u32[]{:S(2)}) copy-start(f32[256,256]{1,0:T(8,128)} %copy-done.41) | copy-start | bytes 786436
  189.0 26.8 %copy-start.48 = (bf16[256,256]{1,0:T(8,128)(2,1)S(1)}, bf16[256,256]{1,0:T(8,128)(2,1)}, u32[]{:S(2)}) copy-start(bf16[256,256]{1,0:T(8,128)(2,1)} %copy-done.47) | copy-start | bytes 393220
  190.6 25.3 %copy-start.2 = (f32[768,128]{1,0:T(8,128)S(1)}, f32[768,128]{1,0:T(8,128)}, u32[]{:S(2)}) copy-start(f32[768,128]{1,0:T(8,128)} %copy-done.1) | copy-start | bytes 1179652
  190.6 25.3 %copy-start.4 = (f32[768,128]{1,0:T(8,128)S(1)}, f32[768,128]{1,0:T(8,128)}, u32[]{:S(2)}) copy-start(f32[768,128]{1,0:T(8,128)} %copy-done.3) | copy-start | bytes 1179652
  190.6 25.3 %copy-start.8 = (f32[256,256]{1,0:T(8,128)S(1)}, f32[256,256]{1,0:T(8,128)}, u32[]{:S(2)}) copy-start(f32[256,256]{1,0:T(8,128)} %copy-done.7) | copy-start | bytes 786436
  190.6 25.2 %copy-start.21 = (f32[256,768]{1,0:T(8,128)S(1)}, f32[256,768]{1,0:T(8,128)}, u32[]{:S(2)}) copy-start(f32[256,768]{1,0:T(8,128)} %copy-done.20) | copy-start | bytes 2359300
  190.6 25.2 %copy-start.46 = (bf16[256,256]{1,0:T(8,128)(2,1)S(1)}, bf16[256,256]{1,0:T(8,128)(2,1)}, u32[]{:S(2)}) copy-start(bf16[256,256]{1,0:T(8,128)(2,1)} %copy-done.45) | copy-start | bytes 393220
  215.2 24.0 %copy-start.53 = (f32[1,1152]{1,0:T(1,128)}, f32[1,1152]{1,0:T(1,128)S(1)}, u32[]{:S(2)}) copy-start(f32[1,1152]{1,0:T(1,128)S(1)} %get-tuple-element.90) | copy-start | bytes 13828
  245.5 29.4 %copy-start.56 = (f32[1,1152]{1,0:T(1,128)S(1)}, f32[1,1152]{1,0:T(1,128)}, u32[]{:S(2)}) copy-start(f32[1,1152]{1,0:T(1,128)} %copy-done.55) | copy-start | bytes 13828
  245.5 29.4 %copy-start.54 = (f32[1,1152]{1,0:T(1,128)S(1)}, f32[1,1152]{1,0:T(1,128)}, u32[]{:S(2)}) copy-start(f32[1,1152]{1,0:T(1,128)} %copy-done.53) | copy-start | bytes 13828
  245.6 29.4 %copy-start.52 = (f32[1,1152]{1,0:T(1,128)S(1)}, f32[1,1152]{1,0:T(1,128)}, u32[]{:S(2)}) copy-start(f32[1,1152]{1,0:T(1,128)} %copy-done.51) | copy-start | bytes 13828
  247.7 28.3 %copy-start.71 = (bf16[1,224,1152]{2,1,0:T(8,128)(2,1)S(1)}, bf16[1,224,1152]{2,1,0:T(8,128)(2,1)}, u32[]{:S(2)}) copy-start(bf16[1,224,1152]{2,1,0:T(8,128)(2,1)} %pad_bitcast_fusion.2) | copy-start | bytes 1548292
  450.6 9.4 %copy-start.29 = (bf16[4,64,1152]{2,1,0:T(8,128)(2,1)S(1)}, bf16[4,64,1152]{2,1,0:T(8,128)(2,1)}, u32[]{:S(2)}) copy-start(bf16[4,64,1152]{2,1,0:T(8,128)(2,1)} %copy-done.28) | copy-start | bytes 1769476
  (75 other events, 202.4 us)
